TPU v7x, 256 devices: a whole 4x4x8 slice. The times are simulated.
256 devices in a mesh: lat: 4 (over y), lon: 32 (over x_hi, z, core), grp: 2 (over x_lo).
Axes of the slice: x: 4 (x_hi: 2, x_lo: 2; x = x_hi * 2 + x_lo), y: 4, z: 8, core: 2. Of those that a mesh axis runs over, the one named last changes fastest.
Arguments:
- fine_tokens: bfloat16 [4, 24, 768, 512], P('grp', 'lat', 'lon'), may hold values from -16 to 16
- region_ids: int32 [4, 24, 768], P('grp', 'lat', 'lon'), may hold values from 0 to 9, as said below
- inward_weight: bfloat16 [512, 1536], replicated, may hold values from -2.5 to 2.5
- outward_weight: bfloat16 [512, 512], replicated, may hold values from -0.25 to 0.25
- merging_weight: bfloat16 [2048, 1024], replicated, may hold values from -0.125 to 0.125
- coarse_cotangent: bfloat16 [4, 12, 384, 1024], P('grp', 'lat', 'lon'), may hold values from -6 to 6
Outputs:
- coarse_field: bfloat16 [4, 12, 384, 1024], P('grp', 'lat', 'lon')
- token_grads: bfloat16 [4, 24, 768, 512], P('grp', 'lat', 'lon')
- inward_grads: float32 [512, 1536], P(None, 'lon')
- outward_grads: float32 [512, 512], P(None, 'lon')
- merging_grads: float32 [2048, 1024], P(None, 'lon')
Inputs may be any that keep to these rules, and one draw needn't show every extreme that they name: `region_ids`: region label of each position of the rolled grid; a query attends only to keys of its own label.
All inputs are finite; a program needn't handle non-finite values.
Results may differ from a plain program's by a relative error of at most 0.02.
Values may be sent and summed in bfloat16 or wider, within the bound.
No kernel may reach another device: no remote copies, remote signals or barrier semaphores. Data moves between devices by JAX's collectives and lax.ppermute only.
A program may use at most 128 MiB of HBM per device.

v0:
```python
import jax
import jax.numpy as jnp
from jax import lax
from jax.sharding import PartitionSpec as P

HEADS = 16
WIN_LEV = 2
WIN_LAT = 6
WIN_LON = 12


def from_behind(value, axis, steps):
    count = lax.axis_size(axis)
    pairs = [(source, (source + steps) % count) for source in range(count)]
    return lax.ppermute(value, axis, pairs)


def layer_norm(values):
    centred = values - jnp.mean(values, axis=-1, keepdims=True)
    inverse_std = lax.rsqrt(jnp.mean(centred * centred, axis=-1, keepdims=True) + 1e-05)
    return (centred * inverse_std, inverse_std)


def norm_back(upstream, normalized, inverse_std):
    return inverse_std * (
        upstream
        - jnp.mean(upstream, axis=-1, keepdims=True)
        - normalized * jnp.mean(upstream * normalized, axis=-1, keepdims=True)
    )


def merge_patches(layout):
    level_count, row_count, column_count, channel_count = layout.shape
    blocks = layout.reshape(level_count, row_count // 2, 2, column_count // 2, 2, channel_count)
    blocks = jnp.transpose(blocks, (0, 1, 3, 4, 2, 5))
    return blocks.reshape(level_count, row_count // 2, column_count // 2, 4 * channel_count)


def split_patches(merged):
    level_count, half_rows, half_columns, merged_width = merged.shape
    blocks = merged.reshape(level_count, half_rows, half_columns, 2, 2, merged_width // 4)
    blocks = jnp.transpose(blocks, (0, 1, 4, 2, 3, 5))
    return blocks.reshape(level_count, 2 * half_rows, 2 * half_columns, merged_width // 4)


def local_windows(layout):
    row_count, column_count = (layout.shape[1], layout.shape[2])
    trailing = layout.shape[3:]
    blocks = layout.reshape(
        (WIN_LEV, row_count // WIN_LAT, WIN_LAT, column_count // WIN_LON, WIN_LON) + trailing
    )
    axes_order = (1, 3, 0, 2, 4) + tuple(range(5, 5 + len(trailing)))
    blocks = jnp.transpose(blocks, axes_order)
    return blocks.reshape(
        (row_count // WIN_LAT * (column_count // WIN_LON), WIN_LEV * WIN_LAT * WIN_LON) + trailing
    )


def local_fields(windows, row_count, column_count):
    trailing = windows.shape[2:]
    blocks = windows.reshape(
        (row_count // WIN_LAT, column_count // WIN_LON, WIN_LEV, WIN_LAT, WIN_LON) + trailing
    )
    axes_order = (2, 0, 3, 1, 4) + tuple(range(5, 5 + len(trailing)))
    blocks = jnp.transpose(blocks, axes_order)
    return blocks.reshape((WIN_LEV, row_count, column_count) + trailing)


def roll_forward(layout):
    level_next = from_behind(layout[: WIN_LEV // 2], "grp", -1)
    layout = jnp.concatenate([layout[WIN_LEV // 2 :], level_next], axis=0)
    row_next = from_behind(layout[:, : WIN_LAT // 2], "lat", -1)
    layout = jnp.concatenate([layout[:, WIN_LAT // 2 :], row_next], axis=1)
    column_next = from_behind(layout[:, :, : WIN_LON // 2], "lon", -1)
    return jnp.concatenate([layout[:, :, WIN_LON // 2 :], column_next], axis=2)


def roll_back(layout):
    column_prior = from_behind(layout[:, :, -(WIN_LON // 2) :], "lon", 1)
    layout = jnp.concatenate([column_prior, layout[:, :, : -(WIN_LON // 2)]], axis=2)
    row_prior = from_behind(layout[:, -(WIN_LAT // 2) :], "lat", 1)
    layout = jnp.concatenate([row_prior, layout[:, : -(WIN_LAT // 2)]], axis=1)
    level_prior = from_behind(layout[-(WIN_LEV // 2) :], "grp", 1)
    return jnp.concatenate([level_prior, layout[: -(WIN_LEV // 2)]], axis=0)


def window_forward(windows, labels, inward_weight, outward_weight):
    window_count, token_count, channel_count = windows.shape
    score_scale = (channel_count // HEADS) ** (-0.5)
    normed_exact, inverse_std = layer_norm(windows.astype(jnp.float32))
    normed = normed_exact.astype(jnp.bfloat16)
    projected = jnp.dot(normed, inward_weight, preferred_element_type=jnp.float32).astype(
        jnp.bfloat16
    )
    split_heads = projected.reshape(window_count, token_count, 3, HEADS, channel_count // HEADS)
    query_heads = split_heads[:, :, 0]
    key_heads = split_heads[:, :, 1]
    value_heads = split_heads[:, :, 2]
    scores = (
        jnp.einsum("wqhd,wkhd->whqk", query_heads, key_heads, preferred_element_type=jnp.float32)
        * score_scale
    )
    allowed = (labels[:, :, None] == labels[:, None, :])[:, None]
    scores = jnp.where(allowed, scores, -1e30)
    highest = jnp.max(scores, axis=-1, keepdims=True)
    weights = jnp.exp(scores - highest)
    attention = weights / jnp.sum(weights, axis=-1, keepdims=True)
    attention_low = attention.astype(jnp.bfloat16)
    attended = jnp.einsum(
        "whqk,wkhd->wqhd", attention_low, value_heads, preferred_element_type=jnp.float32
    ).astype(jnp.bfloat16)
    attended = attended.reshape(window_count, token_count, channel_count)
    branch = jnp.dot(attended, outward_weight, preferred_element_type=jnp.float32)
    result = (windows.astype(jnp.float32) + branch).astype(jnp.bfloat16)
    stored = (
        normed_exact,
        inverse_std,
        normed,
        query_heads,
        key_heads,
        value_heads,
        attention,
        attention_low,
        attended,
    )
    return (result, stored)


def window_backward(upstream, stored, inward_weight, outward_weight):
    (
        normed_exact,
        inverse_std,
        normed,
        query_heads,
        key_heads,
        value_heads,
        attention,
        attention_low,
        attended,
    ) = stored
    window_count, token_count, channel_count = upstream.shape
    score_scale = (channel_count // HEADS) ** (-0.5)
    outward_term = jnp.einsum("wtc,wtd->cd", attended, upstream, preferred_element_type=jnp.float32)
    attended_back = jnp.einsum(
        "wtd,cd->wtc", upstream, outward_weight, preferred_element_type=jnp.float32
    ).astype(jnp.bfloat16)
    attended_back = attended_back.reshape(window_count, token_count, HEADS, channel_count // HEADS)
    attention_back = jnp.einsum(
        "wqhd,wkhd->whqk", attended_back, value_heads, preferred_element_type=jnp.float32
    )
    value_back = jnp.einsum(
        "whqk,wqhd->wkhd", attention_low, attended_back, preferred_element_type=jnp.float32
    )
    score_back = attention * (
        attention_back - jnp.sum(attention * attention_back, axis=-1, keepdims=True)
    )
    score_back = (score_back * score_scale).astype(jnp.bfloat16)
    query_back = jnp.einsum(
        "whqk,wkhd->wqhd", score_back, key_heads, preferred_element_type=jnp.float32
    )
    key_back = jnp.einsum(
        "whqk,wqhd->wkhd", score_back, query_heads, preferred_element_type=jnp.float32
    )
    projected_back = jnp.stack([query_back, key_back, value_back], axis=2)
    projected_back = projected_back.reshape(window_count, token_count, 3 * channel_count).astype(
        jnp.bfloat16
    )
    inward_term = jnp.einsum(
        "wtc,wtd->cd", normed, projected_back, preferred_element_type=jnp.float32
    )
    normed_back = jnp.einsum(
        "wtd,cd->wtc", projected_back, inward_weight, preferred_element_type=jnp.float32
    )
    branch_back = norm_back(normed_back, normed_exact, inverse_std).astype(jnp.bfloat16)
    return (branch_back, inward_term, outward_term)


def body(fine_tokens, region_ids, inward_weight, outward_weight, merging_weight, coarse_cotangent):
    row_count, column_count = (fine_tokens.shape[1], fine_tokens.shape[2])
    rolled = roll_forward(fine_tokens)
    windows = local_windows(rolled)
    labels = local_windows(region_ids)
    block_rolled, stored = window_forward(windows, labels, inward_weight, outward_weight)
    block_out = roll_back(local_fields(block_rolled, row_count, column_count))
    merged = merge_patches(block_out)
    merged_exact, merged_inverse = layer_norm(merged.astype(jnp.float32))
    merged_normed = merged_exact.astype(jnp.bfloat16)
    coarse_field = jnp.dot(
        merged_normed, merging_weight, preferred_element_type=jnp.float32
    ).astype(jnp.bfloat16)
    merging_term = jnp.einsum(
        "abcx,abcy->xy", merged_normed, coarse_cotangent, preferred_element_type=jnp.float32
    )
    merged_upstream = jnp.einsum(
        "abcy,xy->abcx", coarse_cotangent, merging_weight, preferred_element_type=jnp.float32
    )
    merged_back = norm_back(merged_upstream, merged_exact, merged_inverse).astype(jnp.bfloat16)
    block_back = split_patches(merged_back)
    upstream = local_windows(roll_forward(block_back))
    branch_back, inward_term, outward_term = window_backward(
        upstream, stored, inward_weight, outward_weight
    )
    branch_layout = roll_back(local_fields(branch_back, row_count, column_count))
    token_grads = (block_back.astype(jnp.float32) + branch_layout.astype(jnp.float32)).astype(
        jnp.bfloat16
    )
    inward_part, outward_part, merging_part = (
        lax.psum_scatter(
            inward_term.astype(jnp.bfloat16), "lon", scatter_dimension=1, tiled=True
        ).astype(jnp.float32),
        lax.psum_scatter(
            outward_term.astype(jnp.bfloat16), "lon", scatter_dimension=1, tiled=True
        ).astype(jnp.float32),
        lax.psum_scatter(
            merging_term.astype(jnp.bfloat16), "lon", scatter_dimension=1, tiled=True
        ).astype(jnp.float32),
    )
    inward_grads, outward_grads, merging_grads = (
        lax.psum(inward_part.astype(jnp.bfloat16), ("lat", "grp")).astype(jnp.float32),
        lax.psum(outward_part.astype(jnp.bfloat16), ("lat", "grp")).astype(jnp.float32),
        lax.psum(merging_part.astype(jnp.bfloat16), ("lat", "grp")).astype(jnp.float32),
    )
    return (coarse_field, token_grads, inward_grads, outward_grads, merging_grads)


def solution(mesh):
    return jax.shard_map(
        body,
        mesh=mesh,
        in_specs=(
            P("grp", "lat", "lon", None),
            P("grp", "lat", "lon"),
            P(),
            P(),
            P(),
            P("grp", "lat", "lon", None),
        ),
        out_specs=(
            P("grp", "lat", "lon", None),
            P("grp", "lat", "lon", None),
            P(None, "lon"),
            P(None, "lon"),
            P(None, "lon"),
        ),
        check_vma=False,
    )
```

profile of v0, /device:TPU:2, one launch (start us, length us, event | category | flops | bytes accessed | tf_op | source)
XLA Modules:
  0.0 626.6 jit_solution(14633640737003811211)
XLA Ops:
  14.0 3.1 collective-permute-start.1
  17.3 2.6 collective-permute-done.1
  19.8 5.1 collective-permute-start.2
  31.7 5.2 fusion.81
  36.9 3.0 convolution_convert_fusion.2
  41.3 7.3 %collective-permute-done.3 = bf16[2,6,6,512]{3,0,2,1:T(2,128)(2,1)S(1)} collective-permute-done((bf16[2,6,6,512]{3,0,2,1:T(2,128)(2,1)S(1)}, bf16[2,6,6,512]{3,0,2,1:T(2,128)(2,1)S(1)}, u32[]{:S(2)}, u32[]{:S(2)}) %collective-permute-start.3) | collective-permute-done | bytes 73760 | tf_op jit(solution)/shard_map/ppermute | solution.py:15
  49.7 5.8 collective-permute-done.4
  58.1 5.3 collective-permute-done.5
  68.2 3.7 fusion.74
  86.6 3.1 collective-permute-done.7
  100.3 4.2 fusion.38
  104.5 4.0 fusion.50
  108.5 9.0 %fusion.32 = bf16[2,144,1,16,32]{1,4,3,0,2:T(8,128)(2,1)} fusion(f32[2,16,144,144]{2,3,1,0:T(8,128)} %fusion.50, bf16[2,144,3,16,32]{1,4,3,2,0:T(8,128)(2,1)} %bitcast.143, f32[2,16,144,144]{2,3,1,0:T(8,128)} %get-tuple-element.56, f32[2,16,144]{2,1,0:T(8,128)} %copy-done.7), kind=kOutput, calls=%fused_computation.35 | convolution fusion | flops 47264400 | bytes 19759104 | tf_op jit(solution)/shard_map/whqk,wqhd->wkhd/dot_general | solution.py:161
  117.5 9.1 %fusion.35 = bf16[2,144,1,16,32]{1,4,3,0,2:T(8,128)(2,1)} fusion(f32[2,16,144,144]{2,3,1,0:T(8,128)} %fusion.50, bf16[2,144,3,16,32]{1,4,3,2,0:T(8,128)(2,1)} %bitcast.144, f32[2,16,144,144]{2,3,1,0:T(8,128)} %get-tuple-element.56, f32[2,16,144]{2,1,0:T(8,128)} %copy-done.7), kind=kOutput, calls=%fused_computation.36 | convolution fusion | flops 47264400 | bytes 19759104 | tf_op jit(solution)/shard_map/whqk,wkhd->wqhd/dot_general | solution.py:158
  132.2 4.2 bitcast_convert_fusion
  136.4 2.6 fusion.75
  140.3 7.3 %collective-permute-done.9 = bf16[2,6,6,512]{3,0,2,1:T(2,128)(2,1)S(1)} collective-permute-done((bf16[2,6,6,512]{3,0,2,1:T(2,128)(2,1)S(1)}, bf16[2,6,6,512]{3,0,2,1:T(2,128)(2,1)S(1)}, u32[]{:S(2)}, u32[]{:S(2)}) %collective-permute-start.9) | collective-permute-done | bytes 73760 | tf_op jit(solution)/shard_map/ppermute | solution.py:15
  147.9 6.4 %collective-permute-done.10 = bf16[2,3,24,512]{3,0,2,1:T(2,128)(2,1)S(1)} collective-permute-done((bf16[2,3,24,512]{3,0,2,1:T(2,128)(2,1)S(1)}, bf16[2,3,24,512]{3,0,2,1:T(2,128)(2,1)S(1)}, u32[]{:S(2)}, u32[]{:S(2)}) %collective-permute-start.10) | collective-permute-done | bytes 147488 | tf_op jit(solution)/shard_map/ppermute | solution.py:15
  157.1 53.7 %reduce-scatter.6.cloned.1.call-done = bf16[512,16]{0,1:T(8,128)(2,1)} async-done(((bf16[512,512]{0,1:T(8,128)(2,1)}), bf16[512,16]{0,1:T(8,128)(2,1)}) %reduce-scatter.6.cloned.1.call-update) | async-done | bytes 16400 | tf_op jit(solution)/shard_map/reduce_scatter | solution.py:211
  210.8 120.1 %reduce-scatter.4.cloned.1.call-done = bf16[512,48]{0,1:T(8,128)(2,1)} async-done(((bf16[512,1536]{0,1:T(8,128)(2,1)}), bf16[512,48]{0,1:T(8,128)(2,1)}) %reduce-scatter.4.cloned.1.call-update) | async-done | bytes 49168 | tf_op jit(solution)/shard_map/reduce_scatter | solution.py:208
  331.0 3.0 fusion.42
  335.2 126.5 %reduce-scatter.8.cloned.1.call-done = bf16[2048,32]{0,1:T(8,128)(2,1)} async-done(((bf16[2048,1024]{0,1:T(8,128)(2,1)}), bf16[2048,32]{0,1:T(8,128)(2,1)}) %reduce-scatter.8.cloned.1.call-update) | async-done | bytes 131088 | tf_op jit(solution)/shard_map/reduce_scatter | solution.py:214
  464.2 74.1 %all-reduce.6.cloned.1.call-done = (bf16[512,48]{0,1:T(8,128)(2,1)}, bf16[512,16]{0,1:T(8,128)(2,1)}) async-done(((bf16[512,48]{0,1:T(8,128)(2,1)}, bf16[512,16]{0,1:T(8,128)(2,1)}), (bf16[512,48]{0,1:T(8,128)(2,1)}, bf16[512,16]{0,1:T(8,128)(2,1)})) %all-reduce.6.cloned.1.call-update) | async-done | bytes 65552 | tf_op jit(solution)/shard_map/psum | solution.py:219
  541.1 77.3 %all-reduce.4.cloned.1.call-done = bf16[2048,32]{0,1:T(8,128)(2,1)} async-done(((bf16[2048,32]{0,1:T(8,128)(2,1)}), bf16[2048,32]{0,1:T(8,128)(2,1)}) %all-reduce.4.cloned.1.call-update) | async-done | bytes 131088 | tf_op jit(solution)/shard_map/psum | solution.py:221
  (120 shorter events, 66.5 us)
Async XLA Ops:
  7.2 22.3 %copy-start = (bf16[512,1536]{1,0:T(8,128)(2,1)S(1)}, bf16[512,1536]{1,0:T(8,128)(2,1)}, u32[]{:S(2)}) copy-start(bf16[512,1536]{1,0:T(8,128)(2,1)} %param.8) | copy-start | bytes 4718596
  7.2 203.7 %reduce-scatter.6.cloned.1.call-start = ((), (), s32[]{:S(2)}) async-start(), calls=%async_computation.4 | async-start | bytes 540672 | tf_op jit(solution)/shard_map/reduce_scatter | solution.py:211
  8.3 5.7 collective-permute-start
  14.0 5.8 collective-permute-start.1
  19.8 7.3 %collective-permute-start.2 = (bf16[2,6,6,512]{3,2,1,0:T(8,128)(2,1)S(1)}, bf16[2,6,6,512]{3,2,1,0:T(8,128)(2,1)S(1)}, u32[]{:S(2)}, u32[]{:S(2)}) collective-permute-start(bf16[2,6,6,512]{3,2,1,0:T(8,128)(2,1)S(1)} %pad_maximum_fusion.7), channel_id=1, source_target_pairs={{0,62},{2,0},{4,2},{6,4},{8,6},{10,8},{12,10},{14,12},{16,14},{18,... | collective-permute-start | bytes 221192 | tf_op jit(solution)/shard_map/ppermute | solution.py:15
  36.9 3.0 copy-start.7
  36.9 3.0 copy-start.2
  40.0 24.1 %copy-start.6 = (bf16[2,16,32,144]{3,2,1,0:T(8,128)(2,1)}, bf16[2,16,32,144]{3,2,1,0:T(8,128)(2,1)S(1)}, u32[]{:S(2)}) copy-start(bf16[2,16,32,144]{3,2,1,0:T(8,128)(2,1)S(1)} %convolution_convert_fusion.2) | copy-start | bytes 884740
  40.4 27.9 %copy-start.5 = (bf16[2,3,12,1024]{3,0,2,1:T(2,128)(2,1)S(1)}, bf16[2,3,12,1024]{3,0,2,1:T(2,128)(2,1)}, u32[]{:S(2)}) copy-start(bf16[2,3,12,1024]{3,0,2,1:T(2,128)(2,1)} %param.11) | copy-start | bytes 442372
  41.1 7.6 %collective-permute-start.3 = (bf16[2,6,6,512]{3,0,2,1:T(2,128)(2,1)S(1)}, bf16[2,6,6,512]{3,0,2,1:T(2,128)(2,1)S(1)}, u32[]{:S(2)}, u32[]{:S(2)}) collective-permute-start(bf16[2,6,6,512]{3,0,2,1:T(2,128)(2,1)S(1)} %slice.123), channel_id=1, source_target_pairs={{0,2},{2,4},{4,6},{6,8},{8,10},{10,12},{12,14},{14,16},{16,18},{18... | collective-permute-start | bytes 221192 | tf_op jit(solution)/shard_map/ppermute | solution.py:15
  48.8 6.7 %collective-permute-start.4 = (bf16[2,3,24,512]{3,0,2,1:T(2,128)(2,1)S(1)}, bf16[2,3,24,512]{3,0,2,1:T(2,128)(2,1)S(1)}, u32[]{:S(2)}, u32[]{:S(2)}) collective-permute-start(bf16[2,3,24,512]{3,0,2,1:T(2,128)(2,1)S(1)} %fusion.61), channel_id=1, source_target_pairs={{0,64},{64,128},{128,192},{192,0},{1,65},{65,129},{129,193},{193,1... | collective-permute-start | bytes 442376 | tf_op jit(solution)/shard_map/ppermute | solution.py:15
  56.4 7.0 %collective-permute-start.5 = (bf16[1,6,24,512]{3,0,2,1:T(2,128)(2,1)S(1)}, bf16[1,6,24,512]{3,0,2,1:T(2,128)(2,1)S(1)}, u32[]{:S(2)}, u32[]{:S(2)}) collective-permute-start(bf16[1,6,24,512]{3,0,2,1:T(2,128)(2,1)S(1)} %get-tuple-element.49), channel_id=1, source_target_pairs={{0,1},{1,0},{2,3},{3,2},{4,5},{5,4},{6,7},{7,6},{8,9},{9,8},{10,11... | collective-permute-start | bytes 442376 | tf_op jit(solution)/shard_map/ppermute | solution.py:15
  77.9 5.7 collective-permute-start.6
  84.5 5.2 collective-permute-start.7
  89.8 2.3 collective-permute-start.8
  98.1 232.8 %reduce-scatter.4.cloned.1.call-start = ((), (), s32[]{:S(2)}) async-start(), calls=%async_computation.3 | async-start | bytes 1622016 | tf_op jit(solution)/shard_map/reduce_scatter | solution.py:208
  100.3 4.2 copy-start.3
  128.6 1.2 copy-start.1
  132.1 329.5 %reduce-scatter.8.cloned.1.call-start = ((), (), s32[]{:S(2)}) async-start(), calls=%async_computation.5 | async-start | bytes 4325376 | tf_op jit(solution)/shard_map/reduce_scatter | solution.py:214
  136.4 401.9 %all-reduce.6.cloned.1.call-start = ((), (), s32[]{:S(2)}) async-start(), calls=%async_computation.7 | async-start | bytes 131072 | tf_op jit(solution)/shard_map/psum | solution.py:219
  140.0 7.5 %collective-permute-start.9 = (bf16[2,6,6,512]{3,0,2,1:T(2,128)(2,1)S(1)}, bf16[2,6,6,512]{3,0,2,1:T(2,128)(2,1)S(1)}, u32[]{:S(2)}, u32[]{:S(2)}) collective-permute-start(bf16[2,6,6,512]{3,0,2,1:T(2,128)(2,1)S(1)} %slice.135), channel_id=1, source_target_pairs={{0,2},{2,4},{4,6},{6,8},{8,10},{10,12},{12,14},{14,16},{16,18},{18... | collective-permute-start | bytes 221192 | tf_op jit(solution)/shard_map/ppermute | solution.py:15
  147.8 6.4 %collective-permute-start.10 = (bf16[2,3,24,512]{3,0,2,1:T(2,128)(2,1)S(1)}, bf16[2,3,24,512]{3,0,2,1:T(2,128)(2,1)S(1)}, u32[]{:S(2)}, u32[]{:S(2)}) collective-permute-start(bf16[2,3,24,512]{3,0,2,1:T(2,128)(2,1)S(1)} %fusion.60), channel_id=1, source_target_pairs={{0,64},{64,128},{128,192},{192,0},{1,65},{65,129},{129,193},{193,1... | collective-permute-start | bytes 442376 | tf_op jit(solution)/shard_map/ppermute | solution.py:15
  155.9 305.8 %collective-permute-start.11 = (bf16[1,6,24,512]{3,0,2,1:T(2,128)(2,1)}, bf16[1,6,24,512]{3,0,2,1:T(2,128)(2,1)}, u32[]{:S(2)}, u32[]{:S(2)}) collective-permute-start(bf16[1,6,24,512]{3,0,2,1:T(2,128)(2,1)} %get-tuple-element.41), channel_id=1, source_target_pairs={{0,1},{1,0},{2,3},{3,2},{4,5},{5,4},{6,7},{7,6},{8,9},{9,8},{10,11... | collective-permute-start | bytes 442376 | tf_op jit(solution)/shard_map/ppermute | solution.py:15
  330.9 287.5 %all-reduce.4.cloned.1.call-start = ((), (), s32[]{:S(2)}) async-start(), calls=%async_computation.6 | async-start | bytes 262144 | tf_op jit(solution)/shard_map/psum | solution.py:221
  (1 other events, 0.7 us)
Sparse Core Ops, SparseCore 0:
  98.2 112.5 reduce-scatter.5
  215.5 115.3 reduce-scatter.3
  335.7 125.8 reduce-scatter.7
  464.2 74.0 all-reduce.5
  540.9 77.4 all-reduce.3
where the time goes:
time: 629 us; the launch traced here: 627 us
  waiting for transfers between devices  496 us (79%)
  matrix products  56.1 us (9%)
  local copies, waits for them, and re-layouts  27.3 us (4%)
  starting transfers between devices  18.7 us (3%)
  between operations  14.2 us (2%)
  other arithmetic  14 us (2%)
    reduce_scatter x1, waiting for transfers between devices, body(): lax.psum_scatter(merging_term.astype(jnp.bfloat16), 'lon', scatter_dimens...  127 us
    reduce_scatter x1, waiting for transfers between devices, body(): lax.psum_scatter(inward_term.astype(jnp.bfloat16), 'lon', scatter_dimensi...  120 us
    psum x1, waiting for transfers between devices, body(): lax.psum(merging_part.astype(jnp.bfloat16), ('lat', 'grp'))  77.3 us
    psum x1, waiting for transfers between devices, body(): lax.psum(inward_part.astype(jnp.bfloat16), ('lat', 'grp'))  74.1 us
    reduce_scatter x1, waiting for transfers between devices, body(): lax.psum_scatter(outward_term.astype(jnp.bfloat16), 'lon', scatter_dimens...  53.7 us
    ppermute x12, waiting for transfers between devices, from_behind(): return lax.ppermute(value, axis, pairs)  44.4 us
    ppermute x12, starting transfers between devices, from_behind(): return lax.ppermute(value, axis, pairs)  18.2 us
  transfers between devices with their start and end apart: 17, of which 15 were waited for; matrix products, arithmetic and copies ran while one was open for 9% of the time, Pallas kernels for 0%

commit v1 on v0

v1 whole, which is shorter than its diff:
```python
import jax
import jax.numpy as jnp
import numpy as np
from jax import lax
from jax.experimental import pallas as pl
from jax.experimental.pallas import tpu as pltpu
from jax.sharding import Mesh, PartitionSpec as P

HEADS = 16
LON = ("xh", "z", "core")
SCALE = 32 ** (-0.5)
LOW = jnp.bfloat16
WIDE = jnp.float32


def token_maps():
    natural = np.arange(288).reshape(2, 6, 24)
    windows = natural.reshape(2, 6, 2, 12).transpose(2, 0, 1, 3).reshape(288)
    to_windows = np.eye(288, dtype=np.float32)[windows]
    extended = np.concatenate([288 + np.arange(48).reshape(2, 1, 24), natural[:, :5]], axis=1)
    cells = extended.reshape(2, 3, 2, 12, 2).transpose(4, 2, 0, 1, 3).reshape(288)
    to_cells = np.eye(336, dtype=np.float32)[cells]
    last_row = np.zeros((288, 48), np.float32)
    last_row[natural[:, 5].reshape(48), np.arange(48)] = 1.0
    return (to_windows, to_cells, to_windows @ last_row)


TO_WINDOWS, TO_CELLS, LAST_ROW = token_maps()


def dot_nn(a, b):
    return lax.dot_general(a, b, (((1,), (0,)), ((), ())), preferred_element_type=WIDE)


def dot_nt(a, b):
    return lax.dot_general(a, b, (((1,), (1,)), ((), ())), preferred_element_type=WIDE)


def dot_tn(a, b):
    return lax.dot_general(a, b, (((0,), (0,)), ((), ())), preferred_element_type=WIDE)


def head_masks():
    head = lax.broadcasted_iota(jnp.int32, (144, 128), 1) >> 5
    return [(head == h).astype(WIDE).astype(LOW) for h in range(4)]


def normalize(values):
    centred = values - jnp.mean(values, axis=-1, keepdims=True)
    inverse_std = lax.rsqrt(jnp.mean(centred * centred, axis=-1, keepdims=True) + 1e-05)
    return (centred * inverse_std, inverse_std)


def forward_kernel(
    tokens, row_labels, column_labels, to_windows, from_windows, inward, outward,
    block, windows, projected, attention, attended,
):
    values = dot_nn(to_windows[...], tokens[...])
    windows[...] = values.astype(LOW)
    normed = normalize(values)[0].astype(LOW)
    projected[...] = dot_nn(normed, inward[...]).astype(LOW)
    masks = head_masks()
    for w in range(2):
        rows = slice(144 * w, 144 * w + 144)
        allowed = column_labels[w] == row_labels[w]
        for t in range(4):
            query = projected[rows, 128 * t : 128 * t + 128]
            key = projected[rows, 512 + 128 * t : 640 + 128 * t]
            value_t = projected[rows, 1024 + 128 * t : 1152 + 128 * t].T
            parts = []
            for h in range(4):
                scores = dot_nt(key * masks[h], query) * SCALE
                scores = jnp.where(allowed, scores, -1e30)
                weights = jnp.exp(scores - jnp.max(scores, axis=0, keepdims=True))
                share = weights * (1.0 / jnp.sum(weights, axis=0, keepdims=True))
                share = share.astype(LOW)
                attention[w, 4 * t + h] = share
                parts.append(dot_nn(value_t[32 * h : 32 * h + 32], share))
            attended[rows, 128 * t : 128 * t + 128] = jnp.concatenate(parts, axis=0).T.astype(LOW)
    result = (values + dot_nn(attended[...], outward[...])).astype(LOW)
    block[...] = dot_nn(from_windows[...], result).astype(LOW)


def merge_kernel(block, prior, to_cells, from_cells, upstream, normed, back, back_row):
    merged = dot_nn(to_cells[:, :288], block[...]) + dot_nn(to_cells[:, 288:], prior[...])
    pieces = [merged[72 * k : 72 * k + 72] for k in range(4)]
    exact, inverse_std = normalize(jnp.concatenate(pieces, axis=1))
    normed[...] = exact.astype(LOW)
    grads = upstream[...]
    grads = inverse_std * (
        grads
        - jnp.mean(grads, axis=-1, keepdims=True)
        - exact * jnp.mean(grads * exact, axis=-1, keepdims=True)
    )
    stacked = jnp.concatenate([grads[:, 512 * k : 512 * k + 512] for k in range(4)], axis=0)
    stacked = stacked.astype(LOW)
    back[...] = dot_nn(from_cells[:288], stacked).astype(LOW)
    back_row[...] = dot_nn(from_cells[288:], stacked).astype(LOW)


def coarse_kernel(normed, cotangent, weight, coarse, terms):
    coarse[...] = dot_nn(normed[...], weight[...]).astype(LOW)
    for j in range(8):
        chunk = dot_tn(cotangent[:, 128 * j : 128 * j + 128], normed[...]).astype(LOW)
        for i in range(4):
            place = 4 * j + i
            for k in range(8):
                terms[place % 2, place // 16, k // 2, k % 2, place // 2 % 8] = chunk[
                    32 * i : 32 * i + 32, 256 * k : 256 * k + 256
                ]


def backward_kernel(
    back, next_row, windows, projected, attention, attended, to_windows, last_row, from_windows, inward, outward,
    token_grads, terms, projected_back,
):
    upstream = dot_nn(to_windows[...], back[...]) + dot_nn(last_row[...], next_row[...])
    upstream_low = upstream.astype(LOW)
    attended_back = dot_nt(upstream_low, outward[...]).astype(LOW)
    masks = head_masks()
    for w in range(2):
        rows = slice(144 * w, 144 * w + 144)
        for t in range(4):
            query = projected[rows, 128 * t : 128 * t + 128]
            key_t = projected[rows, 512 + 128 * t : 640 + 128 * t].T
            value = projected[rows, 1024 + 128 * t : 1152 + 128 * t]
            grads = attended_back[rows, 128 * t : 128 * t + 128]
            query_parts, key_back, value_back = [], 0.0, 0.0
            for h in range(4):
                low = attention[w, 4 * t + h]
                share = low.astype(WIDE)
                product = share * dot_nt(value * masks[h], grads)
                total = jnp.sum(product, axis=0, keepdims=True)
                score_back = ((product - share * total) * SCALE).astype(LOW)
                value_back += dot_nn(low, grads * masks[h])
                key_back += dot_nn(score_back, query * masks[h])
                query_parts.append(dot_nn(key_t[32 * h : 32 * h + 32], score_back))
            query_back = jnp.concatenate(query_parts, axis=0).T
            projected_back[rows, 128 * t : 128 * t + 128] = query_back.astype(LOW)
            projected_back[rows, 512 + 128 * t : 640 + 128 * t] = key_back.astype(LOW)
            projected_back[rows, 1024 + 128 * t : 1152 + 128 * t] = value_back.astype(LOW)
    normed, inverse_std = normalize(windows[...].astype(WIDE))
    normed_low = normed.astype(LOW)
    for j in range(4):
        inward_t = dot_tn(projected_back[:, 384 * j : 384 * j + 384], normed_low).astype(LOW)
        outward_t = dot_tn(upstream_low[:, 128 * j : 128 * j + 128], attended[...]).astype(LOW)
        for i in range(8):
            place = 8 * j + i
            for k in range(4):
                lanes = slice(128 * k, 128 * k + 128)
                at = (place % 2, place // 16, k)
                terms[at + (0, place // 2 % 8)] = inward_t[48 * i : 48 * i + 32, lanes]
                terms[at + (1, place // 2 % 8, slice(0, 16))] = inward_t[48 * i + 32 : 48 * i + 48, lanes]
                terms[at + (1, place // 2 % 8, slice(16, 32))] = outward_t[16 * i : 16 * i + 16, lanes]
    normed_back = dot_nt(projected_back[...], inward[...])
    branch = inverse_std * (
        normed_back
        - jnp.mean(normed_back, axis=-1, keepdims=True)
        - normed * jnp.mean(normed_back * normed, axis=-1, keepdims=True)
    )
    result = (upstream + branch.astype(LOW).astype(WIDE)).astype(LOW)
    token_grads[...] = dot_nn(from_windows[...], result).astype(LOW)


def call(kernel, outs, *operands, scratch=()):
    return pl.pallas_call(
        kernel,
        out_shape=[jax.ShapeDtypeStruct(shape, LOW) for shape in outs],
        scratch_shapes=[pltpu.VMEM(shape, LOW) for shape in scratch],
        compiler_params=pltpu.CompilerParams(vmem_limit_bytes=48 * 1024 * 1024),
    )(*operands)


def from_behind(value, axis, steps):
    count = lax.axis_size(axis)
    pairs = [(source, (source + steps) % count) for source in range(count)]
    return lax.ppermute(value, axis, pairs)


def local_windows(layout):
    return layout.reshape(2, 6, 2, 12).transpose(2, 0, 1, 3).reshape(2, 144)


def roll_forward(layout, levels, rows, columns):
    level_next = from_behind(layout[:levels], ("grp",), -1)
    layout = jnp.concatenate([layout[levels:], level_next], axis=0)
    row_next = from_behind(layout[:, :rows], ("lat",), -1)
    layout = jnp.concatenate([layout[:, rows:], row_next], axis=1)
    column_next = from_behind(layout[:, :, :columns], LON, -1)
    return jnp.concatenate([layout[:, :, columns:], column_next], axis=2)


def roll_back(layout, levels, rows, columns):
    column_prior = from_behind(layout[:, :, -columns:], LON, 1)
    layout = jnp.concatenate([column_prior, layout[:, :, :-columns]], axis=2)
    row_prior = from_behind(layout[:, -rows:], ("lat",), 1)
    layout = jnp.concatenate([row_prior, layout[:, :-rows]], axis=1)
    level_prior = from_behind(layout[-levels:], ("grp",), 1)
    return jnp.concatenate([level_prior, layout[:-levels]], axis=0)


def wide_sum(parts):
    return jnp.sum(parts.astype(WIDE), axis=0).astype(LOW)


def over_planes(terms):
    core = lax.axis_index("core")
    sent = lax.dynamic_index_in_dim(terms, 1 - core, 0, keepdims=False)
    kept = lax.dynamic_index_in_dim(terms, core, 0, keepdims=False)
    came = from_behind(sent, ("core",), 1)
    summed = (kept.astype(WIDE) + came.astype(WIDE)).astype(LOW)
    summed = summed.reshape((16,) + terms.shape[4:])
    return wide_sum(lax.all_to_all(summed, ("xh", "lat", "grp"), 0, 0))


def body(fine_tokens, region_ids, inward_weight, outward_weight, merging_weight, coarse_cotangent):
    to_windows = jnp.asarray(TO_WINDOWS, LOW)
    from_windows = jnp.asarray(TO_WINDOWS.T, LOW)
    to_cells = jnp.asarray(TO_CELLS, LOW)
    from_cells = jnp.asarray(TO_CELLS.T, LOW)
    last_row = jnp.asarray(LAST_ROW, LOW)
    rolled = roll_forward(fine_tokens, 1, 3, 6).reshape(288, 512)
    cotangent = roll_forward(coarse_cotangent, 1, 1, 3).reshape(72, 1024)
    labels = local_windows(region_ids)
    block, windows, projected, attention, attended = call(
        forward_kernel,
        [(288, 512), (288, 512), (288, 1536), (2, HEADS, 144, 144), (288, 512)],
        rolled, labels.reshape(2, 1, 144), labels.reshape(2, 144, 1), to_windows, from_windows, inward_weight, outward_weight,
    )
    prior = from_behind(block.reshape(2, 6, 24, 512)[:, 5].reshape(48, 512), ("lat",), 1)
    merged_upstream = dot_nt(cotangent, merging_weight)
    merged_normed, back, back_row = call(
        merge_kernel,
        [(72, 2048), (288, 512), (48, 512)],
        block, prior, to_cells, from_cells, merged_upstream,
    )
    next_row = from_behind(back_row, ("lat",), -1)
    coarse_field, merging_terms = call(
        coarse_kernel,
        [(72, 1024), (2, 2, 4, 2, 8, 32, 256)],
        merged_normed, cotangent, merging_weight,
    )
    token_grads, block_terms = call(
        backward_kernel,
        [(288, 512), (2, 2, 4, 2, 8, 32, 128)],
        back, next_row, windows, projected, attention, attended,
        to_windows, last_row, from_windows, inward_weight, outward_weight,
        scratch=[(288, 1536)],
    )
    coarse_field = roll_back(coarse_field.reshape(2, 3, 12, 1024), 1, 1, 3)
    token_grads = roll_back(token_grads.reshape(2, 6, 24, 512), 1, 3, 6)
    planes = jnp.concatenate([over_planes(block_terms), over_planes(merging_terms)], axis=2)
    share = wide_sum(lax.all_to_all(planes, ("z",), 0, 0))
    shares = lax.all_to_all(jnp.broadcast_to(share[None], (8, 32, 384)), ("lat", "grp"), 0, 0)
    shares = shares.reshape(4, 2, 32, 384).astype(WIDE)
    block_grads = shares[..., :128].transpose(0, 3, 1, 2).reshape(512, 64)
    merging_grads = shares[..., 128:].transpose(0, 1, 3, 2).reshape(2048, 32)
    return (coarse_field, token_grads, block_grads[:, :48], block_grads[:, 48:], merging_grads)


def solution(mesh):
    fine = Mesh(mesh.devices.reshape(4, 2, 8, 2, 2), ("lat", "xh", "z", "core", "grp"))
    return jax.shard_map(
        body,
        mesh=fine,
        in_specs=(
            P("grp", "lat", LON, None),
            P("grp", "lat", LON),
            P(),
            P(),
            P(),
            P("grp", "lat", LON, None),
        ),
        out_specs=(
            P("grp", "lat", LON, None),
            P("grp", "lat", LON, None),
            P(None, LON),
            P(None, LON),
            P(None, LON),
        ),
        check_vma=False,
    )
```

time: 629 us -> 162 us (0.26)
  waiting for transfers between devices: 496 us -> 60.3 us
  matrix products: 56.1 us -> 1.4 us
  starting transfers between devices: 18.7 us -> 43.3 us
  Pallas kernels: 0 us -> 23.1 us
  between operations: 14.2 us -> 0.99 us
  local copies, waits for them, and re-layouts: 27.3 us -> 16.5 us
    reduce_scatter x3 -> x0, waiting for transfers between devices: 300 us -> none  [the longest x1 127 us: body(): lax.psum_scatter(merging_term.astype(jnp.bfloat16), 'lon', scatter_dimens...]
    psum x2 -> x0, waiting for transfers between devices: 151 us -> none  [the longest x1 77.3 us: body(): lax.psum(merging_part.astype(jnp.bfloat16), ('lat', 'grp'))]
    dot_general x14 -> x1, matrix products: 50.9 us -> 1.4 us  [dot_nt(): lax.dot_general(a, b, (((1,), (1,)), ((), ())), preferred_element_type=WIDE)]
    all_to_all x0 -> x4, waiting for transfers between devices: none -> 27.9 us  [the longest x2 16.7 us: over_planes(): return wide_sum(lax.all_to_all(summed, ('xh', 'lat', 'grp'), 0, 0))]
    pallas_call x0 -> x4, Pallas kernels: none -> 23.1 us  [call(): pl.pallas_call(kernel, out_shape=[jax.ShapeDtypeStruct(shape, LOW) for sh...]
    all_to_all x0 -> x4, starting transfers between devices: none -> 19.8 us  [the longest x2 9.71 us: over_planes(): return wide_sum(lax.all_to_all(summed, ('xh', 'lat', 'grp'), 0, 0))]
    ppermute x12 -> x16, waiting for transfers between devices: 44.4 us -> 32.4 us  [from_behind(): return lax.ppermute(value, axis, pairs)]
    convert_element_type x9 -> x0, local copies, waits for them, and re-layouts: 8.24 us -> none  [the longest x2 2.86 us: body(): merged_exact, merged_inverse = layer_norm(merged.astype(jnp.float32))]
  transfers between devices with their start and end apart: 17 -> 20, of which waited for: 15 -> 12; matrix products, arithmetic and copies ran while one was open for 9% -> 17% of each run, Pallas kernels for 0% -> 9%
where the time goes in v1:
time: 162 us; the launch traced here: 161 us
  waiting for transfers between devices  60.3 us (37%)
  starting transfers between devices  43.3 us (27%)
  Pallas kernels  23.1 us (14%)
  local copies, waits for them, and re-layouts  16.5 us (10%)
  other arithmetic  15.8 us (10%)
    ppermute x16, waiting for transfers between devices, from_behind(): return lax.ppermute(value, axis, pairs)  32.4 us
    ppermute x16, starting transfers between devices, from_behind(): return lax.ppermute(value, axis, pairs)  23.4 us
    pallas_call x4, Pallas kernels, call(): pl.pallas_call(kernel, out_shape=[jax.ShapeDtypeStruct(shape, LOW) for sh...  23.1 us
    all_to_all x2, waiting for transfers between devices, over_planes(): return wide_sum(lax.all_to_all(summed, ('xh', 'lat', 'grp'), 0, 0))  16.7 us
    all_to_all x2, starting transfers between devices, over_planes(): return wide_sum(lax.all_to_all(summed, ('xh', 'lat', 'grp'), 0, 0))  9.71 us
    all_to_all x1, waiting for transfers between devices, body(): share = wide_sum(lax.all_to_all(planes, ('z',), 0, 0))  7.93 us
    convert_element_type x2, other arithmetic, over_planes(): summed = (kept.astype(WIDE) + came.astype(WIDE)).astype(LOW)  7.07 us
    all_to_all x1, starting transfers between devices, body(): lax.all_to_all(jnp.broadcast_to(share[None], (8, 32, 384)), ('lat', 'grp'...  6.74 us
  transfers between devices with their start and end apart: 20, of which 12 were waited for; matrix products, arithmetic and copies ran while one was open for 17% of the time, Pallas kernels for 9%

profile of v1, /device:TPU:2, one launch (start us, length us, event | category | flops | bytes accessed | tf_op | source)
XLA Modules:
  0.0 161.3 jit_solution(11625227038239882004)
XLA Ops:
  1.9 2.4 %collective-permute-start.4 = (bf16[1,3,12,1024]{3,0,2,1:T(2,128)(2,1)S(1)}, bf16[1,3,12,1024]{3,0,2,1:T(2,128)(2,1)S(1)}, u32[]{:S(2)}, u32[]{:S(2)}) collective-permute-start(bf16[1,3,12,1024]{3,0,2,1:T(2,128)(2,1)S(1)} %get-tuple-element.53), channel_id=1, source_target_pairs={{0,1},{1,0},{2,3},{3,2},{4,5},{5,4},{6,7},{7,6},{8,9},{9,8},{10,11... | collective-permute-start | bytes 221192 | tf_op jit(solution)/shard_map/ppermute | solution.py:177
  9.0 2.9 %collective-permute-start.5 = (bf16[2,1,12,1024]{3,0,2,1:T(2,128)(2,1)S(1)}, bf16[2,1,12,1024]{3,0,2,1:T(2,128)(2,1)S(1)}, u32[]{:S(2)}, u32[]{:S(2)}) collective-permute-start(bf16[2,1,12,1024]{3,0,2,1:T(2,128)(2,1)S(1)} %pad_maximum_fusion.10), channel_id=1, source_target_pairs={{0,192},{64,0},{128,64},{192,128},{1,193},{65,1},{129,65},{193,129... | collective-permute-start | bytes 147464 | tf_op jit(solution)/shard_map/ppermute | solution.py:177
  13.7 4.2 %collective-permute-start.6 = (bf16[2,3,3,1024]{3,0,2,1:T(2,128)(2,1)S(1)}, bf16[2,3,3,1024]{3,0,2,1:T(2,128)(2,1)S(1)}, u32[]{:S(2)}, u32[]{:S(2)}) collective-permute-start(bf16[2,3,3,1024]{3,0,2,1:T(2,128)(2,1)S(1)} %pad_maximum_fusion.11), channel_id=1, source_target_pairs={{0,62},{2,0},{4,2},{6,4},{8,6},{10,8},{12,10},{14,12},{16,14},{18,... | collective-permute-start | bytes 110600 | tf_op jit(solution)/shard_map/ppermute | solution.py:177
  18.5 3.3 %collective-permute-start.1 = (bf16[2,3,24,512]{3,2,1,0:T(8,128)(2,1)}, bf16[2,3,24,512]{3,2,1,0:T(8,128)(2,1)S(1)}, u32[]{:S(2)}, u32[]{:S(2)}) collective-permute-start(bf16[2,3,24,512]{3,2,1,0:T(8,128)(2,1)} %get-tuple-element.47), channel_id=1, source_target_pairs={{0,192},{64,0},{128,64},{192,128},{1,193},{65,1},{129,65},{193,129... | collective-permute-start | bytes 442376 | tf_op jit(solution)/shard_map/ppermute | solution.py:177
  22.2 2.5 %collective-permute-done.1 = bf16[2,3,24,512]{3,2,1,0:T(8,128)(2,1)S(1)} collective-permute-done((bf16[2,3,24,512]{3,2,1,0:T(8,128)(2,1)}, bf16[2,3,24,512]{3,2,1,0:T(8,128)(2,1)S(1)}, u32[]{:S(2)}, u32[]{:S(2)}) %collective-permute-start.1) | collective-permute-done | bytes 147488 | tf_op jit(solution)/shard_map/ppermute | solution.py:177
  24.8 3.8 %collective-permute-start.2 = (bf16[2,6,6,512]{3,2,1,0:T(8,128)(2,1)S(1)}, bf16[2,6,6,512]{3,2,1,0:T(8,128)(2,1)S(1)}, u32[]{:S(2)}, u32[]{:S(2)}) collective-permute-start(bf16[2,6,6,512]{3,2,1,0:T(8,128)(2,1)S(1)} %pad_maximum_fusion.8), channel_id=1, source_target_pairs={{0,62},{2,0},{4,2},{6,4},{8,6},{10,8},{12,10},{14,12},{16,14},{18,... | collective-permute-start | bytes 221192 | tf_op jit(solution)/shard_map/ppermute | solution.py:177
  30.9 7.5 %shard_map.146 = (bf16[288,512]{1,0:T(8,128)(2,1)S(1)}, bf16[288,512]{1,0:T(8,128)(2,1)S(1)}, bf16[288,1536]{1,0:T(8,128)(2,1)S(1)}, bf16[2,16,144,144]{3,2,1,0:T(8,128)(2,1)}, bf16[288,512]{1,0:T(8,128)(2,1)S(1)}) custom-call(bf16[288,512]{1,0:T(8,128)(2,1)S(1)} %bitcast.45, s32[2,1,144]{2,1,0:T(1,128)S(1)} %reshape_reshape.8.row_labels, ...), custom_call_target="tpu_custom_call" | custom-call | tf_op jit(solution)/shard_map/pallas_call | solution.py:166
  40.1 4.2 %collective-permute-done.3.prior = bf16[48,512]{1,0:T(8,128)(2,1)S(1)} collective-permute-done((bf16[48,512]{1,0:T(8,128)(2,1)S(1)}, bf16[48,512]{1,0:T(8,128)(2,1)S(1)}, u32[]{:S(2)}, u32[]{:S(2)}) %collective-permute-start.3) | collective-permute-done | bytes 49184 | tf_op jit(solution)/shard_map/ppermute | solution.py:177
  47.6 4.1 %shard_map.148 = (bf16[72,1024]{1,0:T(8,128)(2,1)S(1)}, bf16[2,2,4,2,8,32,256]{6,5,4,3,2,1,0:T(8,128)(2,1)S(1)}) custom-call(bf16[72,2048]{1,0:T(8,128)(2,1)S(1)} %get-tuple-element.18.normed, bf16[72,1024]{1,0:T(8,128)(2,1)S(1)} %reshape.51.cotangent, bf16[2048,1024]{1,0:T(8,128)(2,1)} %weight.1), custom_call_target="tpu_custom_call" | custom-call | tf_op jit(solution)/shard_map/pallas_call | solution.py:166
  54.3 10.3 %shard_map.149 = (bf16[288,512]{1,0:T(8,128)(2,1)S(1)}, bf16[2,2,4,2,8,32,128]{6,5,4,3,2,1,0:T(8,128)(2,1)}) custom-call(bf16[288,512]{1,0:T(8,128)(2,1)S(1)} %get-tuple-element.20.back, bf16[48,512]{1,0:T(8,128)(2,1)S(1)} %collective-permute-done.10.next_row, bf16[288,512]{1,0:T(8,128)(2,1)S(1)} %get-tuple-element.22.windows, ...), custom_call_target="tpu_custom_call" | custom-call | tf_op jit(solution)/shard_map/pallas_call | solution.py:166
  64.6 2.5 %dynamic-slice_bitcast_fusion.1 = bf16[2,4,2,8,32,128]{5,4,3,2,1,0:T(8,128)(2,1)} fusion(bf16[2,2,4,2,8,32,128]{6,5,4,3,2,1,0:T(8,128)(2,1)} %get-tuple-element.27, s32[]{:T(128)S(6)} %select_n.11), kind=kLoop, calls=%fused_computation.5 | loop fusion | bytes 2097156 | tf_op jit(solution)/shard_map/jit(dynamic_index_in_dim)/squeeze | solution.py:208
  67.6 2.6 %collective-permute-done.14 = bf16[2,4,2,8,32,128]{5,4,3,2,1,0:T(8,128)(2,1)} collective-permute-done((bf16[2,4,2,8,32,128]{5,4,3,2,1,0:T(8,128)(2,1)}, bf16[2,4,2,8,32,128]{5,4,3,2,1,0:T(8,128)(2,1)}, u32[]{:S(2)}, u32[]{:S(2)}) %collective-permute-start.14) | collective-permute-done | bytes 1048608 | tf_op jit(solution)/shard_map/ppermute | solution.py:177
  70.2 2.5 %fusion.1 = bf16[2,4,2,8,32,128]{5,4,3,2,1,0:T(8,128)(2,1)} fusion(bf16[2,4,2,8,32,128]{5,4,3,2,1,0:T(8,128)(2,1)} %collective-permute-done.14, bf16[2,2,4,2,8,32,128]{6,5,4,3,2,1,0:T(8,128)(2,1)S(1)} %copy-done.11, s32[]{:T(128)S(6)} %select_n.10), kind=kLoop, calls=%fused_computation.3 | loop fusion | flops 2097152 | bytes 3145732 | tf_op jit(solution)/shard_map/convert_element_type | solution.py:211
  72.7 4.5 %all-to-all-start = ((bf16[16,8,32,128]{3,2,1,0:T(8,128)(2,1)}), bf16[16,8,32,128]{3,2,1,0:T(8,128)(2,1)S(1)}, u32[]{:S(2)}, u32[]{:S(2)}) async-start(bf16[16,8,32,128]{3,2,1,0:T(8,128)(2,1)} %bitcast.7), calls=%async_computation | async-start | bytes 2097152 | tf_op jit(solution)/shard_map/all_to_all | solution.py:213
  77.2 4.6 %fusion = bf16[2,4,2,8,32,256]{5,4,3,2,1,0:T(8,128)(2,1)} fusion(bf16[2,4,2,8,32,256]{5,4,3,2,1,0:T(8,128)(2,1)} %collective-permute-done.15, bf16[2,2,4,2,8,32,256]{6,5,4,3,2,1,0:T(8,128)(2,1)} %copy-done.1, s32[]{:T(128)S(6)} %select_n.10), kind=kLoop, calls=%fused_computation.1 | loop fusion | flops 4194304 | bytes 6291460 | tf_op jit(solution)/shard_map/convert_element_type | solution.py:211
  81.8 13.6 %all-to-all-done = bf16[16,8,32,128]{3,2,1,0:T(8,128)(2,1)S(1)} async-done(((bf16[16,8,32,128]{3,2,1,0:T(8,128)(2,1)}), bf16[16,8,32,128]{3,2,1,0:T(8,128)(2,1)S(1)}, u32[]{:S(2)}, u32[]{:S(2)}) %all-to-all-start) | async-done | bytes 1048608 | tf_op jit(solution)/shard_map/all_to_all | solution.py:213
  96.3 5.2 %all-to-all-start.1 = ((bf16[16,8,32,256]{3,2,1,0:T(8,128)(2,1)}), bf16[16,8,32,256]{3,2,1,0:T(8,128)(2,1)S(1)}, u32[]{:S(2)}, u32[]{:S(2)}) async-start(bf16[16,8,32,256]{3,2,1,0:T(8,128)(2,1)} %bitcast.10), calls=%async_computation.1 | async-start | bytes 4194304 | tf_op jit(solution)/shard_map/all_to_all | solution.py:213
  103.3 7.3 %collective-permute-done.7 = bf16[2,3,3,1024]{3,2,1,0:T(4,128)(2,1)S(1)} collective-permute-done((bf16[2,3,3,1024]{3,2,1,0:T(4,128)(2,1)S(1)}, bf16[2,3,3,1024]{3,2,1,0:T(4,128)(2,1)S(1)}, u32[]{:S(2)}, u32[]{:S(2)}) %collective-permute-start.7) | collective-permute-done | bytes 36896 | tf_op jit(solution)/shard_map/ppermute | solution.py:177
  113.1 10.1 %collective-permute-done.8 = bf16[2,1,12,1024]{3,2,1,0:T(8,128)(2,1)S(1)} collective-permute-done((bf16[2,1,12,1024]{3,2,1,0:T(8,128)(2,1)S(1)}, bf16[2,1,12,1024]{3,2,1,0:T(8,128)(2,1)S(1)}, u32[]{:S(2)}, u32[]{:S(2)}) %collective-permute-start.8) | collective-permute-done | bytes 49184 | tf_op jit(solution)/shard_map/ppermute | solution.py:177
  127.2 3.2 %all-to-all-done.1 = bf16[16,8,32,256]{3,2,1,0:T(8,128)(2,1)S(1)} async-done(((bf16[16,8,32,256]{3,2,1,0:T(8,128)(2,1)}), bf16[16,8,32,256]{3,2,1,0:T(8,128)(2,1)S(1)}, u32[]{:S(2)}, u32[]{:S(2)}) %all-to-all-start.1) | async-done | bytes 2097184 | tf_op jit(solution)/shard_map/all_to_all | solution.py:213
  131.5 3.4 %all-to-all-start.2 = ((bf16[8,32,384]{2,1,0:T(8,128)(2,1)}), bf16[8,32,384]{2,1,0:T(8,128)(2,1)S(1)}, u32[]{:S(2)}, u32[]{:S(2)}) async-start(bf16[8,32,384]{2,1,0:T(8,128)(2,1)} %pad_maximum_fusion.5), calls=%async_computation.2 | async-start | bytes 393216 | tf_op jit(solution)/shard_map/all_to_all | solution.py:253
  137.5 7.9 %all-to-all-done.2 = bf16[8,32,384]{2,1,0:T(8,128)(2,1)S(1)} async-done(((bf16[8,32,384]{2,1,0:T(8,128)(2,1)}), bf16[8,32,384]{2,1,0:T(8,128)(2,1)S(1)}, u32[]{:S(2)}, u32[]{:S(2)}) %all-to-all-start.2) | async-done | bytes 196640 | tf_op jit(solution)/shard_map/all_to_all | solution.py:253
  146.2 6.7 %all-to-all-start.3 = ((bf16[8,32,384]{2,1,0:T(8,128)(2,1)}), bf16[8,32,384]{2,1,0:T(8,128)(2,1)S(1)}, u32[]{:S(2)}, u32[]{:S(2)}) async-start(bf16[8,32,384]{2,1,0:T(8,128)(2,1)} %broadcast_in_dim.2), calls=%async_computation.3 | async-start | bytes 393216 | tf_op jit(solution)/shard_map/all_to_all | solution.py:254
  155.4 3.3 %all-to-all-done.3 = bf16[8,32,384]{2,1,0:T(8,128)(2,1)S(1)} async-done(((bf16[8,32,384]{2,1,0:T(8,128)(2,1)}), bf16[8,32,384]{2,1,0:T(8,128)(2,1)S(1)}, u32[]{:S(2)}, u32[]{:S(2)}) %all-to-all-start.3) | async-done | bytes 196640 | tf_op jit(solution)/shard_map/all_to_all | solution.py:254
  (99 shorter events, 37.8 us)
Async XLA Ops:
  1.9 6.9 %collective-permute-start.4 = (bf16[1,3,12,1024]{3,0,2,1:T(2,128)(2,1)S(1)}, bf16[1,3,12,1024]{3,0,2,1:T(2,128)(2,1)S(1)}, u32[]{:S(2)}, u32[]{:S(2)}) collective-permute-start(bf16[1,3,12,1024]{3,0,2,1:T(2,128)(2,1)S(1)} %get-tuple-element.53), channel_id=1, source_target_pairs={{0,1},{1,0},{2,3},{3,2},{4,5},{5,4},{6,7},{7,6},{8,9},{9,8},{10,11... | collective-permute-start | bytes 221192 | tf_op jit(solution)/shard_map/ppermute | solution.py:177
  5.9 11.9 %collective-permute-start = (bf16[1,6,24,512]{3,2,1,0:T(8,128)(2,1)}, bf16[1,6,24,512]{3,2,1,0:T(8,128)(2,1)S(1)}, u32[]{:S(2)}, u32[]{:S(2)}) collective-permute-start(bf16[1,6,24,512]{3,2,1,0:T(8,128)(2,1)} %get-tuple-element.49), channel_id=1, source_target_pairs={{0,1},{1,0},{2,3},{3,2},{4,5},{5,4},{6,7},{7,6},{8,9},{9,8},{10,11... | collective-permute-start | bytes 442376 | tf_op jit(solution)/shard_map/ppermute | solution.py:177
  8.9 21.9 %copy-start = (bf16[512,1536]{1,0:T(8,128)(2,1)S(1)}, bf16[512,1536]{1,0:T(8,128)(2,1)}, u32[]{:S(2)}) copy-start(bf16[512,1536]{1,0:T(8,128)(2,1)} %inward.3) | copy-start | bytes 4718596
  8.9 21.9 %copy-start.2 = (bf16[512,512]{1,0:T(8,128)(2,1)S(1)}, bf16[512,512]{1,0:T(8,128)(2,1)}, u32[]{:S(2)}) copy-start(bf16[512,512]{1,0:T(8,128)(2,1)} %outward.3) | copy-start | bytes 1572868
  9.0 21.9 %copy-start.3 = (bf16[288,288]{1,0:T(8,128)(2,1)S(1)}, bf16[288,288]{1,0:T(8,128)(2,1)}, u32[]{:S(2)}) copy-start(bf16[288,288]{1,0:T(8,128)(2,1)} %constant.38.clone.from_windows) | copy-start | bytes 497668
  9.0 4.6 %collective-permute-start.5 = (bf16[2,1,12,1024]{3,0,2,1:T(2,128)(2,1)S(1)}, bf16[2,1,12,1024]{3,0,2,1:T(2,128)(2,1)S(1)}, u32[]{:S(2)}, u32[]{:S(2)}) collective-permute-start(bf16[2,1,12,1024]{3,0,2,1:T(2,128)(2,1)S(1)} %pad_maximum_fusion.10), channel_id=1, source_target_pairs={{0,192},{64,0},{128,64},{192,128},{1,193},{65,1},{129,65},{193,129... | collective-permute-start | bytes 147464 | tf_op jit(solution)/shard_map/ppermute | solution.py:177
  13.7 8.3 %collective-permute-start.6 = (bf16[2,3,3,1024]{3,0,2,1:T(2,128)(2,1)S(1)}, bf16[2,3,3,1024]{3,0,2,1:T(2,128)(2,1)S(1)}, u32[]{:S(2)}, u32[]{:S(2)}) collective-permute-start(bf16[2,3,3,1024]{3,0,2,1:T(2,128)(2,1)S(1)} %pad_maximum_fusion.11), channel_id=1, source_target_pairs={{0,62},{2,0},{4,2},{6,4},{8,6},{10,8},{12,10},{14,12},{16,14},{18,... | collective-permute-start | bytes 110600 | tf_op jit(solution)/shard_map/ppermute | solution.py:177
  18.5 6.2 %collective-permute-start.1 = (bf16[2,3,24,512]{3,2,1,0:T(8,128)(2,1)}, bf16[2,3,24,512]{3,2,1,0:T(8,128)(2,1)S(1)}, u32[]{:S(2)}, u32[]{:S(2)}) collective-permute-start(bf16[2,3,24,512]{3,2,1,0:T(8,128)(2,1)} %get-tuple-element.47), channel_id=1, source_target_pairs={{0,192},{64,0},{128,64},{192,128},{1,193},{65,1},{129,65},{193,129... | collective-permute-start | bytes 442376 | tf_op jit(solution)/shard_map/ppermute | solution.py:177
  24.8 6.0 %collective-permute-start.2 = (bf16[2,6,6,512]{3,2,1,0:T(8,128)(2,1)S(1)}, bf16[2,6,6,512]{3,2,1,0:T(8,128)(2,1)S(1)}, u32[]{:S(2)}, u32[]{:S(2)}) collective-permute-start(bf16[2,6,6,512]{3,2,1,0:T(8,128)(2,1)S(1)} %pad_maximum_fusion.8), channel_id=1, source_target_pairs={{0,62},{2,0},{4,2},{6,4},{8,6},{10,8},{12,10},{14,12},{16,14},{18,... | collective-permute-start | bytes 221192 | tf_op jit(solution)/shard_map/ppermute | solution.py:177
  38.4 5.9 %collective-permute-start.3 = (bf16[48,512]{1,0:T(8,128)(2,1)S(1)}, bf16[48,512]{1,0:T(8,128)(2,1)S(1)}, u32[]{:S(2)}, u32[]{:S(2)}) collective-permute-start(bf16[48,512]{1,0:T(8,128)(2,1)S(1)} %bitcast.55), channel_id=1, source_target_pairs={{0,64},{64,128},{128,192},{192,0},{1,65},{65,129},{129,193},{193,1... | collective-permute-start | bytes 147464 | tf_op jit(solution)/shard_map/ppermute | solution.py:177
  45.5 8.8 %collective-permute-start.10 = (bf16[48,512]{1,0:T(8,128)(2,1)S(1)}, bf16[48,512]{1,0:T(8,128)(2,1)S(1)}, u32[]{:S(2)}, u32[]{:S(2)}) collective-permute-start(bf16[48,512]{1,0:T(8,128)(2,1)S(1)} %get-tuple-element.21), channel_id=1, source_target_pairs={{0,192},{64,0},{128,64},{192,128},{1,193},{65,1},{129,65},{193,129... | collective-permute-start | bytes 147464 | tf_op jit(solution)/shard_map/ppermute | solution.py:177
  54.3 22.9 %collective-permute-start.15 = (bf16[2,4,2,8,32,256]{5,4,3,2,1,0:T(8,128)(2,1)}, bf16[2,4,2,8,32,256]{5,4,3,2,1,0:T(8,128)(2,1)}, u32[]{:S(2)}, u32[]{:S(2)}) collective-permute-start(bf16[2,4,2,8,32,256]{5,4,3,2,1,0:T(8,128)(2,1)} %dynamic-slice_bitcast_fusion), channel_id=1, source_target_pairs={{0,2},{2,0},{1,3},{3,1},{4,6},{6,4},{5,7},{7,5},{8,10},{10,8},{9,1... | collective-permute-start | bytes 6291464 | tf_op jit(solution)/shard_map/ppermute | solution.py:177
  67.1 3.1 %collective-permute-start.14 = (bf16[2,4,2,8,32,128]{5,4,3,2,1,0:T(8,128)(2,1)}, bf16[2,4,2,8,32,128]{5,4,3,2,1,0:T(8,128)(2,1)}, u32[]{:S(2)}, u32[]{:S(2)}) collective-permute-start(bf16[2,4,2,8,32,128]{5,4,3,2,1,0:T(8,128)(2,1)} %dynamic-slice_bitcast_fusion.1), channel_id=1, source_target_pairs={{0,2},{2,0},{1,3},{3,1},{4,6},{6,4},{5,7},{7,5},{8,10},{10,8},{9,1... | collective-permute-start | bytes 3145736 | tf_op jit(solution)/shard_map/ppermute | solution.py:177
  72.7 22.7 %all-to-all-start = ((bf16[16,8,32,128]{3,2,1,0:T(8,128)(2,1)}), bf16[16,8,32,128]{3,2,1,0:T(8,128)(2,1)S(1)}, u32[]{:S(2)}, u32[]{:S(2)}) async-start(bf16[16,8,32,128]{3,2,1,0:T(8,128)(2,1)} %bitcast.7), calls=%async_computation | async-start | bytes 2097152 | tf_op jit(solution)/shard_map/all_to_all | solution.py:213
  96.3 34.0 %all-to-all-start.1 = ((bf16[16,8,32,256]{3,2,1,0:T(8,128)(2,1)}), bf16[16,8,32,256]{3,2,1,0:T(8,128)(2,1)S(1)}, u32[]{:S(2)}, u32[]{:S(2)}) async-start(bf16[16,8,32,256]{3,2,1,0:T(8,128)(2,1)} %bitcast.10), calls=%async_computation.1 | async-start | bytes 4194304 | tf_op jit(solution)/shard_map/all_to_all | solution.py:213
  102.2 24.2 %copy-start.10 = (bf16[16,8,32,128]{3,2,1,0:T(8,128)(2,1)S(1)}, bf16[16,8,32,128]{3,2,1,0:T(8,128)(2,1)}, u32[]{:S(2)}) copy-start(bf16[16,8,32,128]{3,2,1,0:T(8,128)(2,1)} %copy-done.9) | copy-start | bytes 3145732
  103.2 7.4 %collective-permute-start.7 = (bf16[2,3,3,1024]{3,2,1,0:T(4,128)(2,1)S(1)}, bf16[2,3,3,1024]{3,2,1,0:T(4,128)(2,1)S(1)}, u32[]{:S(2)}, u32[]{:S(2)}) collective-permute-start(bf16[2,3,3,1024]{3,2,1,0:T(4,128)(2,1)S(1)} %slice.125), channel_id=1, source_target_pairs={{0,2},{2,4},{4,6},{6,8},{8,10},{10,12},{12,14},{14,16},{16,18},{18... | collective-permute-start | bytes 110600 | tf_op jit(solution)/shard_map/ppermute | solution.py:177
  111.5 11.8 %collective-permute-start.8 = (bf16[2,1,12,1024]{3,2,1,0:T(8,128)(2,1)S(1)}, bf16[2,1,12,1024]{3,2,1,0:T(8,128)(2,1)S(1)}, u32[]{:S(2)}, u32[]{:S(2)}) collective-permute-start(bf16[2,1,12,1024]{3,2,1,0:T(8,128)(2,1)S(1)} %pad_maximum_fusion.9), channel_id=1, source_target_pairs={{0,64},{64,128},{128,192},{192,0},{1,65},{65,129},{129,193},{193,1... | collective-permute-start | bytes 147464 | tf_op jit(solution)/shard_map/ppermute | solution.py:177
  113.1 11.2 %collective-permute-start.11 = (bf16[2,6,6,512]{3,2,1,0:T(8,128)(2,1)S(1)}, bf16[2,6,6,512]{3,2,1,0:T(8,128)(2,1)S(1)}, u32[]{:S(2)}, u32[]{:S(2)}) collective-permute-start(bf16[2,6,6,512]{3,2,1,0:T(8,128)(2,1)S(1)} %slice.129), channel_id=1, source_target_pairs={{0,2},{2,4},{4,6},{6,8},{8,10},{10,12},{12,14},{14,16},{16,18},{18... | collective-permute-start | bytes 221192 | tf_op jit(solution)/shard_map/ppermute | solution.py:177
  125.0 9.9 %collective-permute-start.12 = (bf16[2,3,24,512]{3,2,1,0:T(8,128)(2,1)}, bf16[2,3,24,512]{3,2,1,0:T(8,128)(2,1)}, u32[]{:S(2)}, u32[]{:S(2)}) collective-permute-start(bf16[2,3,24,512]{3,2,1,0:T(8,128)(2,1)} %fusion.4), channel_id=1, source_target_pairs={{0,64},{64,128},{128,192},{192,0},{1,65},{65,129},{129,193},{193,1... | collective-permute-start | bytes 442376 | tf_op jit(solution)/shard_map/ppermute | solution.py:177
  125.7 27.3 %collective-permute-start.9 = (bf16[1,3,12,1024]{3,2,1,0:T(8,128)(2,1)}, bf16[1,3,12,1024]{3,2,1,0:T(8,128)(2,1)}, u32[]{:S(2)}, u32[]{:S(2)}) collective-permute-start(bf16[1,3,12,1024]{3,2,1,0:T(8,128)(2,1)} %get-tuple-element.50), channel_id=1, source_target_pairs={{0,1},{1,0},{2,3},{3,2},{4,5},{5,4},{6,7},{7,6},{8,9},{9,8},{10,11... | collective-permute-start | bytes 221192 | tf_op jit(solution)/shard_map/ppermute | solution.py:177
  131.5 14.0 %all-to-all-start.2 = ((bf16[8,32,384]{2,1,0:T(8,128)(2,1)}), bf16[8,32,384]{2,1,0:T(8,128)(2,1)S(1)}, u32[]{:S(2)}, u32[]{:S(2)}) async-start(bf16[8,32,384]{2,1,0:T(8,128)(2,1)} %pad_maximum_fusion.5), calls=%async_computation.2 | async-start | bytes 393216 | tf_op jit(solution)/shard_map/all_to_all | solution.py:253
  135.9 18.8 %collective-permute-start.13 = (bf16[1,6,24,512]{3,2,1,0:T(8,128)(2,1)S(1)}, bf16[1,6,24,512]{3,2,1,0:T(8,128)(2,1)S(1)}, u32[]{:S(2)}, u32[]{:S(2)}) collective-permute-start(bf16[1,6,24,512]{3,2,1,0:T(8,128)(2,1)S(1)} %get-tuple-element.44), channel_id=1, source_target_pairs={{0,1},{1,0},{2,3},{3,2},{4,5},{5,4},{6,7},{7,6},{8,9},{9,8},{10,11... | collective-permute-start | bytes 442376 | tf_op jit(solution)/shard_map/ppermute | solution.py:177
  146.2 12.5 %all-to-all-start.3 = ((bf16[8,32,384]{2,1,0:T(8,128)(2,1)}), bf16[8,32,384]{2,1,0:T(8,128)(2,1)S(1)}, u32[]{:S(2)}, u32[]{:S(2)}) async-start(bf16[8,32,384]{2,1,0:T(8,128)(2,1)} %broadcast_in_dim.2), calls=%async_computation.3 | async-start | bytes 393216 | tf_op jit(solution)/shard_map/all_to_all | solution.py:254
  (11 other events, 72.1 us)

commit v2 on v1

v2 whole, which is shorter than its diff:
```python
import jax
import jax.numpy as jnp
import numpy as np
from jax import lax
from jax.experimental import pallas as pl
from jax.experimental.pallas import tpu as pltpu
from jax.sharding import Mesh, PartitionSpec as P

HEADS = 16
LON = ("xh", "z", "core")
SCALE = 32 ** (-0.5)
LOW = jnp.bfloat16
WIDE = jnp.float32


def halves(fields):
    return np.concatenate([fields.reshape(-1), (fields + 1000).reshape(-1)])


def join(*parts):
    return np.concatenate([part.reshape(-1) for part in parts])


FINE_AT = np.arange(288).reshape(2, 6, 24)
CELL_AT = 1000 + np.arange(72).reshape(2, 3, 12)


def arrived(source, rows):
    fine = 1000 * source + np.arange(72).reshape(3, 24)
    cells = 1000 * source + 72 + np.arange(12 * rows).reshape(rows, 12)
    return fine, cells, 12 * rows


def shift_in():
    grp, lat, both = arrived(3, 2), arrived(4, 1), arrived(5, 1)
    first = [
        join(FINE_AT[0, 3:], halves(CELL_AT[0, 1:])),
        join(FINE_AT[1, :3], halves(CELL_AT[1, :1])),
        join(FINE_AT[0, :3], halves(CELL_AT[0, :1])),
    ]
    fine = np.stack([np.concatenate([FINE_AT[1, 3:], lat[0]]), np.concatenate([grp[0], both[0]])])
    left = np.stack([np.concatenate([CELL_AT[1, 1:], lat[1]]), np.concatenate([grp[1], both[1]])])
    right = np.stack(
        [np.concatenate([CELL_AT[1, 1:] + 1000, lat[1] + lat[2]]), np.concatenate([grp[1] + grp[2], both[1] + both[2]])]
    )
    second = join(fine[:, :, :6], left[:, :, :3], right[:, :, :3])
    lon_fine = 6000 + np.arange(72).reshape(2, 6, 6)
    lon_cells = 6072 + np.arange(18).reshape(2, 3, 3)
    fine = np.concatenate([fine[:, :, 6:], lon_fine], axis=2)
    left = np.concatenate([left[:, :, 3:], lon_cells], axis=2)
    right = np.concatenate([right[:, :, 3:], lon_cells + 18], axis=2)
    windows = fine.reshape(2, 6, 2, 12).transpose(2, 0, 1, 3)
    return join(*first), second, windows.reshape(-1), join(left, right)


def shift_out():
    first = join(FINE_AT[:, :, 18:], CELL_AT[:, :, 9:], CELL_AT[:, :, 9:] + 1000)
    lon_fine = 6000 + np.arange(72).reshape(2, 6, 6)
    lon_cells = 6072 + np.arange(18).reshape(2, 3, 3)
    fine = np.concatenate([lon_fine, FINE_AT[:, :, :18]], axis=2)
    left = np.concatenate([lon_cells, CELL_AT[:, :, :9]], axis=2)
    right = np.concatenate([lon_cells + 18, CELL_AT[:, :, :9] + 1000], axis=2)
    second = join(
        fine[1, :3], left[1, :2], right[1, :2], fine[0, 3:], left[0, 2], right[0, 2], fine[1, 3:], left[1, 2], right[1, 2]
    )
    grp, lat, both = arrived(3, 2), arrived(4, 1), arrived(5, 1)
    fine = np.stack([np.concatenate([both[0], grp[0]]), np.concatenate([lat[0], fine[0, :3]])])
    left = np.stack([np.concatenate([both[1], grp[1]]), np.concatenate([lat[1], left[0, :2]])])
    right = np.stack(
        [np.concatenate([both[1] + both[2], grp[1] + grp[2]]), np.concatenate([lat[1] + lat[2], right[0, :2]])]
    )
    return first, second, join(fine, left, right)


def block_maps():
    natural = np.arange(288).reshape(2, 6, 24)
    windows = natural.reshape(2, 6, 2, 12).transpose(2, 0, 1, 3).reshape(288)
    extended = np.concatenate([1000 + np.arange(48).reshape(2, 1, 24), natural[:, :5]], axis=1)
    to_cells = extended.reshape(2, 3, 2, 12, 2).transpose(4, 2, 0, 1, 3).reshape(288)
    from_cells = np.full(336, -1)
    from_cells[np.where(to_cells < 1000, to_cells, to_cells - 712)] = np.arange(288)
    replaced = natural.copy()
    replaced[:, 5] = 1000 + np.arange(48).reshape(2, 24)
    return np.argsort(windows), to_cells, from_cells, replaced.reshape(288)[windows]


def row_table():
    columns = [*shift_in(), *shift_out(), *block_maps()]
    table = np.full((432, len(columns)), -1, np.int32)
    for at, column in enumerate(columns):
        table[: len(column), at] = column
    return table


TABLE = row_table()
(
    IN_FIRST, IN_SECOND, IN_WINDOWS, IN_CELLS, OUT_FIRST, OUT_SECOND, OUT_ALL,
    FROM_WINDOWS, TO_CELLS, FROM_CELLS, UPSTREAM,
) = range(11)
ROWS = [int((TABLE[:, at] >= 0).sum()) for at in range(11)]
ROWS[FROM_CELLS] = 336


def gather(table, column, sources):
    names = table[: ROWS[column], column : column + 1]
    total = 0.0
    for source, value in sources.items():
        place = lax.broadcasted_iota(jnp.int32, (ROWS[column], value.shape[0]), 1) + 1000 * source
        total += dot_nn((names == place).astype(WIDE).astype(LOW), value)
    return total


def dot_nn(a, b):
    return lax.dot_general(a, b, (((1,), (0,)), ((), ())), preferred_element_type=WIDE)


def dot_nt(a, b):
    return lax.dot_general(a, b, (((1,), (1,)), ((), ())), preferred_element_type=WIDE)


def dot_tn(a, b):
    return lax.dot_general(a, b, (((0,), (0,)), ((), ())), preferred_element_type=WIDE)


def head_masks():
    head = lax.broadcasted_iota(jnp.int32, (144, 128), 1) >> 5
    return [(head == h).astype(WIDE).astype(LOW) for h in range(4)]


def normalize(values):
    centred = values - jnp.mean(values, axis=-1, keepdims=True)
    inverse_std = lax.rsqrt(jnp.mean(centred * centred, axis=-1, keepdims=True) + 1e-05)
    return (centred * inverse_std, inverse_std)


def own(tokens, cells):
    return {0: tokens[...], 1: cells[:, :512], 2: cells[:, 512:]}


def arrivals(grp, lat, both):
    return {3: grp[...], 4: lat[...], 5: both[...]}


def store_planes(packed, grp, lat, both):
    grp[...] = packed[:120].astype(LOW)
    lat[...] = packed[120:216].astype(LOW)
    both[...] = packed[216:].astype(LOW)


def planes_in_kernel(table, tokens, cells, *outs):
    store_planes(gather(table, IN_FIRST, own(tokens, cells)), *outs)


def columns_in_kernel(table, tokens, cells, grp, lat, both, out):
    out[...] = gather(table, IN_SECOND, own(tokens, cells) | arrivals(grp, lat, both)).astype(LOW)


def columns_out_kernel(table, tokens, cells, out):
    out[...] = gather(table, OUT_FIRST, own(tokens, cells)).astype(LOW)


def planes_out_kernel(table, tokens, cells, lon, *outs):
    store_planes(gather(table, OUT_SECOND, own(tokens, cells) | {6: lon[...]}), *outs)


def all_out_kernel(table, tokens, cells, grp, lat, both, lon, fine, coarse):
    packed = gather(table, OUT_ALL, own(tokens, cells) | arrivals(grp, lat, both) | {6: lon[...]})
    fine[...] = packed[:288].astype(LOW)
    coarse[:, :512] = packed[288:360].astype(LOW)
    coarse[:, 512:] = packed[360:].astype(LOW)


def shift_cotangent(core, table, sources, shifted, kept, sent, columns, picked):
    packed = gather(table, IN_CELLS, sources)
    cotangent = jnp.concatenate([packed[:72], packed[72:]], axis=1)
    shifted[...] = cotangent.astype(LOW)
    columns[...] = cotangent.T.astype(LOW)
    for out, parity in ((kept, core[0]), (sent, 1 - core[0])):
        for g in range(2):
            for m in range(16):
                at = pl.multiple_of(64 * m + 32 * parity + 16 * g, 16)
                picked[16 * m : 16 * m + 16] = columns[pl.ds(at, 16)]
            out[g] = picked[...].astype(WIDE).T.astype(LOW)


def forward_kernel(
    core, table, tokens, cells, grp, lat, both, lon, row_labels, column_labels, far_inward, far_outward,
    block, last_row, windows, projected, far_attention, attended, shifted, kept, sent,
    inward, outward, attention, columns, picked, weights_in, shares_out,
):
    fetches = [
        pltpu.make_async_copy(far_inward, inward, weights_in.at[0]),
        pltpu.make_async_copy(far_outward, outward, weights_in.at[1]),
    ]
    for copy in fetches:
        copy.start()
    stores = []
    arrived_parts = arrivals(grp, lat, both) | {6: lon[...]}
    values = gather(table, IN_WINDOWS, {0: tokens[...]} | arrived_parts)
    windows[...] = values.astype(LOW)
    normed = normalize(values)[0].astype(LOW)
    fetches[0].wait()
    projected[...] = dot_nn(normed, inward[...]).astype(LOW)
    masks = head_masks()
    for w in range(2):
        rows = slice(144 * w, 144 * w + 144)
        allowed = column_labels[w] == row_labels[w]
        for t in range(4):
            query = projected[rows, 128 * t : 128 * t + 128]
            key = projected[rows, 512 + 128 * t : 640 + 128 * t]
            value_t = projected[rows, 1024 + 128 * t : 1152 + 128 * t].T
            parts = []
            for h in range(4):
                scores = dot_nt(key * masks[h], query) * SCALE
                scores = jnp.where(allowed, scores, -1e30)
                weights = jnp.exp(scores - jnp.max(scores, axis=0, keepdims=True))
                share = weights * (1.0 / jnp.sum(weights, axis=0, keepdims=True))
                share = share.astype(LOW)
                attention[w, 4 * t + h] = share
                parts.append(dot_nn(value_t[32 * h : 32 * h + 32], share))
            attended[rows, 128 * t : 128 * t + 128] = jnp.concatenate(parts, axis=0).T.astype(LOW)
            heads = pl.ds(4 * t, 4)
            store = pltpu.make_async_copy(attention.at[w, heads], far_attention.at[w, heads], shares_out.at[w, t])
            store.start()
            stores.append(store)
    fetches[1].wait()
    result = (values + dot_nn(attended[...], outward[...])).astype(LOW)
    natural = gather(table, FROM_WINDOWS, {0: result})
    block[...] = natural.astype(LOW)
    last_row[...] = jnp.concatenate([natural[120:144], natural[264:]], axis=0).astype(LOW)
    cell_parts = {1: cells[:, :512], 2: cells[:, 512:]} | arrived_parts
    shift_cotangent(core, table, cell_parts, shifted, kept, sent, columns, picked)
    for store in stores:
        store.wait()


def merge_kernel(table, block, prior, upstream, columns, other_columns, normed, bundle, back, back_row):
    merged = gather(table, TO_CELLS, {0: block[...], 1: prior[...]})
    pieces = [merged[72 * k : 72 * k + 72] for k in range(4)]
    exact, inverse_std = normalize(jnp.concatenate(pieces, axis=1))
    normed[...] = exact.astype(LOW)
    for k in range(8):
        bundle[k, 0] = columns[k % 2]
        bundle[k, 1] = other_columns[k % 2]
        for half in range(2):
            at = 512 * (k // 2) + 256 * half
            bundle[k, 2 + half] = exact[:, at : at + 256].astype(LOW)
    grads = upstream[...]
    grads = inverse_std * (
        grads
        - jnp.mean(grads, axis=-1, keepdims=True)
        - exact * jnp.mean(grads * exact, axis=-1, keepdims=True)
    )
    stacked = jnp.concatenate([grads[:, 512 * k : 512 * k + 512] for k in range(4)], axis=0)
    stacked = stacked.astype(LOW)
    positions = gather(table, FROM_CELLS, {0: stacked})
    back[...] = positions[:288].astype(LOW)
    back_row[...] = positions[288:].astype(LOW)


def merging_kernel(xh, bundle, other_normed, kept, sent, total):
    for half in range(2):
        terms = 0.0
        for k in range(8):
            terms += dot_tn(bundle[k, 0], bundle[k, 2 + half]) + dot_tn(bundle[k, 1], other_normed[k, half])
        terms = terms.astype(LOW)
        for m in range(16):
            total[32 * m + 16 * half : 32 * m + 16 * half + 16] = terms[16 * m : 16 * m + 16]
    kept[...] = total[pl.ds(pl.multiple_of(256 * xh[0], 256), 256)]
    sent[...] = total[pl.ds(pl.multiple_of(256 - 256 * xh[0], 256), 256)]


def backward_kernel(
    core, table, back, next_row, windows, projected, far_attention, attended, far_inward, outward,
    token_grads, kept, sent, projected_back, inward_t, outward_t, attention, inward, shares_in, weight_in,
):
    loads = [pltpu.make_async_copy(far_attention.at[w], attention.at[w], shares_in.at[w]) for w in range(2)]
    loads.append(pltpu.make_async_copy(far_inward, inward, weight_in))
    for load in loads:
        load.start()
    upstream = gather(table, UPSTREAM, {0: back[...], 1: next_row[...]})
    upstream_low = upstream.astype(LOW)
    attended_back = dot_nt(upstream_low, outward[...]).astype(LOW)
    masks = head_masks()
    for w in range(2):
        rows = slice(144 * w, 144 * w + 144)
        loads[w].wait()
        for t in range(4):
            query = projected[rows, 128 * t : 128 * t + 128]
            key_t = projected[rows, 512 + 128 * t : 640 + 128 * t].T
            value = projected[rows, 1024 + 128 * t : 1152 + 128 * t]
            grads = attended_back[rows, 128 * t : 128 * t + 128]
            query_parts, key_back, value_back = [], 0.0, 0.0
            for h in range(4):
                low = attention[w, 4 * t + h]
                share = low.astype(WIDE)
                product = share * dot_nt(value * masks[h], grads)
                total = jnp.sum(product, axis=0, keepdims=True)
                score_back = ((product - share * total) * SCALE).astype(LOW)
                value_back += dot_nn(low, grads * masks[h])
                key_back += dot_nn(score_back, query * masks[h])
                query_parts.append(dot_nn(key_t[32 * h : 32 * h + 32], score_back))
            query_back = jnp.concatenate(query_parts, axis=0).T
            projected_back[rows, 128 * t : 128 * t + 128] = query_back.astype(LOW)
            projected_back[rows, 512 + 128 * t : 640 + 128 * t] = key_back.astype(LOW)
            projected_back[rows, 1024 + 128 * t : 1152 + 128 * t] = value_back.astype(LOW)
    normed, inverse_std = normalize(windows[...].astype(WIDE))
    normed_low = normed.astype(LOW)
    for j in range(4):
        inward_t[384 * j : 384 * j + 384] = dot_tn(projected_back[:, 384 * j : 384 * j + 384], normed_low).astype(LOW)
    outward_t[...] = dot_tn(upstream_low, attended[...]).astype(LOW)
    mine = core[0]
    for place in range(16):
        for terms, parity in ((kept, mine), (sent, 1 - mine)):
            at = 2 * place + parity
            for k in range(4):
                lanes = slice(128 * k, 128 * k + 128)
                head = pl.ds(pl.multiple_of(48 * at, 16), 32)
                tail = pl.ds(pl.multiple_of(48 * at + 32, 16), 16)
                last = pl.ds(pl.multiple_of(16 * at, 16), 16)
                terms[place // 8, k, 0, place % 8] = inward_t[head, lanes]
                terms[place // 8, k, 1, place % 8, 0:16] = inward_t[tail, lanes]
                terms[place // 8, k, 1, place % 8, 16:32] = outward_t[last, lanes]
    loads[2].wait()
    normed_back = dot_nt(projected_back[...], inward[...])
    branch = inverse_std * (
        normed_back
        - jnp.mean(normed_back, axis=-1, keepdims=True)
        - normed * jnp.mean(normed_back * normed, axis=-1, keepdims=True)
    )
    result = (upstream + branch.astype(LOW).astype(WIDE)).astype(LOW)
    token_grads[...] = gather(table, FROM_WINDOWS, {0: result}).astype(LOW)


def shares_kernel(shares, inward_grads, outward_grads, merging_grads):
    for k in range(4):
        lanes = slice(128 * k, 128 * k + 128)
        inward_grads[0:32, lanes] = shares[2 * k, :, :128].astype(WIDE)
        inward_grads[32:48, lanes] = shares[2 * k + 1, 0:16, :128].astype(WIDE)
        outward_grads[:, lanes] = shares[2 * k + 1, 16:32, :128].astype(WIDE)
        for g in range(2):
            for half in range(2):
                at = 512 * k + 256 * half
                part = shares[2 * k + g, 16 * half : 16 * half + 16, 128:]
                merging_grads[16 * g : 16 * g + 16, at : at + 256] = part.astype(WIDE)


def call(kernel, outs, *operands, scratch=(), scalars=0, room=8, far=(), far_outs=()):
    specs = [pl.BlockSpec()] * len(operands)
    for at in range(scalars):
        specs[at] = pl.BlockSpec(memory_space=pltpu.SMEM)
    for at in far:
        specs[at] = pl.BlockSpec(memory_space=pltpu.HBM)
    out_specs = [pl.BlockSpec(memory_space=pltpu.HBM) if at in far_outs else pl.BlockSpec() for at in range(len(outs))]
    return pl.pallas_call(
        kernel,
        in_specs=specs,
        out_specs=out_specs,
        out_shape=[
            jax.ShapeDtypeStruct(shape[:-1], WIDE) if shape[-1] is WIDE else jax.ShapeDtypeStruct(shape, LOW)
            for shape in outs
        ],
        scratch_shapes=[pltpu.VMEM(shape, LOW) if isinstance(shape, tuple) else shape for shape in scratch],
        compiler_params=pltpu.CompilerParams(vmem_limit_bytes=room * 1024 * 1024),
    )(*operands)


def from_behind(value, axis, steps):
    count = lax.axis_size(axis)
    pairs = [(source, (source + steps) % count) for source in range(count)]
    return lax.ppermute(value, axis, pairs)


def local_windows(layout):
    return layout.reshape(2, 6, 2, 12).transpose(2, 0, 1, 3).reshape(2, 144)


def to_neighbours(parts, steps):
    grp, lat, both = parts
    pairs = [
        (4 * 0 + 2 * row + level, (row + steps) % 4 * 2 + (level + steps) % 2) for row in range(4) for level in range(2)
    ]
    return (
        from_behind(grp, ("grp",), steps),
        from_behind(lat, ("lat",), steps),
        lax.ppermute(both, ("lat", "grp"), pairs),
    )


PLANES = [(120, 512), (96, 512), (96, 512)]


def shift_forward(table, tokens, cells):
    parts = to_neighbours(call(planes_in_kernel, PLANES, table, tokens, cells), -1)
    (columns,) = call(columns_in_kernel, [(108, 512)], table, tokens, cells, *parts)
    return (*parts, from_behind(columns, LON, -1))


def wide_sum(parts):
    return jnp.sum(parts.astype(WIDE), axis=0).astype(LOW)


def over_planes(terms):
    terms = terms.reshape((16,) + terms.shape[3:])
    return wide_sum(lax.all_to_all(terms, ("xh", "lat", "grp"), 0, 0))


def tied(*values):
    return lax.optimization_barrier(values)


def body(fine_tokens, region_ids, inward_weight, outward_weight, merging_weight, coarse_cotangent):
    table = jnp.asarray(TABLE)
    core = lax.axis_index("core").reshape(1)
    tokens = fine_tokens.reshape(288, 512)
    cells = coarse_cotangent.reshape(72, 1024)
    parts = shift_forward(table, tokens, cells)
    labels = local_windows(region_ids)
    block, last_row, windows, projected, attention, attended, shifted, columns, sent_columns = call(
        forward_kernel,
        [
            (288, 512), (48, 512), (288, 512), (288, 1536), (2, HEADS, 144, 144), (288, 512),
            (72, 1024), (2, 72, 256), (2, 72, 256),
        ],
        core, table, tokens, cells, *parts, labels.reshape(2, 1, 144), labels.reshape(2, 144, 1), inward_weight, outward_weight,
        scratch=[
            (512, 1536), (512, 512), (2, HEADS, 144, 144), (1024, 72), (256, 72),
            pltpu.SemaphoreType.DMA((2,)), pltpu.SemaphoreType.DMA((2, 4)),
        ],
        scalars=1, room=54, far=(10, 11), far_outs=(4,),
    )
    prior = from_behind(last_row, ("lat",), 1)
    other_columns = from_behind(sent_columns, ("core",), 1)
    merged_upstream = dot_nt(shifted, merging_weight)
    merged_normed, bundle, back, back_row = call(
        merge_kernel,
        [(72, 2048), (8, 4, 72, 256), (288, 512), (48, 512)],
        table, block, prior, merged_upstream, columns, other_columns,
    )
    next_row = from_behind(back_row, ("lat",), -1)
    next_row, bundle = tied(next_row, bundle)
    bundle = lax.all_to_all(bundle, ("lat", "grp"), 0, 0)
    token_grads, kept, sent = call(
        backward_kernel,
        [(288, 512), (2, 4, 2, 8, 32, 128), (2, 4, 2, 8, 32, 128)],
        core, table, back, next_row, windows, projected, attention, attended, inward_weight, outward_weight,
        scratch=[
            (288, 1536), (1536, 512), (512, 512), (2, HEADS, 144, 144), (512, 1536),
            pltpu.SemaphoreType.DMA((2,)), pltpu.SemaphoreType.DMA,
        ],
        scalars=1, room=54, far=(6, 8),
    )
    merged_normed, token_grads = tied(merged_normed, token_grads)
    coarse_field = dot_nn(merged_normed, merging_weight).astype(LOW)
    kept, sent, bundle, coarse_field = tied(kept, sent, bundle, coarse_field)
    came = from_behind(sent, ("core",), 1)
    block_terms = (kept.astype(WIDE) + came.astype(WIDE)).astype(LOW)
    block_planes = over_planes(block_terms)
    other_normed = from_behind(bundle[:, 2:], ("core",), 1)
    merging_kept, merging_sent = call(
        merging_kernel,
        [(256, 256), (256, 256)],
        lax.axis_index("xh").reshape(1), bundle, other_normed,
        scratch=[(512, 256)], scalars=1,
    )
    merging_came = from_behind(merging_sent, ("xh",), 1)
    (lon_out,) = call(columns_out_kernel, [(108, 512)], table, token_grads, coarse_field)
    lon_out = from_behind(lon_out, LON, 1)
    parts_out = call(planes_out_kernel, PLANES, table, token_grads, coarse_field, lon_out)
    block_planes, merging_came, *parts_out = tied(block_planes, merging_came, *parts_out)
    parts_out = to_neighbours(parts_out, 1)
    merging_planes = (merging_kept.astype(WIDE) + merging_came.astype(WIDE)).astype(LOW).reshape(8, 32, 256)
    planes = jnp.concatenate([block_planes, merging_planes], axis=2)
    share = wide_sum(lax.all_to_all(planes, ("z",), 0, 0))
    share, *parts_out = tied(share, *parts_out)
    shares = lax.all_to_all(jnp.broadcast_to(share[None], (8, 32, 384)), ("lat", "grp"), 0, 0)
    token_grads, coarse_field = call(
        all_out_kernel, [(288, 512), (72, 1024)], table, token_grads, coarse_field, *parts_out, lon_out
    )
    grads = call(shares_kernel, [(48, 512, WIDE), (16, 512, WIDE), (32, 2048, WIDE)], shares)
    return (
        coarse_field.reshape(2, 3, 12, 1024),
        token_grads.reshape(2, 6, 24, 512),
        *(share.T for share in grads),
    )


def solution(mesh):
    fine = Mesh(mesh.devices.reshape(4, 2, 8, 2, 2), ("lat", "xh", "z", "core", "grp"))
    return jax.shard_map(
        body,
        mesh=fine,
        in_specs=(
            P("grp", "lat", LON, None),
            P("grp", "lat", LON),
            P(),
            P(),
            P(),
            P("grp", "lat", LON, None),
        ),
        out_specs=(
            P("grp", "lat", LON, None),
            P("grp", "lat", LON, None),
            P(None, LON),
            P(None, LON),
            P(None, LON),
        ),
        check_vma=False,
    )
```

time: 162 us -> 125 us (0.77)
  waiting for transfers between devices: 60.3 us -> 37.6 us
  other arithmetic: 15.8 us -> 3.42 us
  local copies, waits for them, and re-layouts: 16.5 us -> 8.11 us
  Pallas kernels: 23.1 us -> 31.3 us
  starting transfers between devices: 43.3 us -> 37.6 us
  matrix products: 1.4 us -> 4.54 us
    ppermute x16 -> x12, waiting for transfers between devices: 32.4 us -> 19.2 us  [from_behind(): return lax.ppermute(value, axis, pairs)]
    all_to_all x2, waiting for transfers between devices: 16.7 us -> 7.22 us  [the longest x1 4.54 us: over_planes(): return wide_sum(lax.all_to_all(terms, ('xh', 'lat', 'grp'), 0, 0))]
    pallas_call x4 -> x10, Pallas kernels: 23.1 us -> 31.3 us  [call(): pl.pallas_call(kernel, in_specs=specs, out_specs=out_specs, out_shape=[ja...]
    ppermute x16 -> x12, starting transfers between devices: 23.4 us -> 15.5 us  [from_behind(): return lax.ppermute(value, axis, pairs)]
    concatenate x15 -> x1, other arithmetic: 6.58 us -> 0.7 us  [body(): planes = jnp.concatenate([block_planes, merging_planes], axis=2)]
    slice x9 -> x1, local copies, waits for them, and re-layouts: 5.88 us -> 0.04 us  [body(): other_normed = from_behind(bundle[:, 2:], ('core',), 1)]
    convert_element_type x3 -> x2, other arithmetic: 7.1 us -> 1.31 us  [the longest x1 1.27 us: body(): block_terms = (kept.astype(WIDE) + came.astype(WIDE)).astype(LOW)]
    squeeze x2 -> x0, local copies, waits for them, and re-layouts: 4.12 us -> none  [over_planes(): sent = lax.dynamic_index_in_dim(terms, 1 - core, 0, keepdims=False)]
  transfers between devices with their start and end apart: 20 -> 18, of which waited for: 12 -> 12; matrix products, arithmetic and copies ran while one was open for 17% -> 7% of each run, Pallas kernels for 9% -> 13%
where the time goes in v2:
time: 125 us; the launch traced here: 123 us
  starting transfers between devices  37.6 us (30%)
  waiting for transfers between devices  37.6 us (30%)
  Pallas kernels  31.3 us (25%)
  local copies, waits for them, and re-layouts  8.11 us (6%)
  matrix products  4.54 us (4%)
  other arithmetic  3.42 us (3%)
    pallas_call x10, Pallas kernels, call(): pl.pallas_call(kernel, in_specs=specs, out_specs=out_specs, out_shape=[ja...  31.3 us
    ppermute x12, waiting for transfers between devices, from_behind(): return lax.ppermute(value, axis, pairs)  19.2 us
    ppermute x12, starting transfers between devices, from_behind(): return lax.ppermute(value, axis, pairs)  15.5 us
    all_to_all x1, waiting for transfers between devices, body(): share = wide_sum(lax.all_to_all(planes, ('z',), 0, 0))  6.9 us
    all_to_all x1, starting transfers between devices, body(): bundle = lax.all_to_all(bundle, ('lat', 'grp'), 0, 0)  5.77 us
    all_to_all x1, starting transfers between devices, over_planes(): return wide_sum(lax.all_to_all(terms, ('xh', 'lat', 'grp'), 0, 0))  5.23 us
    unnamed x34, local copies, waits for them, and re-layouts  5.09 us
    all_to_all x1, waiting for transfers between devices, over_planes(): return wide_sum(lax.all_to_all(terms, ('xh', 'lat', 'grp'), 0, 0))  4.54 us
  transfers between devices with their start and end apart: 18, of which 12 were waited for; matrix products, arithmetic and copies ran while one was open for 7% of the time, Pallas kernels for 13%

profile of v2, /device:TPU:2, one launch (start us, length us, event | category | flops | bytes accessed | tf_op | source)
XLA Modules:
  0.0 123.5 jit_solution(8888314600006285408)
XLA Ops:
  4.2 2.4 %collective-permute-start = (bf16[120,512]{1,0:T(8,128)(2,1)S(1)}, bf16[120,512]{1,0:T(8,128)(2,1)S(1)}, u32[]{:S(2)}, u32[]{:S(2)}) collective-permute-start(bf16[120,512]{1,0:T(8,128)(2,1)S(1)} %get-tuple-element.51), channel_id=1, source_target_pairs={{0,1},{1,0},{2,3},{3,2},{4,5},{5,4},{6,7},{7,6},{8,9},{9,8},{10,11... | collective-permute-start | bytes 368648 | tf_op jit(solution)/shard_map/ppermute | solution.py:371
  7.8 1.7 %collective-permute-start.2 = (bf16[96,512]{1,0:T(8,128)(2,1)S(1)}, bf16[96,512]{1,0:T(8,128)(2,1)S(1)}, u32[]{:S(2)}, u32[]{:S(2)}) collective-permute-start(bf16[96,512]{1,0:T(8,128)(2,1)S(1)} %get-tuple-element.53), channel_id=1, source_target_pairs={{0,193},{1,192},{64,1},{65,0},{128,65},{129,64},{192,129},{193,128... | collective-permute-start | bytes 294920 | tf_op jit(solution)/shard_map/ppermute | solution.py:386
  9.5 2.7 %collective-permute-done.1.lat = bf16[96,512]{1,0:T(8,128)(2,1)S(1)} collective-permute-done((bf16[96,512]{1,0:T(8,128)(2,1)S(1)}, bf16[96,512]{1,0:T(8,128)(2,1)S(1)}, u32[]{:S(2)}, u32[]{:S(2)}) %collective-permute-start.1) | collective-permute-done | bytes 98336 | tf_op jit(solution)/shard_map/ppermute | solution.py:371
  13.7 5.5 %collective-permute-start.3 = (bf16[108,512]{1,0:T(8,128)(2,1)S(1)}, bf16[108,512]{1,0:T(8,128)(2,1)S(1)}, u32[]{:S(2)}, u32[]{:S(2)}) collective-permute-start(bf16[108,512]{1,0:T(8,128)(2,1)S(1)} %shard_map.111), channel_id=1, source_target_pairs={{0,62},{2,0},{4,2},{6,4},{8,6},{10,8},{12,10},{14,12},{16,14},{18,... | collective-permute-start | bytes 331784 | tf_op jit(solution)/shard_map/ppermute | solution.py:371
  22.3 11.1 %shard_map.112 = (bf16[288,512]{1,0:T(8,128)(2,1)}, bf16[48,512]{1,0:T(8,128)(2,1)}, bf16[288,512]{1,0:T(8,128)(2,1)}, bf16[288,1536]{1,0:T(8,128)(2,1)}, bf16[2...) custom-call(s32[1]{0:T(128)} %bitcast.core, ...), custom_call_target="tpu_custom_call" | custom-call | tf_op jit(solution)/shard_map/pallas_call | solution.py:355
  34.4 3.7 %fusion.upstream = f32[72,2048]{1,0:T(8,128)S(1)} fusion(bf16[72,1024]{1,0:T(8,128)(2,1)} %get-tuple-element.56, bf16[2048,1024]{1,0:T(8,128)(2,1)} %param.11), kind=kOutput, calls=%fused_computation.5 | convolution fusion | flops 301989888 | bytes 4931584 | tf_op jit(solution)/shard_map/dot_general | solution.py:118
  39.0 2.2 %shard_map.113 = (bf16[72,2048]{1,0:T(8,128)(2,1)S(1)}, bf16[8,4,72,256]{3,2,1,0:T(8,128)(2,1)}, bf16[288,512]{1,0:T(8,128)(2,1)S(1)}, bf16[48,512]{1,0:T(8,128)(2,1)S(1)}) custom-call(s32[432,11]{1,0:T(8,128)S(1)} %copy-done.1, bf16[288,512]{1,0:T(8,128)(2,1)S(1)} %copy-done.10, bf16[48,512]{1,0:T(8,128)(2,1)S(1)} %collective-permute-done.4.prior, ...), custom_call_target="tpu_custom_call" | custom-call | tf_op jit(solution)/shard_map/pallas_call | solution.py:355
  41.9 1.4 %collective-permute-start.6 = (bf16[48,512]{1,0:T(8,128)(2,1)S(1)}, bf16[48,512]{1,0:T(8,128)(2,1)S(1)}, u32[]{:S(2)}, u32[]{:S(2)}) collective-permute-start(bf16[48,512]{1,0:T(8,128)(2,1)S(1)} %get-tuple-element.61), channel_id=1, source_target_pairs={{0,192},{64,0},{128,64},{192,128},{1,193},{65,1},{129,65},{193,129... | collective-permute-start | bytes 147464 | tf_op jit(solution)/shard_map/ppermute | solution.py:371
  43.4 2.7 %collective-permute-done.6.next_row = bf16[48,512]{1,0:T(8,128)(2,1)S(1)} collective-permute-done((bf16[48,512]{1,0:T(8,128)(2,1)S(1)}, bf16[48,512]{1,0:T(8,128)(2,1)S(1)}, u32[]{:S(2)}, u32[]{:S(2)}) %collective-permute-start.6) | collective-permute-done | bytes 49184 | tf_op jit(solution)/shard_map/ppermute | solution.py:371
  46.0 5.8 %all-to-all-start = ((bf16[8,4,72,256]{3,2,1,0:T(8,128)(2,1)}), bf16[8,4,72,256]{3,2,1,0:T(8,128)(2,1)S(1)}, u32[]{:S(2)}, u32[]{:S(2)}) async-start(bf16[8,4,72,256]{3,2,1,0:T(8,128)(2,1)} %get-tuple-element.72), calls=%async_computation | async-start | bytes 2359296 | tf_op jit(solution)/shard_map/all_to_all | solution.py:442
  51.8 12.2 %shard_map.114 = (bf16[288,512]{1,0:T(8,128)(2,1)}, bf16[2,4,2,8,32,128]{5,4,3,2,1,0:T(8,128)(2,1)}, bf16[2,4,2,8,32,128]{5,4,3,2,1,0:T(8,128)(2,1)}) custom-call(s32[1]{0:T(128)} %bitcast.core, s32[432,11]{1,0:T(8,128)} %constant.14.clone.table, bf16[288,512]{1,0:T(8,128)(2,1)} %copy-done.9, bf16[48,512]{1,0:T(8,128)(2,1)} %copy-done.15, ...), custom_call_target="tpu_custom_call" | custom-call | tf_op jit(solution)/shard_map/pallas_call | solution.py:355
  64.9 2.7 %all-to-all-done.bundle = bf16[8,4,72,256]{3,2,1,0:T(8,128)(2,1)S(1)} async-done(((bf16[8,4,72,256]{3,2,1,0:T(8,128)(2,1)}), bf16[8,4,72,256]{3,2,1,0:T(8,128)(2,1)S(1)}, u32[]{:S(2)}, u32[]{:S(2)}) %all-to-all-start) | async-done | bytes 1179680 | tf_op jit(solution)/shard_map/all_to_all | solution.py:442
  67.6 2.9 %collective-permute-done.7 = bf16[2,4,2,8,32,128]{5,4,3,2,1,0:T(8,128)(2,1)S(1)} collective-permute-done((bf16[2,4,2,8,32,128]{5,4,3,2,1,0:T(8,128)(2,1)}, bf16[2,4,2,8,32,128]{5,4,3,2,1,0:T(8,128)(2,1)S(1)}, u32[]{:S(2)}, u32[]{:S(2)}) %collective-permute-start.7) | collective-permute-done | bytes 1048608 | tf_op jit(solution)/shard_map/ppermute | solution.py:371
  71.8 5.2 %all-to-all-start.1 = ((bf16[16,8,32,128]{3,2,1,0:T(8,128)(2,1)}), bf16[16,8,32,128]{3,2,1,0:T(8,128)(2,1)}, u32[]{:S(2)}, u32[]{:S(2)}) async-start(bf16[16,8,32,128]{3,2,1,0:T(8,128)(2,1)} %bitcast.3), calls=%async_computation.1 | async-start | bytes 2097152 | tf_op jit(solution)/shard_map/all_to_all | solution.py:405
  77.1 2.0 %collective-permute-done.8.other_normed = bf16[8,2,72,256]{3,2,1,0:T(8,128)(2,1)S(1)} collective-permute-done((bf16[8,2,72,256]{3,2,1,0:T(8,128)(2,1)S(1)}, bf16[8,2,72,256]{3,2,1,0:T(8,128)(2,1)S(1)}, u32[]{:S(2)}, u32[]{:S(2)}) %collective-permute-start.8) | collective-permute-done | bytes 589856 | tf_op jit(solution)/shard_map/ppermute | solution.py:371
  80.4 2.4 %collective-permute-start.9 = (bf16[256,256]{1,0:T(8,128)(2,1)S(1)}, bf16[256,256]{1,0:T(8,128)(2,1)S(1)}, u32[]{:S(2)}, u32[]{:S(2)}) collective-permute-start(bf16[256,256]{1,0:T(8,128)(2,1)S(1)} %get-tuple-element.78), channel_id=1, source_target_pairs={{0,32},{32,0},{1,33},{33,1},{2,34},{34,2},{3,35},{35,3},{4,36},{36... | collective-permute-start | bytes 393224 | tf_op jit(solution)/shard_map/ppermute | solution.py:371
  83.3 7.9 %collective-permute-done.10.lon = bf16[108,512]{1,0:T(8,128)(2,1)S(1)} collective-permute-done((bf16[108,512]{1,0:T(8,128)(2,1)S(1)}, bf16[108,512]{1,0:T(8,128)(2,1)S(1)}, u32[]{:S(2)}, u32[]{:S(2)}) %collective-permute-start.10) | collective-permute-done | bytes 110624 | tf_op jit(solution)/shard_map/ppermute | solution.py:371
  91.9 4.5 %all-to-all-done.1 = bf16[16,8,32,128]{3,2,1,0:T(8,128)(2,1)} async-done(((bf16[16,8,32,128]{3,2,1,0:T(8,128)(2,1)}), bf16[16,8,32,128]{3,2,1,0:T(8,128)(2,1)}, u32[]{:S(2)}, u32[]{:S(2)}) %all-to-all-start.1) | async-done | bytes 1048608 | tf_op jit(solution)/shard_map/all_to_all | solution.py:405
  98.5 3.4 %all-to-all-start.2 = ((bf16[8,32,384]{2,1,0:T(8,128)(2,1)}), bf16[8,32,384]{2,1,0:T(8,128)(2,1)S(1)}, u32[]{:S(2)}, u32[]{:S(2)}) async-start(bf16[8,32,384]{2,1,0:T(8,128)(2,1)} %pad_maximum_fusion), calls=%async_computation.2 | async-start | bytes 393216 | tf_op jit(solution)/shard_map/all_to_all | solution.py:474
  103.3 1.5 %collective-permute-start.13 = (bf16[96,512]{1,0:T(8,128)(2,1)S(1)}, bf16[96,512]{1,0:T(8,128)(2,1)S(1)}, u32[]{:S(2)}, u32[]{:S(2)}) collective-permute-start(bf16[96,512]{1,0:T(8,128)(2,1)S(1)} %get-tuple-element.87), channel_id=1, source_target_pairs={{0,65},{1,64},{64,129},{65,128},{128,193},{129,192},{192,1},{193,0... | collective-permute-start | bytes 294920 | tf_op jit(solution)/shard_map/ppermute | solution.py:386
  104.7 6.9 %all-to-all-done.2 = bf16[8,32,384]{2,1,0:T(8,128)(2,1)S(1)} async-done(((bf16[8,32,384]{2,1,0:T(8,128)(2,1)}), bf16[8,32,384]{2,1,0:T(8,128)(2,1)S(1)}, u32[]{:S(2)}, u32[]{:S(2)}) %all-to-all-start.2) | async-done | bytes 196640 | tf_op jit(solution)/shard_map/all_to_all | solution.py:474
  112.4 4.5 %all-to-all-start.3 = ((bf16[8,32,384]{2,1,0:T(8,128)(2,1)}), bf16[8,32,384]{2,1,0:T(8,128)(2,1)S(1)}, u32[]{:S(2)}, u32[]{:S(2)}) async-start(bf16[8,32,384]{2,1,0:T(8,128)(2,1)} %broadcast_in_dim.2), calls=%async_computation.3 | async-start | bytes 393216 | tf_op jit(solution)/shard_map/all_to_all | solution.py:476
  116.9 1.8 %shard_map.118 = (bf16[288,512]{1,0:T(8,128)(2,1)}, bf16[72,1024]{1,0:T(8,128)(2,1)S(1)}) custom-call(s32[432,11]{1,0:T(8,128)S(1)} %copy-done.2, bf16[288,512]{1,0:T(8,128)(2,1)S(1)} %copy-done.4, bf16[72,1024]{1,0:T(8,128)(2,1)S(1)} %convolution_convert_fusion.cells, bf16[120,512]{1,0:T(8,128)(2,1)S(1)} %collective-permute-done.11.grp, ...), custom_call_target="tpu_custom_call" | custom-call | tf_op jit(solution)/shard_map/pallas_call | solution.py:355
  119.6 3.1 %all-to-all-done.3.shares = bf16[8,32,384]{2,1,0:T(8,128)(2,1)S(1)} async-done(((bf16[8,32,384]{2,1,0:T(8,128)(2,1)}), bf16[8,32,384]{2,1,0:T(8,128)(2,1)S(1)}, u32[]{:S(2)}, u32[]{:S(2)}) %all-to-all-start.3) | async-done | bytes 196640 | tf_op jit(solution)/shard_map/all_to_all | solution.py:476
  (71 shorter events, 22.4 us)
Async XLA Ops:
  1.6 20.0 %copy-start.5 = (bf16[72,1024]{1,0:T(8,128)(2,1)}, bf16[72,1024]{1,0:T(8,128)(2,1)S(1)}, u32[]{:S(2)}) copy-start(bf16[72,1024]{1,0:T(8,128)(2,1)S(1)} %reshape.40.cells) | copy-start | bytes 442372
  4.2 9.2 %collective-permute-start = (bf16[120,512]{1,0:T(8,128)(2,1)S(1)}, bf16[120,512]{1,0:T(8,128)(2,1)S(1)}, u32[]{:S(2)}, u32[]{:S(2)}) collective-permute-start(bf16[120,512]{1,0:T(8,128)(2,1)S(1)} %get-tuple-element.51), channel_id=1, source_target_pairs={{0,1},{1,0},{2,3},{3,2},{4,5},{5,4},{6,7},{7,6},{8,9},{9,8},{10,11... | collective-permute-start | bytes 368648 | tf_op jit(solution)/shard_map/ppermute | solution.py:371
  6.5 5.7 %collective-permute-start.1 = (bf16[96,512]{1,0:T(8,128)(2,1)S(1)}, bf16[96,512]{1,0:T(8,128)(2,1)S(1)}, u32[]{:S(2)}, u32[]{:S(2)}) collective-permute-start(bf16[96,512]{1,0:T(8,128)(2,1)S(1)} %get-tuple-element.52), channel_id=1, source_target_pairs={{0,192},{64,0},{128,64},{192,128},{1,193},{65,1},{129,65},{193,129... | collective-permute-start | bytes 294920 | tf_op jit(solution)/shard_map/ppermute | solution.py:371
  7.8 5.5 %collective-permute-start.2 = (bf16[96,512]{1,0:T(8,128)(2,1)S(1)}, bf16[96,512]{1,0:T(8,128)(2,1)S(1)}, u32[]{:S(2)}, u32[]{:S(2)}) collective-permute-start(bf16[96,512]{1,0:T(8,128)(2,1)S(1)} %get-tuple-element.53), channel_id=1, source_target_pairs={{0,193},{1,192},{64,1},{65,0},{128,65},{129,64},{192,129},{193,128... | collective-permute-start | bytes 294920 | tf_op jit(solution)/shard_map/ppermute | solution.py:386
  12.2 9.5 %copy-start.7 = (bf16[96,512]{1,0:T(8,128)(2,1)}, bf16[96,512]{1,0:T(8,128)(2,1)S(1)}, u32[]{:S(2)}) copy-start(bf16[96,512]{1,0:T(8,128)(2,1)S(1)} %collective-permute-done.1.lat) | copy-start | bytes 294916
  13.7 7.9 %collective-permute-start.3 = (bf16[108,512]{1,0:T(8,128)(2,1)S(1)}, bf16[108,512]{1,0:T(8,128)(2,1)S(1)}, u32[]{:S(2)}, u32[]{:S(2)}) collective-permute-start(bf16[108,512]{1,0:T(8,128)(2,1)S(1)} %shard_map.111), channel_id=1, source_target_pairs={{0,62},{2,0},{4,2},{6,4},{8,6},{10,8},{12,10},{14,12},{16,14},{18,... | collective-permute-start | bytes 331784 | tf_op jit(solution)/shard_map/ppermute | solution.py:371
  20.7 18.3 %copy-start.1 = (s32[432,11]{1,0:T(8,128)S(1)}, s32[432,11]{1,0:T(8,128)}, u32[]{:S(2)}) copy-start(s32[432,11]{1,0:T(8,128)} %constant.14.clone.table) | copy-start | bytes 57028
  33.4 5.6 %collective-permute-start.4 = (bf16[48,512]{1,0:T(8,128)(2,1)}, bf16[48,512]{1,0:T(8,128)(2,1)S(1)}, u32[]{:S(2)}, u32[]{:S(2)}) collective-permute-start(bf16[48,512]{1,0:T(8,128)(2,1)} %get-tuple-element.55), channel_id=1, source_target_pairs={{0,64},{64,128},{128,192},{192,0},{1,65},{65,129},{129,193},{193,1... | collective-permute-start | bytes 147464 | tf_op jit(solution)/shard_map/ppermute | solution.py:371
  34.4 4.6 %collective-permute-start.5 = (bf16[2,72,256]{2,1,0:T(8,128)(2,1)}, bf16[2,72,256]{2,1,0:T(8,128)(2,1)S(1)}, u32[]{:S(2)}, u32[]{:S(2)}) collective-permute-start(bf16[2,72,256]{2,1,0:T(8,128)(2,1)} %get-tuple-element.58), channel_id=1, source_target_pairs={{0,2},{2,0},{1,3},{3,1},{4,6},{6,4},{5,7},{7,5},{8,10},{10,8},{9,1... | collective-permute-start | bytes 221192 | tf_op jit(solution)/shard_map/ppermute | solution.py:371
  41.9 4.1 %collective-permute-start.6 = (bf16[48,512]{1,0:T(8,128)(2,1)S(1)}, bf16[48,512]{1,0:T(8,128)(2,1)S(1)}, u32[]{:S(2)}, u32[]{:S(2)}) collective-permute-start(bf16[48,512]{1,0:T(8,128)(2,1)S(1)} %get-tuple-element.61), channel_id=1, source_target_pairs={{0,192},{64,0},{128,64},{192,128},{1,193},{65,1},{129,65},{193,129... | collective-permute-start | bytes 147464 | tf_op jit(solution)/shard_map/ppermute | solution.py:371
  46.0 21.6 %all-to-all-start = ((bf16[8,4,72,256]{3,2,1,0:T(8,128)(2,1)}), bf16[8,4,72,256]{3,2,1,0:T(8,128)(2,1)S(1)}, u32[]{:S(2)}, u32[]{:S(2)}) async-start(bf16[8,4,72,256]{3,2,1,0:T(8,128)(2,1)} %get-tuple-element.72), calls=%async_computation | async-start | bytes 2359296 | tf_op jit(solution)/shard_map/all_to_all | solution.py:442
  51.8 12.3 %copy-start.12 = (bf16[2048,1024]{1,0:T(8,128)(2,1)S(1)}, bf16[2048,1024]{1,0:T(8,128)(2,1)}, u32[]{:S(2)}) copy-start(bf16[2048,1024]{1,0:T(8,128)(2,1)} %param.11) | copy-start | bytes 12582916
  64.9 17.9 %copy-start.2 = (s32[432,11]{1,0:T(8,128)S(1)}, s32[432,11]{1,0:T(8,128)}, u32[]{:S(2)}) copy-start(s32[432,11]{1,0:T(8,128)} %constant.14.clone.table) | copy-start | bytes 57028
  64.9 17.9 %copy-start.4 = (bf16[288,512]{1,0:T(8,128)(2,1)S(1)}, bf16[288,512]{1,0:T(8,128)(2,1)}, u32[]{:S(2)}) copy-start(bf16[288,512]{1,0:T(8,128)(2,1)} %get-tuple-element.69.tokens) | copy-start | bytes 884740
  67.6 2.9 %collective-permute-start.7 = (bf16[2,4,2,8,32,128]{5,4,3,2,1,0:T(8,128)(2,1)}, bf16[2,4,2,8,32,128]{5,4,3,2,1,0:T(8,128)(2,1)S(1)}, u32[]{:S(2)}, u32[]{:S(2)}) collective-permute-start(bf16[2,4,2,8,32,128]{5,4,3,2,1,0:T(8,128)(2,1)} %get-tuple-element.76), channel_id=1, source_target_pairs={{0,2},{2,0},{1,3},{3,1},{4,6},{6,4},{5,7},{7,5},{8,10},{10,8},{9,1... | collective-permute-start | bytes 3145736 | tf_op jit(solution)/shard_map/ppermute | solution.py:371
  71.8 24.6 %all-to-all-start.1 = ((bf16[16,8,32,128]{3,2,1,0:T(8,128)(2,1)}), bf16[16,8,32,128]{3,2,1,0:T(8,128)(2,1)}, u32[]{:S(2)}, u32[]{:S(2)}) async-start(bf16[16,8,32,128]{3,2,1,0:T(8,128)(2,1)} %bitcast.3), calls=%async_computation.1 | async-start | bytes 2097152 | tf_op jit(solution)/shard_map/all_to_all | solution.py:405
  77.0 2.1 %collective-permute-start.8 = (bf16[8,2,72,256]{3,2,1,0:T(8,128)(2,1)S(1)}, bf16[8,2,72,256]{3,2,1,0:T(8,128)(2,1)S(1)}, u32[]{:S(2)}, u32[]{:S(2)}) collective-permute-start(bf16[8,2,72,256]{3,2,1,0:T(8,128)(2,1)S(1)} %slice.3), channel_id=1, source_target_pairs={{0,2},{2,0},{1,3},{3,1},{4,6},{6,4},{5,7},{7,5},{8,10},{10,8},{9,1... | collective-permute-start | bytes 1769480 | tf_op jit(solution)/shard_map/ppermute | solution.py:371
  80.4 17.3 %collective-permute-start.9 = (bf16[256,256]{1,0:T(8,128)(2,1)S(1)}, bf16[256,256]{1,0:T(8,128)(2,1)S(1)}, u32[]{:S(2)}, u32[]{:S(2)}) collective-permute-start(bf16[256,256]{1,0:T(8,128)(2,1)S(1)} %get-tuple-element.78), channel_id=1, source_target_pairs={{0,32},{32,0},{1,33},{33,1},{2,34},{34,2},{3,35},{35,3},{4,36},{36... | collective-permute-start | bytes 393224 | tf_op jit(solution)/shard_map/ppermute | solution.py:371
  83.2 8.0 %collective-permute-start.10 = (bf16[108,512]{1,0:T(8,128)(2,1)S(1)}, bf16[108,512]{1,0:T(8,128)(2,1)S(1)}, u32[]{:S(2)}, u32[]{:S(2)}) collective-permute-start(bf16[108,512]{1,0:T(8,128)(2,1)S(1)} %shard_map.116), channel_id=1, source_target_pairs={{0,2},{2,4},{4,6},{6,8},{8,10},{10,12},{12,14},{14,16},{16,18},{18... | collective-permute-start | bytes 331784 | tf_op jit(solution)/shard_map/ppermute | solution.py:371
  98.5 13.1 %all-to-all-start.2 = ((bf16[8,32,384]{2,1,0:T(8,128)(2,1)}), bf16[8,32,384]{2,1,0:T(8,128)(2,1)S(1)}, u32[]{:S(2)}, u32[]{:S(2)}) async-start(bf16[8,32,384]{2,1,0:T(8,128)(2,1)} %pad_maximum_fusion), calls=%async_computation.2 | async-start | bytes 393216 | tf_op jit(solution)/shard_map/all_to_all | solution.py:474
  101.9 9.8 %collective-permute-start.11 = (bf16[120,512]{1,0:T(8,128)(2,1)S(1)}, bf16[120,512]{1,0:T(8,128)(2,1)S(1)}, u32[]{:S(2)}, u32[]{:S(2)}) collective-permute-start(bf16[120,512]{1,0:T(8,128)(2,1)S(1)} %get-tuple-element.85), channel_id=1, source_target_pairs={{0,1},{1,0},{2,3},{3,2},{4,5},{5,4},{6,7},{7,6},{8,9},{9,8},{10,11... | collective-permute-start | bytes 368648 | tf_op jit(solution)/shard_map/ppermute | solution.py:371
  103.3 8.4 %collective-permute-start.12 = (bf16[96,512]{1,0:T(8,128)(2,1)S(1)}, bf16[96,512]{1,0:T(8,128)(2,1)S(1)}, u32[]{:S(2)}, u32[]{:S(2)}) collective-permute-start(bf16[96,512]{1,0:T(8,128)(2,1)S(1)} %get-tuple-element.86), channel_id=1, source_target_pairs={{0,64},{64,128},{128,192},{192,0},{1,65},{65,129},{129,193},{193,1... | collective-permute-start | bytes 294920 | tf_op jit(solution)/shard_map/ppermute | solution.py:371
  103.3 8.4 %collective-permute-start.13 = (bf16[96,512]{1,0:T(8,128)(2,1)S(1)}, bf16[96,512]{1,0:T(8,128)(2,1)S(1)}, u32[]{:S(2)}, u32[]{:S(2)}) collective-permute-start(bf16[96,512]{1,0:T(8,128)(2,1)S(1)} %get-tuple-element.87), channel_id=1, source_target_pairs={{0,65},{1,64},{64,129},{65,128},{128,193},{129,192},{192,1},{193,0... | collective-permute-start | bytes 294920 | tf_op jit(solution)/shard_map/ppermute | solution.py:386
  112.4 10.3 %all-to-all-start.3 = ((bf16[8,32,384]{2,1,0:T(8,128)(2,1)}), bf16[8,32,384]{2,1,0:T(8,128)(2,1)S(1)}, u32[]{:S(2)}, u32[]{:S(2)}) async-start(bf16[8,32,384]{2,1,0:T(8,128)(2,1)} %broadcast_in_dim.2), calls=%async_computation.3 | async-start | bytes 393216 | tf_op jit(solution)/shard_map/all_to_all | solution.py:476
  (10 other events, 43.4 us)

commit v3 on v2

--- a/solution.py
+++ b/solution.py
@@ -102,10 +102,13 @@
 
 
 def gather(table, column, sources):
-    names = table[: ROWS[column], column : column + 1]
+    return gather_named(table[: ROWS[column], column : column + 1], sources)
+
+
+def gather_named(names, sources):
     total = 0.0
     for source, value in sources.items():
-        place = lax.broadcasted_iota(jnp.int32, (ROWS[column], value.shape[0]), 1) + 1000 * source
+        place = lax.broadcasted_iota(jnp.int32, (names.shape[0], value.shape[0]), 1) + 1000 * source
         total += dot_nn((names == place).astype(WIDE).astype(LOW), value)
     return total
 
@@ -147,8 +150,18 @@
     both[...] = packed[216:].astype(LOW)
 
 
-def planes_in_kernel(table, tokens, cells, *outs):
-    store_planes(gather(table, IN_FIRST, own(tokens, cells)), *outs)
+def runs(target):
+    target = np.asarray(target)
+    begins = [0] + [at for at in range(1, len(target)) if target[at] != target[at - 1] + 1]
+    return [(at, int(target[at]) - at) for at in begins]
+
+
+def planes_in_kernel(tokens, cells, *outs):
+    row = lax.broadcasted_iota(jnp.int32, (ROWS[IN_FIRST], 1), 0)
+    ahead = jnp.zeros_like(row)
+    for begin, difference in runs(TABLE[: ROWS[IN_FIRST], IN_FIRST]):
+        ahead = jnp.where(row >= begin, difference, ahead)
+    store_planes(gather_named(row + ahead, own(tokens, cells)), *outs)
 
 
 def columns_in_kernel(table, tokens, cells, grp, lat, both, out):
@@ -185,8 +198,8 @@
 
 def forward_kernel(
     core, table, tokens, cells, grp, lat, both, lon, row_labels, column_labels, far_inward, far_outward,
-    block, last_row, windows, projected, far_attention, attended, shifted, kept, sent,
-    inward, outward, attention, columns, picked, weights_in, shares_out,
+    block, last_row, far_windows, far_projected, far_attention, attended, shifted, kept, sent,
+    inward, outward, attention, columns, picked, windows, projected, weights_in, shares_out, early_out,
 ):
     fetches = [
         pltpu.make_async_copy(far_inward, inward, weights_in.at[0]),
@@ -194,13 +207,18 @@
     ]
     for copy in fetches:
         copy.start()
-    stores = []
+    stores = [
+        pltpu.make_async_copy(windows, far_windows, early_out.at[0]),
+        pltpu.make_async_copy(projected, far_projected, early_out.at[1]),
+    ]
     arrived_parts = arrivals(grp, lat, both) | {6: lon[...]}
     values = gather(table, IN_WINDOWS, {0: tokens[...]} | arrived_parts)
     windows[...] = values.astype(LOW)
+    stores[0].start()
     normed = normalize(values)[0].astype(LOW)
     fetches[0].wait()
     projected[...] = dot_nn(normed, inward[...]).astype(LOW)
+    stores[1].start()
     masks = head_masks()
     for w in range(2):
         rows = slice(144 * w, 144 * w + 144)
@@ -234,10 +252,23 @@
         store.wait()
 
 
-def merge_kernel(table, block, prior, upstream, columns, other_columns, normed, bundle, back, back_row):
+def merge_kernel(table, block, prior, upstream, columns, other_columns, normed, bundle, far_back, back_row, back, back_out):
     merged = gather(table, TO_CELLS, {0: block[...], 1: prior[...]})
     pieces = [merged[72 * k : 72 * k + 72] for k in range(4)]
     exact, inverse_std = normalize(jnp.concatenate(pieces, axis=1))
+    grads = upstream[...]
+    grads = inverse_std * (
+        grads
+        - jnp.mean(grads, axis=-1, keepdims=True)
+        - exact * jnp.mean(grads * exact, axis=-1, keepdims=True)
+    )
+    stacked = jnp.concatenate([grads[:, 512 * k : 512 * k + 512] for k in range(4)], axis=0)
+    stacked = stacked.astype(LOW)
+    positions = gather(table, FROM_CELLS, {0: stacked})
+    back[...] = positions[:288].astype(LOW)
+    store = pltpu.make_async_copy(back, far_back, back_out)
+    store.start()
+    back_row[...] = positions[288:].astype(LOW)
     normed[...] = exact.astype(LOW)
     for k in range(8):
         bundle[k, 0] = columns[k % 2]
@@ -245,17 +276,7 @@
         for half in range(2):
             at = 512 * (k // 2) + 256 * half
             bundle[k, 2 + half] = exact[:, at : at + 256].astype(LOW)
-    grads = upstream[...]
-    grads = inverse_std * (
-        grads
-        - jnp.mean(grads, axis=-1, keepdims=True)
-        - exact * jnp.mean(grads * exact, axis=-1, keepdims=True)
-    )
-    stacked = jnp.concatenate([grads[:, 512 * k : 512 * k + 512] for k in range(4)], axis=0)
-    stacked = stacked.astype(LOW)
-    positions = gather(table, FROM_CELLS, {0: stacked})
-    back[...] = positions[:288].astype(LOW)
-    back_row[...] = positions[288:].astype(LOW)
+    store.wait()
 
 
 def merging_kernel(xh, bundle, other_normed, kept, sent, total):
@@ -272,7 +293,8 @@
 
 def backward_kernel(
     core, table, back, next_row, windows, projected, far_attention, attended, far_inward, outward,
-    token_grads, kept, sent, projected_back, inward_t, outward_t, attention, inward, shares_in, weight_in,
+    token_grads, far_kept, far_sent,
+    projected_back, inward_t, outward_t, attention, inward, kept, sent, shares_in, weight_in, terms_out,
 ):
     loads = [pltpu.make_async_copy(far_attention.at[w], attention.at[w], shares_in.at[w]) for w in range(2)]
     loads.append(pltpu.make_async_copy(far_inward, inward, weight_in))
@@ -321,6 +343,12 @@
                 terms[place // 8, k, 0, place % 8] = inward_t[head, lanes]
                 terms[place // 8, k, 1, place % 8, 0:16] = inward_t[tail, lanes]
                 terms[place // 8, k, 1, place % 8, 16:32] = outward_t[last, lanes]
+    stores = [
+        pltpu.make_async_copy(sent, far_sent, terms_out.at[0]),
+        pltpu.make_async_copy(kept, far_kept, terms_out.at[1]),
+    ]
+    for store in stores:
+        store.start()
     loads[2].wait()
     normed_back = dot_nt(projected_back[...], inward[...])
     branch = inverse_std * (
@@ -330,6 +358,8 @@
     )
     result = (upstream + branch.astype(LOW).astype(WIDE)).astype(LOW)
     token_grads[...] = gather(table, FROM_WINDOWS, {0: result}).astype(LOW)
+    for store in stores:
+        store.wait()
 
 
 def shares_kernel(shares, inward_grads, outward_grads, merging_grads):
@@ -391,7 +421,7 @@
 
 
 def shift_forward(table, tokens, cells):
-    parts = to_neighbours(call(planes_in_kernel, PLANES, table, tokens, cells), -1)
+    parts = to_neighbours(call(planes_in_kernel, PLANES, tokens, cells), -1)
     (columns,) = call(columns_in_kernel, [(108, 512)], table, tokens, cells, *parts)
     return (*parts, from_behind(columns, LON, -1))
 
@@ -424,10 +454,10 @@
         ],
         core, table, tokens, cells, *parts, labels.reshape(2, 1, 144), labels.reshape(2, 144, 1), inward_weight, outward_weight,
         scratch=[
-            (512, 1536), (512, 512), (2, HEADS, 144, 144), (1024, 72), (256, 72),
-            pltpu.SemaphoreType.DMA((2,)), pltpu.SemaphoreType.DMA((2, 4)),
+            (512, 1536), (512, 512), (2, HEADS, 144, 144), (1024, 72), (256, 72), (288, 512), (288, 1536),
+            pltpu.SemaphoreType.DMA((2,)), pltpu.SemaphoreType.DMA((2, 4)), pltpu.SemaphoreType.DMA((2,)),
         ],
-        scalars=1, room=54, far=(10, 11), far_outs=(4,),
+        scalars=1, room=54, far=(10, 11), far_outs=(2, 3, 4),
     )
     prior = from_behind(last_row, ("lat",), 1)
     other_columns = from_behind(sent_columns, ("core",), 1)
@@ -436,6 +466,7 @@
         merge_kernel,
         [(72, 2048), (8, 4, 72, 256), (288, 512), (48, 512)],
         table, block, prior, merged_upstream, columns, other_columns,
+        scratch=[(288, 512), pltpu.SemaphoreType.DMA], far_outs=(2,),
     )
     next_row = from_behind(back_row, ("lat",), -1)
     next_row, bundle = tied(next_row, bundle)
@@ -446,9 +477,10 @@
         core, table, back, next_row, windows, projected, attention, attended, inward_weight, outward_weight,
         scratch=[
             (288, 1536), (1536, 512), (512, 512), (2, HEADS, 144, 144), (512, 1536),
-            pltpu.SemaphoreType.DMA((2,)), pltpu.SemaphoreType.DMA,
+            (2, 4, 2, 8, 32, 128), (2, 4, 2, 8, 32, 128),
+            pltpu.SemaphoreType.DMA((2,)), pltpu.SemaphoreType.DMA, pltpu.SemaphoreType.DMA((2,)),
         ],
-        scalars=1, room=54, far=(6, 8),
+        scalars=1, room=54, far=(6, 8), far_outs=(1, 2),
     )
     merged_normed, token_grads = tied(merged_normed, token_grads)
     coarse_field = dot_nn(merged_normed, merging_weight).astype(LOW)
@@ -472,7 +504,8 @@
     merging_planes = (merging_kept.astype(WIDE) + merging_came.astype(WIDE)).astype(LOW).reshape(8, 32, 256)
     planes = jnp.concatenate([block_planes, merging_planes], axis=2)
     share = wide_sum(lax.all_to_all(planes, ("z",), 0, 0))
-    share, *parts_out = tied(share, *parts_out)
+    share, first = tied(share, parts_out[0])
+    parts_out = (first, *parts_out[1:])
     shares = lax.all_to_all(jnp.broadcast_to(share[None], (8, 32, 384)), ("lat", "grp"), 0, 0)
     token_grads, coarse_field = call(
         all_out_kernel, [(288, 512), (72, 1024)], table, token_grads, coarse_field, *parts_out, lon_out

time: 125 us -> 129 us (1.032)
  waiting for transfers between devices: 37.6 us -> 41.1 us
  starting transfers between devices: 37.6 us -> 39.1 us
    ppermute x12, waiting for transfers between devices: 19.2 us -> 22.8 us  [from_behind(): return lax.ppermute(value, axis, pairs)]
    all_to_all x1, waiting for transfers between devices: 3.15 us -> 0.01 us  [body(): lax.all_to_all(jnp.broadcast_to(share[None], (8, 32, 384)), ('lat', 'grp'...]
    ppermute x2, waiting for transfers between devices: 1.12 us -> 2.76 us  [to_neighbours(): lax.ppermute(both, ('lat', 'grp'), pairs)]
    ppermute x12, starting transfers between devices: 15.5 us -> 17 us  [from_behind(): return lax.ppermute(value, axis, pairs)]
    all_to_all x1, waiting for transfers between devices: 6.9 us -> 8.36 us  [body(): share = wide_sum(lax.all_to_all(planes, ('z',), 0, 0))]
  transfers between devices with their start and end apart: 18 -> 18, of which waited for: 12 -> 13; matrix products, arithmetic and copies ran while one was open for 7% -> 7% of each run, Pallas kernels for 13% -> 13%
where the time goes in v3:
time: 129 us; the launch traced here: 128 us
  waiting for transfers between devices  41.1 us (32%)
  starting transfers between devices  39.1 us (30%)
  Pallas kernels  31.1 us (24%)
  local copies, waits for them, and re-layouts  8.14 us (6%)
  matrix products  4.54 us (4%)
  other arithmetic  3.42 us (3%)
    pallas_call x10, Pallas kernels, call(): pl.pallas_call(kernel, in_specs=specs, out_specs=out_specs, out_shape=[ja...  31.1 us
    ppermute x12, waiting for transfers between devices, from_behind(): return lax.ppermute(value, axis, pairs)  22.8 us
    ppermute x12, starting transfers between devices, from_behind(): return lax.ppermute(value, axis, pairs)  17 us
    all_to_all x1, waiting for transfers between devices, body(): share = wide_sum(lax.all_to_all(planes, ('z',), 0, 0))  8.36 us
    all_to_all x1, starting transfers between devices, body(): bundle = lax.all_to_all(bundle, ('lat', 'grp'), 0, 0)  5.78 us
    all_to_all x1, starting transfers between devices, over_planes(): return wide_sum(lax.all_to_all(terms, ('xh', 'lat', 'grp'), 0, 0))  5.23 us
    unnamed x34, local copies, waits for them, and re-layouts  5.12 us
    all_to_all x1, starting transfers between devices, body(): lax.all_to_all(jnp.broadcast_to(share[None], (8, 32, 384)), ('lat', 'grp'...  4.54 us
  transfers between devices with their start and end apart: 18, of which 13 were waited for; matrix products, arithmetic and copies ran while one was open for 7% of the time, Pallas kernels for 13%

profile of v3, /device:TPU:2, one launch (start us, length us, event | category | flops | bytes accessed | tf_op | source)
XLA Modules:
  0.0 128.3 jit_solution(3150803830961345805)
XLA Ops:
  3.1 2.4 %collective-permute-start = (bf16[120,512]{1,0:T(8,128)(2,1)S(1)}, bf16[120,512]{1,0:T(8,128)(2,1)S(1)}, u32[]{:S(2)}, u32[]{:S(2)}) collective-permute-start(bf16[120,512]{1,0:T(8,128)(2,1)S(1)} %get-tuple-element.49), channel_id=1, source_target_pairs={{0,1},{1,0},{2,3},{3,2},{4,5},{5,4},{6,7},{7,6},{8,9},{9,8},{10,11... | collective-permute-start | bytes 368648 | tf_op jit(solution)/shard_map/ppermute | solution.py:401
  6.8 1.7 %collective-permute-start.2 = (bf16[96,512]{1,0:T(8,128)(2,1)S(1)}, bf16[96,512]{1,0:T(8,128)(2,1)S(1)}, u32[]{:S(2)}, u32[]{:S(2)}) collective-permute-start(bf16[96,512]{1,0:T(8,128)(2,1)S(1)} %get-tuple-element.51), channel_id=1, source_target_pairs={{0,193},{1,192},{64,1},{65,0},{128,65},{129,64},{192,129},{193,128... | collective-permute-start | bytes 294920 | tf_op jit(solution)/shard_map/ppermute | solution.py:416
  8.4 2.7 %collective-permute-done.1.lat = bf16[96,512]{1,0:T(8,128)(2,1)S(1)} collective-permute-done((bf16[96,512]{1,0:T(8,128)(2,1)S(1)}, bf16[96,512]{1,0:T(8,128)(2,1)S(1)}, u32[]{:S(2)}, u32[]{:S(2)}) %collective-permute-start.1) | collective-permute-done | bytes 98336 | tf_op jit(solution)/shard_map/ppermute | solution.py:401
  13.7 5.5 %collective-permute-start.3 = (bf16[108,512]{1,0:T(8,128)(2,1)S(1)}, bf16[108,512]{1,0:T(8,128)(2,1)S(1)}, u32[]{:S(2)}, u32[]{:S(2)}) collective-permute-start(bf16[108,512]{1,0:T(8,128)(2,1)S(1)} %shard_map.111), channel_id=1, source_target_pairs={{0,62},{2,0},{4,2},{6,4},{8,6},{10,8},{12,10},{14,12},{16,14},{18,... | collective-permute-start | bytes 331784 | tf_op jit(solution)/shard_map/ppermute | solution.py:401
  22.2 10.7 %shard_map.112 = (bf16[288,512]{1,0:T(8,128)(2,1)}, bf16[48,512]{1,0:T(8,128)(2,1)}, bf16[288,512]{1,0:T(8,128)(2,1)}, bf16[288,1536]{1,0:T(8,128)(2,1)}, bf16[2...) custom-call(s32[1]{0:T(128)} %bitcast.core, ...), custom_call_target="tpu_custom_call" | custom-call | tf_op jit(solution)/shard_map/pallas_call | solution.py:385
  34.0 3.7 %fusion.upstream = f32[72,2048]{1,0:T(8,128)S(1)} fusion(bf16[72,1024]{1,0:T(8,128)(2,1)} %get-tuple-element.54, bf16[2048,1024]{1,0:T(8,128)(2,1)} %param.11), kind=kOutput, calls=%fused_computation.5 | convolution fusion | flops 301989888 | bytes 4931584 | tf_op jit(solution)/shard_map/dot_general | solution.py:121
  38.6 2.3 %shard_map.113 = (bf16[72,2048]{1,0:T(8,128)(2,1)S(1)}, bf16[8,4,72,256]{3,2,1,0:T(8,128)(2,1)}, bf16[288,512]{1,0:T(8,128)(2,1)S(1)}, bf16[48,512]{1,0:T(8,128)(2,1)S(1)}) custom-call(s32[432,11]{1,0:T(8,128)S(1)} %copy-done.1, bf16[288,512]{1,0:T(8,128)(2,1)S(1)} %copy-done.10, bf16[48,512]{1,0:T(8,128)(2,1)S(1)} %collective-permute-done.4.prior, ...), custom_call_target="tpu_custom_call" | custom-call | tf_op jit(solution)/shard_map/pallas_call | solution.py:385
  43.1 2.7 %collective-permute-done.6.next_row = bf16[48,512]{1,0:T(8,128)(2,1)S(1)} collective-permute-done((bf16[48,512]{1,0:T(8,128)(2,1)S(1)}, bf16[48,512]{1,0:T(8,128)(2,1)S(1)}, u32[]{:S(2)}, u32[]{:S(2)}) %collective-permute-start.6) | collective-permute-done | bytes 49184 | tf_op jit(solution)/shard_map/ppermute | solution.py:401
  45.8 5.8 %all-to-all-start = ((bf16[8,4,72,256]{3,2,1,0:T(8,128)(2,1)}), bf16[8,4,72,256]{3,2,1,0:T(8,128)(2,1)S(1)}, u32[]{:S(2)}, u32[]{:S(2)}) async-start(bf16[8,4,72,256]{3,2,1,0:T(8,128)(2,1)} %get-tuple-element.70), calls=%async_computation | async-start | bytes 2359296 | tf_op jit(solution)/shard_map/all_to_all | solution.py:473
  51.5 12.3 %shard_map.114 = (bf16[288,512]{1,0:T(8,128)(2,1)}, bf16[2,4,2,8,32,128]{5,4,3,2,1,0:T(8,128)(2,1)}, bf16[2,4,2,8,32,128]{5,4,3,2,1,0:T(8,128)(2,1)}) custom-call(s32[1]{0:T(128)} %bitcast.core, s32[432,11]{1,0:T(8,128)} %constant.14.clone.table, bf16[288,512]{1,0:T(8,128)(2,1)} %copy-done.9, bf16[48,512]{1,0:T(8,128)(2,1)} %copy-done.15, ...), custom_call_target="tpu_custom_call" | custom-call | tf_op jit(solution)/shard_map/pallas_call | solution.py:385
  64.8 2.6 %all-to-all-done.bundle = bf16[8,4,72,256]{3,2,1,0:T(8,128)(2,1)S(1)} async-done(((bf16[8,4,72,256]{3,2,1,0:T(8,128)(2,1)}), bf16[8,4,72,256]{3,2,1,0:T(8,128)(2,1)S(1)}, u32[]{:S(2)}, u32[]{:S(2)}) %all-to-all-start) | async-done | bytes 1179680 | tf_op jit(solution)/shard_map/all_to_all | solution.py:473
  67.4 2.9 %collective-permute-done.7 = bf16[2,4,2,8,32,128]{5,4,3,2,1,0:T(8,128)(2,1)S(1)} collective-permute-done((bf16[2,4,2,8,32,128]{5,4,3,2,1,0:T(8,128)(2,1)}, bf16[2,4,2,8,32,128]{5,4,3,2,1,0:T(8,128)(2,1)S(1)}, u32[]{:S(2)}, u32[]{:S(2)}) %collective-permute-start.7) | collective-permute-done | bytes 1048608 | tf_op jit(solution)/shard_map/ppermute | solution.py:401
  71.5 5.2 %all-to-all-start.1 = ((bf16[16,8,32,128]{3,2,1,0:T(8,128)(2,1)}), bf16[16,8,32,128]{3,2,1,0:T(8,128)(2,1)}, u32[]{:S(2)}, u32[]{:S(2)}) async-start(bf16[16,8,32,128]{3,2,1,0:T(8,128)(2,1)} %bitcast.3), calls=%async_computation.1 | async-start | bytes 2097152 | tf_op jit(solution)/shard_map/all_to_all | solution.py:435
  76.9 2.0 %collective-permute-done.8.other_normed = bf16[8,2,72,256]{3,2,1,0:T(8,128)(2,1)S(1)} collective-permute-done((bf16[8,2,72,256]{3,2,1,0:T(8,128)(2,1)S(1)}, bf16[8,2,72,256]{3,2,1,0:T(8,128)(2,1)S(1)}, u32[]{:S(2)}, u32[]{:S(2)}) %collective-permute-start.8) | collective-permute-done | bytes 589856 | tf_op jit(solution)/shard_map/ppermute | solution.py:401
  80.2 2.4 %collective-permute-start.9 = (bf16[256,256]{1,0:T(8,128)(2,1)S(1)}, bf16[256,256]{1,0:T(8,128)(2,1)S(1)}, u32[]{:S(2)}, u32[]{:S(2)}) collective-permute-start(bf16[256,256]{1,0:T(8,128)(2,1)S(1)} %get-tuple-element.76), channel_id=1, source_target_pairs={{0,32},{32,0},{1,33},{33,1},{2,34},{34,2},{3,35},{35,3},{4,36},{36... | collective-permute-start | bytes 393224 | tf_op jit(solution)/shard_map/ppermute | solution.py:401
  83.0 7.9 %collective-permute-done.10.lon = bf16[108,512]{1,0:T(8,128)(2,1)S(1)} collective-permute-done((bf16[108,512]{1,0:T(8,128)(2,1)S(1)}, bf16[108,512]{1,0:T(8,128)(2,1)S(1)}, u32[]{:S(2)}, u32[]{:S(2)}) %collective-permute-start.10) | collective-permute-done | bytes 110624 | tf_op jit(solution)/shard_map/ppermute | solution.py:401
  91.6 4.5 %all-to-all-done.1 = bf16[16,8,32,128]{3,2,1,0:T(8,128)(2,1)} async-done(((bf16[16,8,32,128]{3,2,1,0:T(8,128)(2,1)}), bf16[16,8,32,128]{3,2,1,0:T(8,128)(2,1)}, u32[]{:S(2)}, u32[]{:S(2)}) %all-to-all-start.1) | async-done | bytes 1048608 | tf_op jit(solution)/shard_map/all_to_all | solution.py:435
  98.3 3.4 %all-to-all-start.2 = ((bf16[8,32,384]{2,1,0:T(8,128)(2,1)}), bf16[8,32,384]{2,1,0:T(8,128)(2,1)S(1)}, u32[]{:S(2)}, u32[]{:S(2)}) async-start(bf16[8,32,384]{2,1,0:T(8,128)(2,1)} %pad_maximum_fusion), calls=%async_computation.2 | async-start | bytes 393216 | tf_op jit(solution)/shard_map/all_to_all | solution.py:506
  103.0 8.4 %all-to-all-done.2 = bf16[8,32,384]{2,1,0:T(8,128)(2,1)S(1)} async-done(((bf16[8,32,384]{2,1,0:T(8,128)(2,1)}), bf16[8,32,384]{2,1,0:T(8,128)(2,1)S(1)}, u32[]{:S(2)}, u32[]{:S(2)}) %all-to-all-start.2) | async-done | bytes 196640 | tf_op jit(solution)/shard_map/all_to_all | solution.py:506
  112.1 4.5 %all-to-all-start.3 = ((bf16[8,32,384]{2,1,0:T(8,128)(2,1)}), bf16[8,32,384]{2,1,0:T(8,128)(2,1)S(1)}, u32[]{:S(2)}, u32[]{:S(2)}) async-start(bf16[8,32,384]{2,1,0:T(8,128)(2,1)} %broadcast_in_dim.2), calls=%async_computation.3 | async-start | bytes 393216 | tf_op jit(solution)/shard_map/all_to_all | solution.py:509
  116.6 1.5 %collective-permute-start.12 = (bf16[96,512]{1,0:T(8,128)(2,1)S(1)}, bf16[96,512]{1,0:T(8,128)(2,1)S(1)}, u32[]{:S(2)}, u32[]{:S(2)}) collective-permute-start(bf16[96,512]{1,0:T(8,128)(2,1)S(1)} %get-tuple-element.85), channel_id=1, source_target_pairs={{0,64},{64,128},{128,192},{192,0},{1,65},{65,129},{129,193},{193,1... | collective-permute-start | bytes 294920 | tf_op jit(solution)/shard_map/ppermute | solution.py:401
  119.6 3.6 %collective-permute-done.12.lat = bf16[96,512]{1,0:T(8,128)(2,1)S(1)} collective-permute-done((bf16[96,512]{1,0:T(8,128)(2,1)S(1)}, bf16[96,512]{1,0:T(8,128)(2,1)S(1)}, u32[]{:S(2)}, u32[]{:S(2)}) %collective-permute-start.12) | collective-permute-done | bytes 98336 | tf_op jit(solution)/shard_map/ppermute | solution.py:401
  123.2 1.6 %collective-permute-done.13.both = bf16[96,512]{1,0:T(8,128)(2,1)S(1)} collective-permute-done((bf16[96,512]{1,0:T(8,128)(2,1)S(1)}, bf16[96,512]{1,0:T(8,128)(2,1)S(1)}, u32[]{:S(2)}, u32[]{:S(2)}) %collective-permute-start.13) | collective-permute-done | bytes 98336 | tf_op jit(solution)/shard_map/ppermute | solution.py:416
  124.9 1.8 %shard_map.118 = (bf16[288,512]{1,0:T(8,128)(2,1)}, bf16[72,1024]{1,0:T(8,128)(2,1)S(1)}) custom-call(s32[432,11]{1,0:T(8,128)S(1)} %copy-done.2, bf16[288,512]{1,0:T(8,128)(2,1)S(1)} %copy-done.4, bf16[72,1024]{1,0:T(8,128)(2,1)S(1)} %convolution_convert_fusion.cells, bf16[120,512]{1,0:T(8,128)(2,1)S(1)} %collective-permute-done.11.grp, ...), custom_call_target="tpu_custom_call" | custom-call | tf_op jit(solution)/shard_map/pallas_call | solution.py:385
  (71 shorter events, 25.2 us)
Async XLA Ops:
  1.6 20.0 %copy-start.5 = (bf16[72,1024]{1,0:T(8,128)(2,1)}, bf16[72,1024]{1,0:T(8,128)(2,1)S(1)}, u32[]{:S(2)}) copy-start(bf16[72,1024]{1,0:T(8,128)(2,1)S(1)} %reshape.40.cells) | copy-start | bytes 442372
  3.1 9.2 %collective-permute-start = (bf16[120,512]{1,0:T(8,128)(2,1)S(1)}, bf16[120,512]{1,0:T(8,128)(2,1)S(1)}, u32[]{:S(2)}, u32[]{:S(2)}) collective-permute-start(bf16[120,512]{1,0:T(8,128)(2,1)S(1)} %get-tuple-element.49), channel_id=1, source_target_pairs={{0,1},{1,0},{2,3},{3,2},{4,5},{5,4},{6,7},{7,6},{8,9},{9,8},{10,11... | collective-permute-start | bytes 368648 | tf_op jit(solution)/shard_map/ppermute | solution.py:401
  5.5 5.7 %collective-permute-start.1 = (bf16[96,512]{1,0:T(8,128)(2,1)S(1)}, bf16[96,512]{1,0:T(8,128)(2,1)S(1)}, u32[]{:S(2)}, u32[]{:S(2)}) collective-permute-start(bf16[96,512]{1,0:T(8,128)(2,1)S(1)} %get-tuple-element.50), channel_id=1, source_target_pairs={{0,192},{64,0},{128,64},{192,128},{1,193},{65,1},{129,65},{193,129... | collective-permute-start | bytes 294920 | tf_op jit(solution)/shard_map/ppermute | solution.py:401
  6.8 5.5 %collective-permute-start.2 = (bf16[96,512]{1,0:T(8,128)(2,1)S(1)}, bf16[96,512]{1,0:T(8,128)(2,1)S(1)}, u32[]{:S(2)}, u32[]{:S(2)}) collective-permute-start(bf16[96,512]{1,0:T(8,128)(2,1)S(1)} %get-tuple-element.51), channel_id=1, source_target_pairs={{0,193},{1,192},{64,1},{65,0},{128,65},{129,64},{192,129},{193,128... | collective-permute-start | bytes 294920 | tf_op jit(solution)/shard_map/ppermute | solution.py:416
  11.2 10.4 %copy-start.7 = (bf16[96,512]{1,0:T(8,128)(2,1)}, bf16[96,512]{1,0:T(8,128)(2,1)S(1)}, u32[]{:S(2)}) copy-start(bf16[96,512]{1,0:T(8,128)(2,1)S(1)} %collective-permute-done.1.lat) | copy-start | bytes 294916
  13.7 7.9 %collective-permute-start.3 = (bf16[108,512]{1,0:T(8,128)(2,1)S(1)}, bf16[108,512]{1,0:T(8,128)(2,1)S(1)}, u32[]{:S(2)}, u32[]{:S(2)}) collective-permute-start(bf16[108,512]{1,0:T(8,128)(2,1)S(1)} %shard_map.111), channel_id=1, source_target_pairs={{0,62},{2,0},{4,2},{6,4},{8,6},{10,8},{12,10},{14,12},{16,14},{18,... | collective-permute-start | bytes 331784 | tf_op jit(solution)/shard_map/ppermute | solution.py:401
  20.7 17.9 %copy-start.1 = (s32[432,11]{1,0:T(8,128)S(1)}, s32[432,11]{1,0:T(8,128)}, u32[]{:S(2)}) copy-start(s32[432,11]{1,0:T(8,128)} %constant.14.clone.table) | copy-start | bytes 57028
  33.0 5.6 %collective-permute-start.4 = (bf16[48,512]{1,0:T(8,128)(2,1)}, bf16[48,512]{1,0:T(8,128)(2,1)S(1)}, u32[]{:S(2)}, u32[]{:S(2)}) collective-permute-start(bf16[48,512]{1,0:T(8,128)(2,1)} %get-tuple-element.53), channel_id=1, source_target_pairs={{0,64},{64,128},{128,192},{192,0},{1,65},{65,129},{129,193},{193,1... | collective-permute-start | bytes 147464 | tf_op jit(solution)/shard_map/ppermute | solution.py:401
  34.0 4.6 %collective-permute-start.5 = (bf16[2,72,256]{2,1,0:T(8,128)(2,1)}, bf16[2,72,256]{2,1,0:T(8,128)(2,1)S(1)}, u32[]{:S(2)}, u32[]{:S(2)}) collective-permute-start(bf16[2,72,256]{2,1,0:T(8,128)(2,1)} %get-tuple-element.56), channel_id=1, source_target_pairs={{0,2},{2,0},{1,3},{3,1},{4,6},{6,4},{5,7},{7,5},{8,10},{10,8},{9,1... | collective-permute-start | bytes 221192 | tf_op jit(solution)/shard_map/ppermute | solution.py:401
  41.7 4.1 %collective-permute-start.6 = (bf16[48,512]{1,0:T(8,128)(2,1)S(1)}, bf16[48,512]{1,0:T(8,128)(2,1)S(1)}, u32[]{:S(2)}, u32[]{:S(2)}) collective-permute-start(bf16[48,512]{1,0:T(8,128)(2,1)S(1)} %get-tuple-element.59), channel_id=1, source_target_pairs={{0,192},{64,0},{128,64},{192,128},{1,193},{65,1},{129,65},{193,129... | collective-permute-start | bytes 147464 | tf_op jit(solution)/shard_map/ppermute | solution.py:401
  45.8 21.6 %all-to-all-start = ((bf16[8,4,72,256]{3,2,1,0:T(8,128)(2,1)}), bf16[8,4,72,256]{3,2,1,0:T(8,128)(2,1)S(1)}, u32[]{:S(2)}, u32[]{:S(2)}) async-start(bf16[8,4,72,256]{3,2,1,0:T(8,128)(2,1)} %get-tuple-element.70), calls=%async_computation | async-start | bytes 2359296 | tf_op jit(solution)/shard_map/all_to_all | solution.py:473
  51.5 12.3 %copy-start.12 = (bf16[2048,1024]{1,0:T(8,128)(2,1)S(1)}, bf16[2048,1024]{1,0:T(8,128)(2,1)}, u32[]{:S(2)}) copy-start(bf16[2048,1024]{1,0:T(8,128)(2,1)} %param.11) | copy-start | bytes 12582916
  64.7 17.9 %copy-start.2 = (s32[432,11]{1,0:T(8,128)S(1)}, s32[432,11]{1,0:T(8,128)}, u32[]{:S(2)}) copy-start(s32[432,11]{1,0:T(8,128)} %constant.14.clone.table) | copy-start | bytes 57028
  64.7 17.9 %copy-start.4 = (bf16[288,512]{1,0:T(8,128)(2,1)S(1)}, bf16[288,512]{1,0:T(8,128)(2,1)}, u32[]{:S(2)}) copy-start(bf16[288,512]{1,0:T(8,128)(2,1)} %get-tuple-element.67.tokens) | copy-start | bytes 884740
  67.4 2.9 %collective-permute-start.7 = (bf16[2,4,2,8,32,128]{5,4,3,2,1,0:T(8,128)(2,1)}, bf16[2,4,2,8,32,128]{5,4,3,2,1,0:T(8,128)(2,1)S(1)}, u32[]{:S(2)}, u32[]{:S(2)}) collective-permute-start(bf16[2,4,2,8,32,128]{5,4,3,2,1,0:T(8,128)(2,1)} %get-tuple-element.74), channel_id=1, source_target_pairs={{0,2},{2,0},{1,3},{3,1},{4,6},{6,4},{5,7},{7,5},{8,10},{10,8},{9,1... | collective-permute-start | bytes 3145736 | tf_op jit(solution)/shard_map/ppermute | solution.py:401
  71.5 24.6 %all-to-all-start.1 = ((bf16[16,8,32,128]{3,2,1,0:T(8,128)(2,1)}), bf16[16,8,32,128]{3,2,1,0:T(8,128)(2,1)}, u32[]{:S(2)}, u32[]{:S(2)}) async-start(bf16[16,8,32,128]{3,2,1,0:T(8,128)(2,1)} %bitcast.3), calls=%async_computation.1 | async-start | bytes 2097152 | tf_op jit(solution)/shard_map/all_to_all | solution.py:435
  76.8 2.1 %collective-permute-start.8 = (bf16[8,2,72,256]{3,2,1,0:T(8,128)(2,1)S(1)}, bf16[8,2,72,256]{3,2,1,0:T(8,128)(2,1)S(1)}, u32[]{:S(2)}, u32[]{:S(2)}) collective-permute-start(bf16[8,2,72,256]{3,2,1,0:T(8,128)(2,1)S(1)} %slice.3), channel_id=1, source_target_pairs={{0,2},{2,0},{1,3},{3,1},{4,6},{6,4},{5,7},{7,5},{8,10},{10,8},{9,1... | collective-permute-start | bytes 1769480 | tf_op jit(solution)/shard_map/ppermute | solution.py:401
  80.2 17.3 %collective-permute-start.9 = (bf16[256,256]{1,0:T(8,128)(2,1)S(1)}, bf16[256,256]{1,0:T(8,128)(2,1)S(1)}, u32[]{:S(2)}, u32[]{:S(2)}) collective-permute-start(bf16[256,256]{1,0:T(8,128)(2,1)S(1)} %get-tuple-element.76), channel_id=1, source_target_pairs={{0,32},{32,0},{1,33},{33,1},{2,34},{34,2},{3,35},{35,3},{4,36},{36... | collective-permute-start | bytes 393224 | tf_op jit(solution)/shard_map/ppermute | solution.py:401
  83.0 8.0 %collective-permute-start.10 = (bf16[108,512]{1,0:T(8,128)(2,1)S(1)}, bf16[108,512]{1,0:T(8,128)(2,1)S(1)}, u32[]{:S(2)}, u32[]{:S(2)}) collective-permute-start(bf16[108,512]{1,0:T(8,128)(2,1)S(1)} %shard_map.116), channel_id=1, source_target_pairs={{0,2},{2,4},{4,6},{6,8},{8,10},{10,12},{12,14},{14,16},{16,18},{18... | collective-permute-start | bytes 331784 | tf_op jit(solution)/shard_map/ppermute | solution.py:401
  98.3 13.1 %all-to-all-start.2 = ((bf16[8,32,384]{2,1,0:T(8,128)(2,1)}), bf16[8,32,384]{2,1,0:T(8,128)(2,1)S(1)}, u32[]{:S(2)}, u32[]{:S(2)}) async-start(bf16[8,32,384]{2,1,0:T(8,128)(2,1)} %pad_maximum_fusion), calls=%async_computation.2 | async-start | bytes 393216 | tf_op jit(solution)/shard_map/all_to_all | solution.py:506
  101.7 9.7 %collective-permute-start.11 = (bf16[120,512]{1,0:T(8,128)(2,1)S(1)}, bf16[120,512]{1,0:T(8,128)(2,1)S(1)}, u32[]{:S(2)}, u32[]{:S(2)}) collective-permute-start(bf16[120,512]{1,0:T(8,128)(2,1)S(1)} %get-tuple-element.83), channel_id=1, source_target_pairs={{0,1},{1,0},{2,3},{3,2},{4,5},{5,4},{6,7},{7,6},{8,9},{9,8},{10,11... | collective-permute-start | bytes 368648 | tf_op jit(solution)/shard_map/ppermute | solution.py:401
  112.1 15.4 %all-to-all-start.3 = ((bf16[8,32,384]{2,1,0:T(8,128)(2,1)}), bf16[8,32,384]{2,1,0:T(8,128)(2,1)S(1)}, u32[]{:S(2)}, u32[]{:S(2)}) async-start(bf16[8,32,384]{2,1,0:T(8,128)(2,1)} %broadcast_in_dim.2), calls=%async_computation.3 | async-start | bytes 393216 | tf_op jit(solution)/shard_map/all_to_all | solution.py:509
  116.6 6.6 %collective-permute-start.12 = (bf16[96,512]{1,0:T(8,128)(2,1)S(1)}, bf16[96,512]{1,0:T(8,128)(2,1)S(1)}, u32[]{:S(2)}, u32[]{:S(2)}) collective-permute-start(bf16[96,512]{1,0:T(8,128)(2,1)S(1)} %get-tuple-element.85), channel_id=1, source_target_pairs={{0,64},{64,128},{128,192},{192,0},{1,65},{65,129},{129,193},{193,1... | collective-permute-start | bytes 294920 | tf_op jit(solution)/shard_map/ppermute | solution.py:401
  118.1 6.7 %collective-permute-start.13 = (bf16[96,512]{1,0:T(8,128)(2,1)S(1)}, bf16[96,512]{1,0:T(8,128)(2,1)S(1)}, u32[]{:S(2)}, u32[]{:S(2)}) collective-permute-start(bf16[96,512]{1,0:T(8,128)(2,1)S(1)} %get-tuple-element.86), channel_id=1, source_target_pairs={{0,65},{1,64},{64,129},{65,128},{128,193},{129,192},{192,1},{193,0... | collective-permute-start | bytes 294920 | tf_op jit(solution)/shard_map/ppermute | solution.py:416
  (10 other events, 44.4 us)

commit v4 on v3

--- a/solution.py
+++ b/solution.py
@@ -54,21 +54,24 @@
 
 
 def shift_out():
-    first = join(FINE_AT[:, :, 18:], CELL_AT[:, :, 9:], CELL_AT[:, :, 9:] + 1000)
+    first = join(
+        FINE_AT[1, :3], halves(CELL_AT[1, :2]), FINE_AT[0, 3:], halves(CELL_AT[0, 2:]), FINE_AT[1, 3:], halves(CELL_AT[1, 2:])
+    )
+    grp, lat, both = arrived(3, 2), arrived(4, 1), arrived(5, 1)
+    fine = np.stack([np.concatenate([both[0], grp[0]]), np.concatenate([lat[0], FINE_AT[0, :3]])])
+    left = np.stack([np.concatenate([both[1], grp[1]]), np.concatenate([lat[1], CELL_AT[0, :2]])])
+    right = np.stack(
+        [
+            np.concatenate([both[1] + both[2], grp[1] + grp[2]]),
+            np.concatenate([lat[1] + lat[2], CELL_AT[0, :2] + 1000]),
+        ]
+    )
+    second = join(fine[:, :, 18:], left[:, :, 9:], right[:, :, 9:])
     lon_fine = 6000 + np.arange(72).reshape(2, 6, 6)
     lon_cells = 6072 + np.arange(18).reshape(2, 3, 3)
-    fine = np.concatenate([lon_fine, FINE_AT[:, :, :18]], axis=2)
-    left = np.concatenate([lon_cells, CELL_AT[:, :, :9]], axis=2)
-    right = np.concatenate([lon_cells + 18, CELL_AT[:, :, :9] + 1000], axis=2)
-    second = join(
-        fine[1, :3], left[1, :2], right[1, :2], fine[0, 3:], left[0, 2], right[0, 2], fine[1, 3:], left[1, 2], right[1, 2]
-    )
-    grp, lat, both = arrived(3, 2), arrived(4, 1), arrived(5, 1)
-    fine = np.stack([np.concatenate([both[0], grp[0]]), np.concatenate([lat[0], fine[0, :3]])])
-    left = np.stack([np.concatenate([both[1], grp[1]]), np.concatenate([lat[1], left[0, :2]])])
-    right = np.stack(
-        [np.concatenate([both[1] + both[2], grp[1] + grp[2]]), np.concatenate([lat[1] + lat[2], right[0, :2]])]
-    )
+    fine = np.concatenate([lon_fine, fine[:, :, :18]], axis=2)
+    left = np.concatenate([lon_cells, left[:, :, :9]], axis=2)
+    right = np.concatenate([lon_cells + 18, right[:, :, :9]], axis=2)
     return first, second, join(fine, left, right)
 
 
@@ -156,24 +159,29 @@
     return [(at, int(target[at]) - at) for at in begins]
 
 
+def column_names(column):
+    row = lax.broadcasted_iota(jnp.int32, (ROWS[column], 1), 0)
+    ahead = jnp.zeros_like(row)
+    for begin, difference in runs(TABLE[: ROWS[column], column]):
+        ahead = jnp.where(row >= begin, difference, ahead)
+    return row + ahead
+
+
 def planes_in_kernel(tokens, cells, *outs):
-    row = lax.broadcasted_iota(jnp.int32, (ROWS[IN_FIRST], 1), 0)
-    ahead = jnp.zeros_like(row)
-    for begin, difference in runs(TABLE[: ROWS[IN_FIRST], IN_FIRST]):
-        ahead = jnp.where(row >= begin, difference, ahead)
-    store_planes(gather_named(row + ahead, own(tokens, cells)), *outs)
-
-
-def columns_in_kernel(table, tokens, cells, grp, lat, both, out):
-    out[...] = gather(table, IN_SECOND, own(tokens, cells) | arrivals(grp, lat, both)).astype(LOW)
-
-
-def columns_out_kernel(table, tokens, cells, out):
-    out[...] = gather(table, OUT_FIRST, own(tokens, cells)).astype(LOW)
-
-
-def planes_out_kernel(table, tokens, cells, lon, *outs):
-    store_planes(gather(table, OUT_SECOND, own(tokens, cells) | {6: lon[...]}), *outs)
+    store_planes(gather_named(column_names(IN_FIRST), own(tokens, cells)), *outs)
+
+
+def columns_in_kernel(tokens, cells, grp, lat, both, out):
+    sources = own(tokens, cells) | arrivals(grp, lat, both)
+    out[...] = gather_named(column_names(IN_SECOND), sources).astype(LOW)
+
+
+def planes_out_kernel(table, tokens, cells, *outs):
+    store_planes(gather(table, OUT_FIRST, own(tokens, cells)), *outs)
+
+
+def columns_out_kernel(table, tokens, cells, grp, lat, both, out):
+    out[...] = gather(table, OUT_SECOND, own(tokens, cells) | arrivals(grp, lat, both)).astype(LOW)
 
 
 def all_out_kernel(table, tokens, cells, grp, lat, both, lon, fine, coarse):
@@ -422,7 +430,7 @@
 
 def shift_forward(table, tokens, cells):
     parts = to_neighbours(call(planes_in_kernel, PLANES, tokens, cells), -1)
-    (columns,) = call(columns_in_kernel, [(108, 512)], table, tokens, cells, *parts)
+    (columns,) = call(columns_in_kernel, [(108, 512)], tokens, cells, *parts)
     return (*parts, from_behind(columns, LON, -1))
 
 
@@ -484,9 +492,12 @@
     )
     merged_normed, token_grads = tied(merged_normed, token_grads)
     coarse_field = dot_nn(merged_normed, merging_weight).astype(LOW)
-    kept, sent, bundle, coarse_field = tied(kept, sent, bundle, coarse_field)
+    packed = call(planes_out_kernel, PLANES, table, token_grads, coarse_field)
+    kept, sent, bundle, *packed = tied(kept, sent, bundle, *packed)
     came = from_behind(sent, ("core",), 1)
     block_terms = (kept.astype(WIDE) + came.astype(WIDE)).astype(LOW)
+    parts_out = to_neighbours(packed, 1)
+    block_terms, *parts_out = tied(block_terms, *parts_out)
     block_planes = over_planes(block_terms)
     other_normed = from_behind(bundle[:, 2:], ("core",), 1)
     merging_kept, merging_sent = call(
@@ -496,20 +507,16 @@
         scratch=[(512, 256)], scalars=1,
     )
     merging_came = from_behind(merging_sent, ("xh",), 1)
-    (lon_out,) = call(columns_out_kernel, [(108, 512)], table, token_grads, coarse_field)
+    (lon_out,) = call(columns_out_kernel, [(108, 512)], table, token_grads, coarse_field, *parts_out)
     lon_out = from_behind(lon_out, LON, 1)
-    parts_out = call(planes_out_kernel, PLANES, table, token_grads, coarse_field, lon_out)
-    block_planes, merging_came, *parts_out = tied(block_planes, merging_came, *parts_out)
-    parts_out = to_neighbours(parts_out, 1)
+    token_grads, coarse_field = call(
+        all_out_kernel, [(288, 512), (72, 1024)], table, token_grads, coarse_field, *parts_out, lon_out
+    )
+    block_planes, merging_came, coarse_field = tied(block_planes, merging_came, coarse_field)
     merging_planes = (merging_kept.astype(WIDE) + merging_came.astype(WIDE)).astype(LOW).reshape(8, 32, 256)
     planes = jnp.concatenate([block_planes, merging_planes], axis=2)
     share = wide_sum(lax.all_to_all(planes, ("z",), 0, 0))
-    share, first = tied(share, parts_out[0])
-    parts_out = (first, *parts_out[1:])
     shares = lax.all_to_all(jnp.broadcast_to(share[None], (8, 32, 384)), ("lat", "grp"), 0, 0)
-    token_grads, coarse_field = call(
-        all_out_kernel, [(288, 512), (72, 1024)], table, token_grads, coarse_field, *parts_out, lon_out
-    )
     grads = call(shares_kernel, [(48, 512, WIDE), (16, 512, WIDE), (32, 2048, WIDE)], shares)
     return (
         coarse_field.reshape(2, 3, 12, 1024),

time: 129 us -> 127 us (0.984)
  blocking collectives: 0 us -> 13.7 us
  waiting for transfers between devices: 41.1 us -> 30.5 us
  starting transfers between devices: 39.1 us -> 35.2 us
    all_to_all x0 -> x1, blocking collectives: none -> 13.7 us  [body(): share = wide_sum(lax.all_to_all(planes, ('z',), 0, 0))]
    all_to_all x1 -> x0, waiting for transfers between devices: 8.36 us -> none  [body(): share = wide_sum(lax.all_to_all(planes, ('z',), 0, 0))]
    all_to_all x1, waiting for transfers between devices: 0.01 us -> 4.94 us  [body(): lax.all_to_all(jnp.broadcast_to(share[None], (8, 32, 384)), ('lat', 'grp'...]
    all_to_all x1 -> x0, starting transfers between devices: 3.39 us -> none  [body(): share = wide_sum(lax.all_to_all(planes, ('z',), 0, 0))]
    all_to_all x1, waiting for transfers between devices: 4.54 us -> 1.28 us  [over_planes(): return wide_sum(lax.all_to_all(terms, ('xh', 'lat', 'grp'), 0, 0))]
    ppermute x2, waiting for transfers between devices: 2.76 us -> 1.13 us  [to_neighbours(): lax.ppermute(both, ('lat', 'grp'), pairs)]
    ppermute x12, waiting for transfers between devices: 22.8 us -> 21.2 us  [from_behind(): return lax.ppermute(value, axis, pairs)]
    ppermute x12, starting transfers between devices: 17 us -> 15.7 us  [from_behind(): return lax.ppermute(value, axis, pairs)]
  transfers between devices with their start and end apart: 18 -> 17, of which waited for: 13 -> 12; matrix products, arithmetic and copies ran while one was open for 7% -> 9% of each run, Pallas kernels for 13% -> 13%
where the time goes in v4:
time: 127 us
  starting transfers between devices  35.2 us (28%)
  Pallas kernels  31.1 us (24%)
  waiting for transfers between devices  30.5 us (24%)
  blocking collectives  13.7 us (11%)
  local copies, waits for them, and re-layouts  8.04 us (6%)
  matrix products  4.54 us (4%)
  other arithmetic  2.74 us (2%)
    pallas_call x10, Pallas kernels, call(): pl.pallas_call(kernel, in_specs=specs, out_specs=out_specs, out_shape=[ja...  31.1 us
    ppermute x12, waiting for transfers between devices, from_behind(): return lax.ppermute(value, axis, pairs)  21.2 us
    ppermute x12, starting transfers between devices, from_behind(): return lax.ppermute(value, axis, pairs)  15.7 us
    all_to_all x1, blocking collectives, body(): share = wide_sum(lax.all_to_all(planes, ('z',), 0, 0))  13.7 us
    all_to_all x1, starting transfers between devices, over_planes(): return wide_sum(lax.all_to_all(terms, ('xh', 'lat', 'grp'), 0, 0))  6.44 us
    all_to_all x1, starting transfers between devices, body(): bundle = lax.all_to_all(bundle, ('lat', 'grp'), 0, 0)  5.78 us
    all_to_all x1, waiting for transfers between devices, body(): lax.all_to_all(jnp.broadcast_to(share[None], (8, 32, 384)), ('lat', 'grp'...  4.94 us
    all_to_all x1, starting transfers between devices, body(): lax.all_to_all(jnp.broadcast_to(share[None], (8, 32, 384)), ('lat', 'grp'...  4.75 us
  transfers between devices with their start and end apart: 17, of which 12 were waited for; matrix products, arithmetic and copies ran while one was open for 9% of the time, Pallas kernels for 13%

profile of v4, /device:TPU:2, one launch (start us, length us, event | category | flops | bytes accessed | tf_op | source)
XLA Modules:
  0.0 126.6 jit_solution(15888628549773386759)
XLA Ops:
  3.1 2.4 %collective-permute-start = (bf16[120,512]{1,0:T(8,128)(2,1)S(1)}, bf16[120,512]{1,0:T(8,128)(2,1)S(1)}, u32[]{:S(2)}, u32[]{:S(2)}) collective-permute-start(bf16[120,512]{1,0:T(8,128)(2,1)S(1)} %get-tuple-element.51), channel_id=1, source_target_pairs={{0,1},{1,0},{2,3},{3,2},{4,5},{5,4},{6,7},{7,6},{8,9},{9,8},{10,11... | collective-permute-start | bytes 368648 | tf_op jit(solution)/shard_map/ppermute | solution.py:409
  5.5 1.3 %collective-permute-start.1 = (bf16[96,512]{1,0:T(8,128)(2,1)S(1)}, bf16[96,512]{1,0:T(8,128)(2,1)S(1)}, u32[]{:S(2)}, u32[]{:S(2)}) collective-permute-start(bf16[96,512]{1,0:T(8,128)(2,1)S(1)} %get-tuple-element.52), channel_id=1, source_target_pairs={{0,192},{64,0},{128,64},{192,128},{1,193},{65,1},{129,65},{193,129... | collective-permute-start | bytes 294920 | tf_op jit(solution)/shard_map/ppermute | solution.py:409
  6.8 1.7 %collective-permute-start.2 = (bf16[96,512]{1,0:T(8,128)(2,1)S(1)}, bf16[96,512]{1,0:T(8,128)(2,1)S(1)}, u32[]{:S(2)}, u32[]{:S(2)}) collective-permute-start(bf16[96,512]{1,0:T(8,128)(2,1)S(1)} %get-tuple-element.53), channel_id=1, source_target_pairs={{0,193},{1,192},{64,1},{65,0},{128,65},{129,64},{192,129},{193,128... | collective-permute-start | bytes 294920 | tf_op jit(solution)/shard_map/ppermute | solution.py:424
  8.4 2.7 %collective-permute-done.1.lat = bf16[96,512]{1,0:T(8,128)(2,1)S(1)} collective-permute-done((bf16[96,512]{1,0:T(8,128)(2,1)S(1)}, bf16[96,512]{1,0:T(8,128)(2,1)S(1)}, u32[]{:S(2)}, u32[]{:S(2)}) %collective-permute-start.1) | collective-permute-done | bytes 98336 | tf_op jit(solution)/shard_map/ppermute | solution.py:409
  12.7 5.5 %collective-permute-start.3 = (bf16[108,512]{1,0:T(8,128)(2,1)S(1)}, bf16[108,512]{1,0:T(8,128)(2,1)S(1)}, u32[]{:S(2)}, u32[]{:S(2)}) collective-permute-start(bf16[108,512]{1,0:T(8,128)(2,1)S(1)} %shard_map.111), channel_id=1, source_target_pairs={{0,62},{2,0},{4,2},{6,4},{8,6},{10,8},{12,10},{14,12},{16,14},{18,... | collective-permute-start | bytes 331784 | tf_op jit(solution)/shard_map/ppermute | solution.py:409
  21.2 10.7 %shard_map.112 = (bf16[288,512]{1,0:T(8,128)(2,1)}, bf16[48,512]{1,0:T(8,128)(2,1)}, bf16[288,512]{1,0:T(8,128)(2,1)}, bf16[288,1536]{1,0:T(8,128)(2,1)}, bf16[2...) custom-call(s32[1]{0:T(128)} %bitcast.core, ...), custom_call_target="tpu_custom_call" | custom-call | tf_op jit(solution)/shard_map/pallas_call | solution.py:393
  33.0 3.7 %fusion.upstream = f32[72,2048]{1,0:T(8,128)S(1)} fusion(bf16[72,1024]{1,0:T(8,128)(2,1)} %get-tuple-element.56, bf16[2048,1024]{1,0:T(8,128)(2,1)} %param.11), kind=kOutput, calls=%fused_computation.5 | convolution fusion | flops 301989888 | bytes 4931584 | tf_op jit(solution)/shard_map/dot_general | solution.py:124
  37.6 2.3 %shard_map.113 = (bf16[72,2048]{1,0:T(8,128)(2,1)S(1)}, bf16[8,4,72,256]{3,2,1,0:T(8,128)(2,1)}, bf16[288,512]{1,0:T(8,128)(2,1)S(1)}, bf16[48,512]{1,0:T(8,128)(2,1)S(1)}) custom-call(s32[432,11]{1,0:T(8,128)S(1)} %copy-done, bf16[288,512]{1,0:T(8,128)(2,1)S(1)} %copy-done.9, bf16[48,512]{1,0:T(8,128)(2,1)S(1)} %collective-permute-done.4.prior, ...), custom_call_target="tpu_custom_call" | custom-call | tf_op jit(solution)/shard_map/pallas_call | solution.py:393
  40.6 1.4 %collective-permute-start.6 = (bf16[48,512]{1,0:T(8,128)(2,1)S(1)}, bf16[48,512]{1,0:T(8,128)(2,1)S(1)}, u32[]{:S(2)}, u32[]{:S(2)}) collective-permute-start(bf16[48,512]{1,0:T(8,128)(2,1)S(1)} %get-tuple-element.60), channel_id=1, source_target_pairs={{0,192},{64,0},{128,64},{192,128},{1,193},{65,1},{129,65},{193,129... | collective-permute-start | bytes 147464 | tf_op jit(solution)/shard_map/ppermute | solution.py:409
  42.1 2.7 %collective-permute-done.6.next_row = bf16[48,512]{1,0:T(8,128)(2,1)S(1)} collective-permute-done((bf16[48,512]{1,0:T(8,128)(2,1)S(1)}, bf16[48,512]{1,0:T(8,128)(2,1)S(1)}, u32[]{:S(2)}, u32[]{:S(2)}) %collective-permute-start.6) | collective-permute-done | bytes 49184 | tf_op jit(solution)/shard_map/ppermute | solution.py:409
  44.7 5.8 %all-to-all-start = ((bf16[8,4,72,256]{3,2,1,0:T(8,128)(2,1)}), bf16[8,4,72,256]{3,2,1,0:T(8,128)(2,1)S(1)}, u32[]{:S(2)}, u32[]{:S(2)}) async-start(bf16[8,4,72,256]{3,2,1,0:T(8,128)(2,1)} %get-tuple-element.69), calls=%async_computation | async-start | bytes 2359296 | tf_op jit(solution)/shard_map/all_to_all | solution.py:481
  50.5 12.4 %shard_map.114 = (bf16[288,512]{1,0:T(8,128)(2,1)}, bf16[2,4,2,8,32,128]{5,4,3,2,1,0:T(8,128)(2,1)}, bf16[2,4,2,8,32,128]{5,4,3,2,1,0:T(8,128)(2,1)}) custom-call(s32[1]{0:T(128)} %bitcast.core, s32[432,11]{1,0:T(8,128)} %constant.14.clone.table, bf16[288,512]{1,0:T(8,128)(2,1)} %copy-done.8, bf16[48,512]{1,0:T(8,128)(2,1)} %copy-done.14, ...), custom_call_target="tpu_custom_call" | custom-call | tf_op jit(solution)/shard_map/pallas_call | solution.py:393
  64.4 1.9 %all-to-all-done.bundle = bf16[8,4,72,256]{3,2,1,0:T(8,128)(2,1)S(1)} async-done(((bf16[8,4,72,256]{3,2,1,0:T(8,128)(2,1)}), bf16[8,4,72,256]{3,2,1,0:T(8,128)(2,1)S(1)}, u32[]{:S(2)}, u32[]{:S(2)}) %all-to-all-start) | async-done | bytes 1179680 | tf_op jit(solution)/shard_map/all_to_all | solution.py:481
  70.5 4.4 %collective-permute-done.9.lat = bf16[96,512]{1,0:T(8,128)(2,1)S(1)} collective-permute-done((bf16[96,512]{1,0:T(8,128)(2,1)S(1)}, bf16[96,512]{1,0:T(8,128)(2,1)S(1)}, u32[]{:S(2)}, u32[]{:S(2)}) %collective-permute-start.9) | collective-permute-done | bytes 98336 | tf_op jit(solution)/shard_map/ppermute | solution.py:409
  74.9 6.4 %all-to-all-start.1 = ((bf16[16,8,32,128]{3,2,1,0:T(8,128)(2,1)}), bf16[16,8,32,128]{3,2,1,0:T(8,128)(2,1)}, u32[]{:S(2)}, u32[]{:S(2)}) async-start(bf16[16,8,32,128]{3,2,1,0:T(8,128)(2,1)} %bitcast.3), calls=%async_computation.1 | async-start | bytes 2097152 | tf_op jit(solution)/shard_map/all_to_all | solution.py:443
  82.2 2.2 %collective-permute-done.11.other_normed = bf16[8,2,72,256]{3,2,1,0:T(8,128)(2,1)S(1)} collective-permute-done((bf16[8,2,72,256]{3,2,1,0:T(8,128)(2,1)}, bf16[8,2,72,256]{3,2,1,0:T(8,128)(2,1)S(1)}, u32[]{:S(2)}, u32[]{:S(2)}) %collective-permute-start.11) | collective-permute-done | bytes 589856 | tf_op jit(solution)/shard_map/ppermute | solution.py:409
  84.4 1.3 %shard_map.116 = (bf16[256,256]{1,0:T(8,128)(2,1)S(1)}, bf16[256,256]{1,0:T(8,128)(2,1)S(1)}) custom-call(s32[1]{0:T(128)} %bitcast.4.xh, bf16[8,4,72,256]{3,2,1,0:T(8,128)(2,1)S(1)} %all-to-all-done.bundle, bf16[8,2,72,256]{3,2,1,0:T(8,128)(2,1)S(1)} %collective-permute-done.11.other_normed), custom_call_target="tpu_custom_call" | custom-call | tf_op jit(solution)/shard_map/pallas_call | solution.py:393
  85.7 2.2 %collective-permute-start.12 = (bf16[256,256]{1,0:T(8,128)(2,1)S(1)}, bf16[256,256]{1,0:T(8,128)(2,1)S(1)}, u32[]{:S(2)}, u32[]{:S(2)}) collective-permute-start(bf16[256,256]{1,0:T(8,128)(2,1)S(1)} %get-tuple-element.84), channel_id=1, source_target_pairs={{0,32},{32,0},{1,33},{33,1},{2,34},{34,2},{3,35},{35,3},{4,36},{36... | collective-permute-start | bytes 393224 | tf_op jit(solution)/shard_map/ppermute | solution.py:409
  88.4 8.0 %collective-permute-done.13.lon = bf16[108,512]{1,0:T(8,128)(2,1)S(1)} collective-permute-done((bf16[108,512]{1,0:T(8,128)(2,1)S(1)}, bf16[108,512]{1,0:T(8,128)(2,1)S(1)}, u32[]{:S(2)}, u32[]{:S(2)}) %collective-permute-start.13) | collective-permute-done | bytes 110624 | tf_op jit(solution)/shard_map/ppermute | solution.py:409
  96.3 1.8 %shard_map.118 = (bf16[288,512]{1,0:T(8,128)(2,1)}, bf16[72,1024]{1,0:T(8,128)(2,1)S(1)}) custom-call(s32[432,11]{1,0:T(8,128)S(1)} %copy-done.1, bf16[288,512]{1,0:T(8,128)(2,1)S(1)} %copy-done.3, bf16[72,1024]{1,0:T(8,128)(2,1)S(1)} %convolution_convert_fusion.cells, bf16[120,512]{1,0:T(8,128)(2,1)S(1)} %collective-permute-done.8.grp, ...), custom_call_target="tpu_custom_call" | custom-call | tf_op jit(solution)/shard_map/pallas_call | solution.py:393
  99.4 1.4 %reduce_sum.24 = bf16[8,32,128]{2,1,0:T(8,128)(2,1)S(1)} reduce(bf16[16,8,32,128]{3,2,1,0:T(8,128)(2,1)} %all-to-all-done.1, bf16[]{:T(256)} %constant.12.clone.1), dimensions={0}, to_apply=%region_0.0 | reduce | flops 491520 | bytes 1114114 | tf_op jit(solution)/shard_map/reduce_sum | solution.py:438
  100.9 13.7 %all_to_all.20 = bf16[8,32,384]{2,1,0:T(8,128)(2,1)S(1)} all-to-all(bf16[8,32,384]{2,1,0:T(8,128)(2,1)S(1)} %pad_maximum_fusion), channel_id=1, replica_groups=mesh['lat'=4,'xh'=2,'z'=8,'core'=2,'grp'=2] {'z'}, dimensions={0} | all-to-all | bytes 393216 | tf_op jit(solution)/shard_map/all_to_all | solution.py:518
  115.3 4.8 %all-to-all-start.3 = ((bf16[8,32,384]{2,1,0:T(8,128)(2,1)}), bf16[8,32,384]{2,1,0:T(8,128)(2,1)S(1)}, u32[]{:S(2)}, u32[]{:S(2)}) async-start(bf16[8,32,384]{2,1,0:T(8,128)(2,1)} %broadcast_in_dim.2), calls=%async_computation.3 | async-start | bytes 393216 | tf_op jit(solution)/shard_map/all_to_all | solution.py:519
  120.9 4.9 %all-to-all-done.3.shares = bf16[8,32,384]{2,1,0:T(8,128)(2,1)S(1)} async-done(((bf16[8,32,384]{2,1,0:T(8,128)(2,1)}), bf16[8,32,384]{2,1,0:T(8,128)(2,1)S(1)}, u32[]{:S(2)}, u32[]{:S(2)}) %all-to-all-start.3) | async-done | bytes 196640 | tf_op jit(solution)/shard_map/all_to_all | solution.py:519
  (68 shorter events, 20.3 us)
Async XLA Ops:
  1.6 18.9 %copy-start.4 = (bf16[72,1024]{1,0:T(8,128)(2,1)}, bf16[72,1024]{1,0:T(8,128)(2,1)S(1)}, u32[]{:S(2)}) copy-start(bf16[72,1024]{1,0:T(8,128)(2,1)S(1)} %reshape.40.cells) | copy-start | bytes 442372
  3.1 9.2 %collective-permute-start = (bf16[120,512]{1,0:T(8,128)(2,1)S(1)}, bf16[120,512]{1,0:T(8,128)(2,1)S(1)}, u32[]{:S(2)}, u32[]{:S(2)}) collective-permute-start(bf16[120,512]{1,0:T(8,128)(2,1)S(1)} %get-tuple-element.51), channel_id=1, source_target_pairs={{0,1},{1,0},{2,3},{3,2},{4,5},{5,4},{6,7},{7,6},{8,9},{9,8},{10,11... | collective-permute-start | bytes 368648 | tf_op jit(solution)/shard_map/ppermute | solution.py:409
  5.5 5.7 %collective-permute-start.1 = (bf16[96,512]{1,0:T(8,128)(2,1)S(1)}, bf16[96,512]{1,0:T(8,128)(2,1)S(1)}, u32[]{:S(2)}, u32[]{:S(2)}) collective-permute-start(bf16[96,512]{1,0:T(8,128)(2,1)S(1)} %get-tuple-element.52), channel_id=1, source_target_pairs={{0,192},{64,0},{128,64},{192,128},{1,193},{65,1},{129,65},{193,129... | collective-permute-start | bytes 294920 | tf_op jit(solution)/shard_map/ppermute | solution.py:409
  6.8 5.5 %collective-permute-start.2 = (bf16[96,512]{1,0:T(8,128)(2,1)S(1)}, bf16[96,512]{1,0:T(8,128)(2,1)S(1)}, u32[]{:S(2)}, u32[]{:S(2)}) collective-permute-start(bf16[96,512]{1,0:T(8,128)(2,1)S(1)} %get-tuple-element.53), channel_id=1, source_target_pairs={{0,193},{1,192},{64,1},{65,0},{128,65},{129,64},{192,129},{193,128... | collective-permute-start | bytes 294920 | tf_op jit(solution)/shard_map/ppermute | solution.py:424
  11.2 9.4 %copy-start.6 = (bf16[96,512]{1,0:T(8,128)(2,1)}, bf16[96,512]{1,0:T(8,128)(2,1)S(1)}, u32[]{:S(2)}) copy-start(bf16[96,512]{1,0:T(8,128)(2,1)S(1)} %collective-permute-done.1.lat) | copy-start | bytes 294916
  12.3 8.3 %copy-start.7 = (bf16[96,512]{1,0:T(8,128)(2,1)}, bf16[96,512]{1,0:T(8,128)(2,1)S(1)}, u32[]{:S(2)}) copy-start(bf16[96,512]{1,0:T(8,128)(2,1)S(1)} %collective-permute-done.2.both) | copy-start | bytes 294916
  12.3 8.3 %copy-start.5 = (bf16[120,512]{1,0:T(8,128)(2,1)}, bf16[120,512]{1,0:T(8,128)(2,1)S(1)}, u32[]{:S(2)}) copy-start(bf16[120,512]{1,0:T(8,128)(2,1)S(1)} %collective-permute-done.grp) | copy-start | bytes 368644
  12.7 7.9 %collective-permute-start.3 = (bf16[108,512]{1,0:T(8,128)(2,1)S(1)}, bf16[108,512]{1,0:T(8,128)(2,1)S(1)}, u32[]{:S(2)}, u32[]{:S(2)}) collective-permute-start(bf16[108,512]{1,0:T(8,128)(2,1)S(1)} %shard_map.111), channel_id=1, source_target_pairs={{0,62},{2,0},{4,2},{6,4},{8,6},{10,8},{12,10},{14,12},{16,14},{18,... | collective-permute-start | bytes 331784 | tf_op jit(solution)/shard_map/ppermute | solution.py:409
  19.6 17.9 %copy-start = (s32[432,11]{1,0:T(8,128)S(1)}, s32[432,11]{1,0:T(8,128)}, u32[]{:S(2)}) copy-start(s32[432,11]{1,0:T(8,128)} %constant.14.clone.table) | copy-start | bytes 57028
  32.0 5.6 %collective-permute-start.4 = (bf16[48,512]{1,0:T(8,128)(2,1)}, bf16[48,512]{1,0:T(8,128)(2,1)S(1)}, u32[]{:S(2)}, u32[]{:S(2)}) collective-permute-start(bf16[48,512]{1,0:T(8,128)(2,1)} %get-tuple-element.55), channel_id=1, source_target_pairs={{0,64},{64,128},{128,192},{192,0},{1,65},{65,129},{129,193},{193,1... | collective-permute-start | bytes 147464 | tf_op jit(solution)/shard_map/ppermute | solution.py:409
  33.0 4.6 %collective-permute-start.5 = (bf16[2,72,256]{2,1,0:T(8,128)(2,1)}, bf16[2,72,256]{2,1,0:T(8,128)(2,1)S(1)}, u32[]{:S(2)}, u32[]{:S(2)}) collective-permute-start(bf16[2,72,256]{2,1,0:T(8,128)(2,1)} %get-tuple-element.58), channel_id=1, source_target_pairs={{0,2},{2,0},{1,3},{3,1},{4,6},{6,4},{5,7},{7,5},{8,10},{10,8},{9,1... | collective-permute-start | bytes 221192 | tf_op jit(solution)/shard_map/ppermute | solution.py:409
  40.6 4.1 %collective-permute-start.6 = (bf16[48,512]{1,0:T(8,128)(2,1)S(1)}, bf16[48,512]{1,0:T(8,128)(2,1)S(1)}, u32[]{:S(2)}, u32[]{:S(2)}) collective-permute-start(bf16[48,512]{1,0:T(8,128)(2,1)S(1)} %get-tuple-element.60), channel_id=1, source_target_pairs={{0,192},{64,0},{128,64},{192,128},{1,193},{65,1},{129,65},{193,129... | collective-permute-start | bytes 147464 | tf_op jit(solution)/shard_map/ppermute | solution.py:409
  44.7 21.6 %all-to-all-start = ((bf16[8,4,72,256]{3,2,1,0:T(8,128)(2,1)}), bf16[8,4,72,256]{3,2,1,0:T(8,128)(2,1)S(1)}, u32[]{:S(2)}, u32[]{:S(2)}) async-start(bf16[8,4,72,256]{3,2,1,0:T(8,128)(2,1)} %get-tuple-element.69), calls=%async_computation | async-start | bytes 2359296 | tf_op jit(solution)/shard_map/all_to_all | solution.py:481
  50.5 12.4 %copy-start.11 = (bf16[2048,1024]{1,0:T(8,128)(2,1)S(1)}, bf16[2048,1024]{1,0:T(8,128)(2,1)}, u32[]{:S(2)}) copy-start(bf16[2048,1024]{1,0:T(8,128)(2,1)} %param.11) | copy-start | bytes 12582916
  50.5 13.3 %copy-start.1 = (s32[432,11]{1,0:T(8,128)S(1)}, s32[432,11]{1,0:T(8,128)}, u32[]{:S(2)}) copy-start(s32[432,11]{1,0:T(8,128)} %constant.14.clone.table) | copy-start | bytes 57028
  66.3 2.9 %collective-permute-start.7 = (bf16[2,4,2,8,32,128]{5,4,3,2,1,0:T(8,128)(2,1)}, bf16[2,4,2,8,32,128]{5,4,3,2,1,0:T(8,128)(2,1)S(1)}, u32[]{:S(2)}, u32[]{:S(2)}) collective-permute-start(bf16[2,4,2,8,32,128]{5,4,3,2,1,0:T(8,128)(2,1)} %get-tuple-element.78), channel_id=1, source_target_pairs={{0,2},{2,0},{1,3},{3,1},{4,6},{6,4},{5,7},{7,5},{8,10},{10,8},{9,1... | collective-permute-start | bytes 3145736 | tf_op jit(solution)/shard_map/ppermute | solution.py:409
  66.3 8.5 %collective-permute-start.9 = (bf16[96,512]{1,0:T(8,128)(2,1)S(1)}, bf16[96,512]{1,0:T(8,128)(2,1)S(1)}, u32[]{:S(2)}, u32[]{:S(2)}) collective-permute-start(bf16[96,512]{1,0:T(8,128)(2,1)S(1)} %get-tuple-element.80), channel_id=1, source_target_pairs={{0,64},{64,128},{128,192},{192,0},{1,65},{65,129},{129,193},{193,1... | collective-permute-start | bytes 294920 | tf_op jit(solution)/shard_map/ppermute | solution.py:409
  66.9 8.0 %collective-permute-start.10 = (bf16[96,512]{1,0:T(8,128)(2,1)S(1)}, bf16[96,512]{1,0:T(8,128)(2,1)S(1)}, u32[]{:S(2)}, u32[]{:S(2)}) collective-permute-start(bf16[96,512]{1,0:T(8,128)(2,1)S(1)} %get-tuple-element.81), channel_id=1, source_target_pairs={{0,65},{1,64},{64,129},{65,128},{128,193},{129,192},{192,1},{193,0... | collective-permute-start | bytes 294920 | tf_op jit(solution)/shard_map/ppermute | solution.py:424
  67.8 7.1 %collective-permute-start.8 = (bf16[120,512]{1,0:T(8,128)(2,1)S(1)}, bf16[120,512]{1,0:T(8,128)(2,1)S(1)}, u32[]{:S(2)}, u32[]{:S(2)}) collective-permute-start(bf16[120,512]{1,0:T(8,128)(2,1)S(1)} %get-tuple-element.79), channel_id=1, source_target_pairs={{0,1},{1,0},{2,3},{3,2},{4,5},{5,4},{6,7},{7,6},{8,9},{9,8},{10,11... | collective-permute-start | bytes 368648 | tf_op jit(solution)/shard_map/ppermute | solution.py:409
  74.9 24.5 %all-to-all-start.1 = ((bf16[16,8,32,128]{3,2,1,0:T(8,128)(2,1)}), bf16[16,8,32,128]{3,2,1,0:T(8,128)(2,1)}, u32[]{:S(2)}, u32[]{:S(2)}) async-start(bf16[16,8,32,128]{3,2,1,0:T(8,128)(2,1)} %bitcast.3), calls=%async_computation.1 | async-start | bytes 2097152 | tf_op jit(solution)/shard_map/all_to_all | solution.py:443
  82.2 2.2 %collective-permute-start.11 = (bf16[8,2,72,256]{3,2,1,0:T(8,128)(2,1)}, bf16[8,2,72,256]{3,2,1,0:T(8,128)(2,1)S(1)}, u32[]{:S(2)}, u32[]{:S(2)}) collective-permute-start(bf16[8,2,72,256]{3,2,1,0:T(8,128)(2,1)} %slice.3), channel_id=1, source_target_pairs={{0,2},{2,0},{1,3},{3,1},{4,6},{6,4},{5,7},{7,5},{8,10},{10,8},{9,1... | collective-permute-start | bytes 1769480 | tf_op jit(solution)/shard_map/ppermute | solution.py:409
  85.7 15.1 %collective-permute-start.12 = (bf16[256,256]{1,0:T(8,128)(2,1)S(1)}, bf16[256,256]{1,0:T(8,128)(2,1)S(1)}, u32[]{:S(2)}, u32[]{:S(2)}) collective-permute-start(bf16[256,256]{1,0:T(8,128)(2,1)S(1)} %get-tuple-element.84), channel_id=1, source_target_pairs={{0,32},{32,0},{1,33},{33,1},{2,34},{34,2},{3,35},{35,3},{4,36},{36... | collective-permute-start | bytes 393224 | tf_op jit(solution)/shard_map/ppermute | solution.py:409
  88.3 8.1 %collective-permute-start.13 = (bf16[108,512]{1,0:T(8,128)(2,1)S(1)}, bf16[108,512]{1,0:T(8,128)(2,1)S(1)}, u32[]{:S(2)}, u32[]{:S(2)}) collective-permute-start(bf16[108,512]{1,0:T(8,128)(2,1)S(1)} %shard_map.117), channel_id=1, source_target_pairs={{0,2},{2,4},{4,6},{6,8},{8,10},{10,12},{12,14},{14,16},{16,18},{18... | collective-permute-start | bytes 331784 | tf_op jit(solution)/shard_map/ppermute | solution.py:409
  115.3 10.5 %all-to-all-start.3 = ((bf16[8,32,384]{2,1,0:T(8,128)(2,1)}), bf16[8,32,384]{2,1,0:T(8,128)(2,1)S(1)}, u32[]{:S(2)}, u32[]{:S(2)}) async-start(bf16[8,32,384]{2,1,0:T(8,128)(2,1)} %broadcast_in_dim.2), calls=%async_computation.3 | async-start | bytes 393216 | tf_op jit(solution)/shard_map/all_to_all | solution.py:519
  (8 other events, 26.7 us)

commit v5 on v4

--- a/solution.py
+++ b/solution.py
@@ -497,7 +497,6 @@
     came = from_behind(sent, ("core",), 1)
     block_terms = (kept.astype(WIDE) + came.astype(WIDE)).astype(LOW)
     parts_out = to_neighbours(packed, 1)
-    block_terms, *parts_out = tied(block_terms, *parts_out)
     block_planes = over_planes(block_terms)
     other_normed = from_behind(bundle[:, 2:], ("core",), 1)
     merging_kept, merging_sent = call(
@@ -507,15 +506,17 @@
         scratch=[(512, 256)], scalars=1,
     )
     merging_came = from_behind(merging_sent, ("xh",), 1)
+    block_planes, merging_came, grp_out, lat_out = tied(block_planes, merging_came, *parts_out[:2])
+    parts_out = (grp_out, lat_out, parts_out[2])
     (lon_out,) = call(columns_out_kernel, [(108, 512)], table, token_grads, coarse_field, *parts_out)
-    lon_out = from_behind(lon_out, LON, 1)
-    token_grads, coarse_field = call(
-        all_out_kernel, [(288, 512), (72, 1024)], table, token_grads, coarse_field, *parts_out, lon_out
-    )
-    block_planes, merging_came, coarse_field = tied(block_planes, merging_came, coarse_field)
     merging_planes = (merging_kept.astype(WIDE) + merging_came.astype(WIDE)).astype(LOW).reshape(8, 32, 256)
     planes = jnp.concatenate([block_planes, merging_planes], axis=2)
     share = wide_sum(lax.all_to_all(planes, ("z",), 0, 0))
+    lon_out = from_behind(lon_out, LON, 1)
+    share, lon_out = tied(share, lon_out)
+    token_grads, coarse_field = call(
+        all_out_kernel, [(288, 512), (72, 1024)], table, token_grads, coarse_field, *parts_out, lon_out
+    )
     shares = lax.all_to_all(jnp.broadcast_to(share[None], (8, 32, 384)), ("lat", "grp"), 0, 0)
     grads = call(shares_kernel, [(48, 512, WIDE), (16, 512, WIDE), (32, 2048, WIDE)], shares)
     return (

time: 127 us -> 128 us (level)
  blocking collectives: 13.7 us -> 0 us
  waiting for transfers between devices: 30.5 us -> 39.4 us
  starting transfers between devices: 35.2 us -> 39.7 us
    all_to_all x1 -> x0, blocking collectives: 13.7 us -> none  [body(): share = wide_sum(lax.all_to_all(planes, ('z',), 0, 0))]
    all_to_all x1, waiting for transfers between devices: 1.28 us -> 8.64 us  [over_planes(): return wide_sum(lax.all_to_all(terms, ('xh', 'lat', 'grp'), 0, 0))]
    ppermute x2, waiting for transfers between devices: 1.13 us -> 6.43 us  [to_neighbours(): lax.ppermute(both, ('lat', 'grp'), pairs)]
    ppermute x12, waiting for transfers between devices: 21.2 us -> 16.8 us  [from_behind(): return lax.ppermute(value, axis, pairs)]
    all_to_all x0 -> x1, starting transfers between devices: none -> 4.25 us  [body(): share = wide_sum(lax.all_to_all(planes, ('z',), 0, 0))]
    all_to_all x0 -> x1, waiting for transfers between devices: none -> 2.54 us  [body(): share = wide_sum(lax.all_to_all(planes, ('z',), 0, 0))]
    all_to_all x1, waiting for transfers between devices: 4.94 us -> 3.14 us  [body(): lax.all_to_all(jnp.broadcast_to(share[None], (8, 32, 384)), ('lat', 'grp'...]
  transfers between devices with their start and end apart: 17 -> 18, of which waited for: 12 -> 13; matrix products, arithmetic and copies ran while one was open for 9% -> 8% of each run, Pallas kernels for 13% -> 13%
where the time goes in v5:
time: 128 us; the launch traced here: 127 us
  starting transfers between devices  39.7 us (31%)
  waiting for transfers between devices  39.4 us (31%)
  Pallas kernels  31.1 us (24%)
  local copies, waits for them, and re-layouts  8.05 us (6%)
  matrix products  4.54 us (4%)
  other arithmetic  3.43 us (3%)
    pallas_call x10, Pallas kernels, call(): pl.pallas_call(kernel, in_specs=specs, out_specs=out_specs, out_shape=[ja...  31.1 us
    ppermute x12, starting transfers between devices, from_behind(): return lax.ppermute(value, axis, pairs)  16.8 us
    ppermute x12, waiting for transfers between devices, from_behind(): return lax.ppermute(value, axis, pairs)  16.8 us
    all_to_all x1, waiting for transfers between devices, over_planes(): return wide_sum(lax.all_to_all(terms, ('xh', 'lat', 'grp'), 0, 0))  8.64 us
    ppermute x2, waiting for transfers between devices, to_neighbours(): lax.ppermute(both, ('lat', 'grp'), pairs)  6.43 us
    all_to_all x1, starting transfers between devices, body(): bundle = lax.all_to_all(bundle, ('lat', 'grp'), 0, 0)  5.77 us
    all_to_all x1, starting transfers between devices, over_planes(): return wide_sum(lax.all_to_all(terms, ('xh', 'lat', 'grp'), 0, 0))  5.23 us
    all_to_all x1, starting transfers between devices, body(): lax.all_to_all(jnp.broadcast_to(share[None], (8, 32, 384)), ('lat', 'grp'...  4.52 us
  transfers between devices with their start and end apart: 18, of which 13 were waited for; matrix products, arithmetic and copies ran while one was open for 8% of the time, Pallas kernels for 13%

profile of v5, /device:TPU:2, one launch (start us, length us, event | category | flops | bytes accessed | tf_op | source)
XLA Modules:
  0.0 127.1 jit_solution(4926144709977793549)
XLA Ops:
  3.1 2.4 %collective-permute-start = (bf16[120,512]{1,0:T(8,128)(2,1)S(1)}, bf16[120,512]{1,0:T(8,128)(2,1)S(1)}, u32[]{:S(2)}, u32[]{:S(2)}) collective-permute-start(bf16[120,512]{1,0:T(8,128)(2,1)S(1)} %get-tuple-element.50), channel_id=1, source_target_pairs={{0,1},{1,0},{2,3},{3,2},{4,5},{5,4},{6,7},{7,6},{8,9},{9,8},{10,11... | collective-permute-start | bytes 368648 | tf_op jit(solution)/shard_map/ppermute | solution.py:409
  6.8 1.7 %collective-permute-start.2 = (bf16[96,512]{1,0:T(8,128)(2,1)S(1)}, bf16[96,512]{1,0:T(8,128)(2,1)S(1)}, u32[]{:S(2)}, u32[]{:S(2)}) collective-permute-start(bf16[96,512]{1,0:T(8,128)(2,1)S(1)} %get-tuple-element.52), channel_id=1, source_target_pairs={{0,193},{1,192},{64,1},{65,0},{128,65},{129,64},{192,129},{193,128... | collective-permute-start | bytes 294920 | tf_op jit(solution)/shard_map/ppermute | solution.py:424
  8.4 2.7 %collective-permute-done.1.lat = bf16[96,512]{1,0:T(8,128)(2,1)S(1)} collective-permute-done((bf16[96,512]{1,0:T(8,128)(2,1)S(1)}, bf16[96,512]{1,0:T(8,128)(2,1)S(1)}, u32[]{:S(2)}, u32[]{:S(2)}) %collective-permute-start.1) | collective-permute-done | bytes 98336 | tf_op jit(solution)/shard_map/ppermute | solution.py:409
  12.7 5.5 %collective-permute-start.3 = (bf16[108,512]{1,0:T(8,128)(2,1)S(1)}, bf16[108,512]{1,0:T(8,128)(2,1)S(1)}, u32[]{:S(2)}, u32[]{:S(2)}) collective-permute-start(bf16[108,512]{1,0:T(8,128)(2,1)S(1)} %shard_map.111), channel_id=1, source_target_pairs={{0,62},{2,0},{4,2},{6,4},{8,6},{10,8},{12,10},{14,12},{16,14},{18,... | collective-permute-start | bytes 331784 | tf_op jit(solution)/shard_map/ppermute | solution.py:409
  21.2 10.7 %shard_map.112 = (bf16[288,512]{1,0:T(8,128)(2,1)}, bf16[48,512]{1,0:T(8,128)(2,1)}, bf16[288,512]{1,0:T(8,128)(2,1)}, bf16[288,1536]{1,0:T(8,128)(2,1)}, bf16[2...) custom-call(s32[1]{0:T(128)} %bitcast.core, ...), custom_call_target="tpu_custom_call" | custom-call | tf_op jit(solution)/shard_map/pallas_call | solution.py:393
  33.0 3.7 %fusion.upstream = f32[72,2048]{1,0:T(8,128)S(1)} fusion(bf16[72,1024]{1,0:T(8,128)(2,1)} %get-tuple-element.55, bf16[2048,1024]{1,0:T(8,128)(2,1)} %param.11), kind=kOutput, calls=%fused_computation.5 | convolution fusion | flops 301989888 | bytes 4931584 | tf_op jit(solution)/shard_map/dot_general | solution.py:124
  37.6 2.3 %shard_map.113 = (bf16[72,2048]{1,0:T(8,128)(2,1)S(1)}, bf16[8,4,72,256]{3,2,1,0:T(8,128)(2,1)}, bf16[288,512]{1,0:T(8,128)(2,1)S(1)}, bf16[48,512]{1,0:T(8,128)(2,1)S(1)}) custom-call(s32[432,11]{1,0:T(8,128)S(1)} %copy-done, bf16[288,512]{1,0:T(8,128)(2,1)S(1)} %copy-done.9, bf16[48,512]{1,0:T(8,128)(2,1)S(1)} %collective-permute-done.4.prior, ...), custom_call_target="tpu_custom_call" | custom-call | tf_op jit(solution)/shard_map/pallas_call | solution.py:393
  42.1 2.7 %collective-permute-done.6.next_row = bf16[48,512]{1,0:T(8,128)(2,1)S(1)} collective-permute-done((bf16[48,512]{1,0:T(8,128)(2,1)S(1)}, bf16[48,512]{1,0:T(8,128)(2,1)S(1)}, u32[]{:S(2)}, u32[]{:S(2)}) %collective-permute-start.6) | collective-permute-done | bytes 49184 | tf_op jit(solution)/shard_map/ppermute | solution.py:409
  44.7 5.8 %all-to-all-start = ((bf16[8,4,72,256]{3,2,1,0:T(8,128)(2,1)}), bf16[8,4,72,256]{3,2,1,0:T(8,128)(2,1)S(1)}, u32[]{:S(2)}, u32[]{:S(2)}) async-start(bf16[8,4,72,256]{3,2,1,0:T(8,128)(2,1)} %get-tuple-element.72), calls=%async_computation | async-start | bytes 2359296 | tf_op jit(solution)/shard_map/all_to_all | solution.py:481
  50.5 12.4 %shard_map.114 = (bf16[288,512]{1,0:T(8,128)(2,1)}, bf16[2,4,2,8,32,128]{5,4,3,2,1,0:T(8,128)(2,1)}, bf16[2,4,2,8,32,128]{5,4,3,2,1,0:T(8,128)(2,1)}) custom-call(s32[1]{0:T(128)} %bitcast.core, s32[432,11]{1,0:T(8,128)} %constant.14.clone.table, bf16[288,512]{1,0:T(8,128)(2,1)} %copy-done.8, bf16[48,512]{1,0:T(8,128)(2,1)} %copy-done.14, ...), custom_call_target="tpu_custom_call" | custom-call | tf_op jit(solution)/shard_map/pallas_call | solution.py:393
  64.4 1.9 %all-to-all-done.bundle = bf16[8,4,72,256]{3,2,1,0:T(8,128)(2,1)S(1)} async-done(((bf16[8,4,72,256]{3,2,1,0:T(8,128)(2,1)}), bf16[8,4,72,256]{3,2,1,0:T(8,128)(2,1)S(1)}, u32[]{:S(2)}, u32[]{:S(2)}) %all-to-all-start) | async-done | bytes 1179680 | tf_op jit(solution)/shard_map/all_to_all | solution.py:481
  66.3 2.9 %collective-permute-done.7 = bf16[2,4,2,8,32,128]{5,4,3,2,1,0:T(8,128)(2,1)S(1)} collective-permute-done((bf16[2,4,2,8,32,128]{5,4,3,2,1,0:T(8,128)(2,1)}, bf16[2,4,2,8,32,128]{5,4,3,2,1,0:T(8,128)(2,1)S(1)}, u32[]{:S(2)}, u32[]{:S(2)}) %collective-permute-start.7) | collective-permute-done | bytes 1048608 | tf_op jit(solution)/shard_map/ppermute | solution.py:409
  70.5 5.2 %all-to-all-start.1 = ((bf16[16,8,32,128]{3,2,1,0:T(8,128)(2,1)}), bf16[16,8,32,128]{3,2,1,0:T(8,128)(2,1)}, u32[]{:S(2)}, u32[]{:S(2)}) async-start(bf16[16,8,32,128]{3,2,1,0:T(8,128)(2,1)} %bitcast.3), calls=%async_computation.1 | async-start | bytes 2097152 | tf_op jit(solution)/shard_map/all_to_all | solution.py:443
  76.6 2.2 %collective-permute-done.8.other_normed = bf16[8,2,72,256]{3,2,1,0:T(8,128)(2,1)S(1)} collective-permute-done((bf16[8,2,72,256]{3,2,1,0:T(8,128)(2,1)}, bf16[8,2,72,256]{3,2,1,0:T(8,128)(2,1)S(1)}, u32[]{:S(2)}, u32[]{:S(2)}) %collective-permute-start.8) | collective-permute-done | bytes 589856 | tf_op jit(solution)/shard_map/ppermute | solution.py:409
  80.1 2.2 %collective-permute-start.9 = (bf16[256,256]{1,0:T(8,128)(2,1)S(1)}, bf16[256,256]{1,0:T(8,128)(2,1)S(1)}, u32[]{:S(2)}, u32[]{:S(2)}) collective-permute-start(bf16[256,256]{1,0:T(8,128)(2,1)S(1)} %get-tuple-element.79), channel_id=1, source_target_pairs={{0,32},{32,0},{1,33},{33,1},{2,34},{34,2},{3,35},{35,3},{4,36},{36... | collective-permute-start | bytes 393224 | tf_op jit(solution)/shard_map/ppermute | solution.py:409
  83.8 1.5 %collective-permute-start.11 = (bf16[96,512]{1,0:T(8,128)(2,1)S(1)}, bf16[96,512]{1,0:T(8,128)(2,1)S(1)}, u32[]{:S(2)}, u32[]{:S(2)}) collective-permute-start(bf16[96,512]{1,0:T(8,128)(2,1)S(1)} %get-tuple-element.81), channel_id=1, source_target_pairs={{0,64},{64,128},{128,192},{192,0},{1,65},{65,129},{129,193},{193,1... | collective-permute-start | bytes 294920 | tf_op jit(solution)/shard_map/ppermute | solution.py:409
  85.2 8.6 %all-to-all-done.1 = bf16[16,8,32,128]{3,2,1,0:T(8,128)(2,1)} async-done(((bf16[16,8,32,128]{3,2,1,0:T(8,128)(2,1)}), bf16[16,8,32,128]{3,2,1,0:T(8,128)(2,1)}, u32[]{:S(2)}, u32[]{:S(2)}) %all-to-all-start.1) | async-done | bytes 1048608 | tf_op jit(solution)/shard_map/all_to_all | solution.py:443
  96.0 4.3 %all-to-all-start.2 = ((bf16[8,32,384]{2,1,0:T(8,128)(2,1)}), bf16[8,32,384]{2,1,0:T(8,128)(2,1)S(1)}, u32[]{:S(2)}, u32[]{:S(2)}) async-start(bf16[8,32,384]{2,1,0:T(8,128)(2,1)} %pad_maximum_fusion), calls=%async_computation.2 | async-start | bytes 393216 | tf_op jit(solution)/shard_map/all_to_all | solution.py:514
  101.7 5.3 %collective-permute-done.12.both = bf16[96,512]{1,0:T(8,128)(2,1)S(1)} collective-permute-done((bf16[96,512]{1,0:T(8,128)(2,1)S(1)}, bf16[96,512]{1,0:T(8,128)(2,1)S(1)}, u32[]{:S(2)}, u32[]{:S(2)}) %collective-permute-start.12) | collective-permute-done | bytes 98336 | tf_op jit(solution)/shard_map/ppermute | solution.py:424
  107.5 2.5 %all-to-all-done.2 = bf16[8,32,384]{2,1,0:T(8,128)(2,1)S(1)} async-done(((bf16[8,32,384]{2,1,0:T(8,128)(2,1)}), bf16[8,32,384]{2,1,0:T(8,128)(2,1)S(1)}, u32[]{:S(2)}, u32[]{:S(2)}) %all-to-all-start.2) | async-done | bytes 196640 | tf_op jit(solution)/shard_map/all_to_all | solution.py:514
  110.1 5.2 %collective-permute-done.13.lon = bf16[108,512]{1,0:T(8,128)(2,1)S(1)} collective-permute-done((bf16[108,512]{1,0:T(8,128)(2,1)S(1)}, bf16[108,512]{1,0:T(8,128)(2,1)S(1)}, u32[]{:S(2)}, u32[]{:S(2)}) %collective-permute-start.13) | collective-permute-done | bytes 110624 | tf_op jit(solution)/shard_map/ppermute | solution.py:409
  116.1 4.5 %all-to-all-start.3 = ((bf16[8,32,384]{2,1,0:T(8,128)(2,1)}), bf16[8,32,384]{2,1,0:T(8,128)(2,1)S(1)}, u32[]{:S(2)}, u32[]{:S(2)}) async-start(bf16[8,32,384]{2,1,0:T(8,128)(2,1)} %broadcast_in_dim.2), calls=%async_computation.3 | async-start | bytes 393216 | tf_op jit(solution)/shard_map/all_to_all | solution.py:520
  120.6 1.8 %shard_map.118 = (bf16[288,512]{1,0:T(8,128)(2,1)}, bf16[72,1024]{1,0:T(8,128)(2,1)S(1)}) custom-call(s32[432,11]{1,0:T(8,128)S(1)} %copy-done.1, bf16[288,512]{1,0:T(8,128)(2,1)S(1)} %copy-done.3, bf16[72,1024]{1,0:T(8,128)(2,1)S(1)} %convolution_convert_fusion.cells, bf16[120,512]{1,0:T(8,128)(2,1)S(1)} %collective-permute-done.10.grp, ...), custom_call_target="tpu_custom_call" | custom-call | tf_op jit(solution)/shard_map/pallas_call | solution.py:393
  123.2 3.1 %all-to-all-done.3.shares = bf16[8,32,384]{2,1,0:T(8,128)(2,1)S(1)} async-done(((bf16[8,32,384]{2,1,0:T(8,128)(2,1)}), bf16[8,32,384]{2,1,0:T(8,128)(2,1)S(1)}, u32[]{:S(2)}, u32[]{:S(2)}) %all-to-all-start.3) | async-done | bytes 196640 | tf_op jit(solution)/shard_map/all_to_all | solution.py:520
  (69 shorter events, 25.1 us)
Async XLA Ops:
  1.6 18.9 %copy-start.4 = (bf16[72,1024]{1,0:T(8,128)(2,1)}, bf16[72,1024]{1,0:T(8,128)(2,1)S(1)}, u32[]{:S(2)}) copy-start(bf16[72,1024]{1,0:T(8,128)(2,1)S(1)} %reshape.40.cells) | copy-start | bytes 442372
  3.1 9.2 %collective-permute-start = (bf16[120,512]{1,0:T(8,128)(2,1)S(1)}, bf16[120,512]{1,0:T(8,128)(2,1)S(1)}, u32[]{:S(2)}, u32[]{:S(2)}) collective-permute-start(bf16[120,512]{1,0:T(8,128)(2,1)S(1)} %get-tuple-element.50), channel_id=1, source_target_pairs={{0,1},{1,0},{2,3},{3,2},{4,5},{5,4},{6,7},{7,6},{8,9},{9,8},{10,11... | collective-permute-start | bytes 368648 | tf_op jit(solution)/shard_map/ppermute | solution.py:409
  5.5 5.7 %collective-permute-start.1 = (bf16[96,512]{1,0:T(8,128)(2,1)S(1)}, bf16[96,512]{1,0:T(8,128)(2,1)S(1)}, u32[]{:S(2)}, u32[]{:S(2)}) collective-permute-start(bf16[96,512]{1,0:T(8,128)(2,1)S(1)} %get-tuple-element.51), channel_id=1, source_target_pairs={{0,192},{64,0},{128,64},{192,128},{1,193},{65,1},{129,65},{193,129... | collective-permute-start | bytes 294920 | tf_op jit(solution)/shard_map/ppermute | solution.py:409
  6.8 5.5 %collective-permute-start.2 = (bf16[96,512]{1,0:T(8,128)(2,1)S(1)}, bf16[96,512]{1,0:T(8,128)(2,1)S(1)}, u32[]{:S(2)}, u32[]{:S(2)}) collective-permute-start(bf16[96,512]{1,0:T(8,128)(2,1)S(1)} %get-tuple-element.52), channel_id=1, source_target_pairs={{0,193},{1,192},{64,1},{65,0},{128,65},{129,64},{192,129},{193,128... | collective-permute-start | bytes 294920 | tf_op jit(solution)/shard_map/ppermute | solution.py:424
  11.2 9.4 %copy-start.6 = (bf16[96,512]{1,0:T(8,128)(2,1)}, bf16[96,512]{1,0:T(8,128)(2,1)S(1)}, u32[]{:S(2)}) copy-start(bf16[96,512]{1,0:T(8,128)(2,1)S(1)} %collective-permute-done.1.lat) | copy-start | bytes 294916
  12.3 8.3 %copy-start.7 = (bf16[96,512]{1,0:T(8,128)(2,1)}, bf16[96,512]{1,0:T(8,128)(2,1)S(1)}, u32[]{:S(2)}) copy-start(bf16[96,512]{1,0:T(8,128)(2,1)S(1)} %collective-permute-done.2.both) | copy-start | bytes 294916
  12.7 7.9 %collective-permute-start.3 = (bf16[108,512]{1,0:T(8,128)(2,1)S(1)}, bf16[108,512]{1,0:T(8,128)(2,1)S(1)}, u32[]{:S(2)}, u32[]{:S(2)}) collective-permute-start(bf16[108,512]{1,0:T(8,128)(2,1)S(1)} %shard_map.111), channel_id=1, source_target_pairs={{0,62},{2,0},{4,2},{6,4},{8,6},{10,8},{12,10},{14,12},{16,14},{18,... | collective-permute-start | bytes 331784 | tf_op jit(solution)/shard_map/ppermute | solution.py:409
  19.6 17.9 %copy-start = (s32[432,11]{1,0:T(8,128)S(1)}, s32[432,11]{1,0:T(8,128)}, u32[]{:S(2)}) copy-start(s32[432,11]{1,0:T(8,128)} %constant.14.clone.table) | copy-start | bytes 57028
  31.9 5.6 %collective-permute-start.4 = (bf16[48,512]{1,0:T(8,128)(2,1)}, bf16[48,512]{1,0:T(8,128)(2,1)S(1)}, u32[]{:S(2)}, u32[]{:S(2)}) collective-permute-start(bf16[48,512]{1,0:T(8,128)(2,1)} %get-tuple-element.54), channel_id=1, source_target_pairs={{0,64},{64,128},{128,192},{192,0},{1,65},{65,129},{129,193},{193,1... | collective-permute-start | bytes 147464 | tf_op jit(solution)/shard_map/ppermute | solution.py:409
  33.0 4.6 %collective-permute-start.5 = (bf16[2,72,256]{2,1,0:T(8,128)(2,1)}, bf16[2,72,256]{2,1,0:T(8,128)(2,1)S(1)}, u32[]{:S(2)}, u32[]{:S(2)}) collective-permute-start(bf16[2,72,256]{2,1,0:T(8,128)(2,1)} %get-tuple-element.57), channel_id=1, source_target_pairs={{0,2},{2,0},{1,3},{3,1},{4,6},{6,4},{5,7},{7,5},{8,10},{10,8},{9,1... | collective-permute-start | bytes 221192 | tf_op jit(solution)/shard_map/ppermute | solution.py:409
  40.6 4.1 %collective-permute-start.6 = (bf16[48,512]{1,0:T(8,128)(2,1)S(1)}, bf16[48,512]{1,0:T(8,128)(2,1)S(1)}, u32[]{:S(2)}, u32[]{:S(2)}) collective-permute-start(bf16[48,512]{1,0:T(8,128)(2,1)S(1)} %get-tuple-element.60), channel_id=1, source_target_pairs={{0,192},{64,0},{128,64},{192,128},{1,193},{65,1},{129,65},{193,129... | collective-permute-start | bytes 147464 | tf_op jit(solution)/shard_map/ppermute | solution.py:409
  44.7 21.6 %all-to-all-start = ((bf16[8,4,72,256]{3,2,1,0:T(8,128)(2,1)}), bf16[8,4,72,256]{3,2,1,0:T(8,128)(2,1)S(1)}, u32[]{:S(2)}, u32[]{:S(2)}) async-start(bf16[8,4,72,256]{3,2,1,0:T(8,128)(2,1)} %get-tuple-element.72), calls=%async_computation | async-start | bytes 2359296 | tf_op jit(solution)/shard_map/all_to_all | solution.py:481
  50.5 12.4 %copy-start.11 = (bf16[2048,1024]{1,0:T(8,128)(2,1)S(1)}, bf16[2048,1024]{1,0:T(8,128)(2,1)}, u32[]{:S(2)}) copy-start(bf16[2048,1024]{1,0:T(8,128)(2,1)} %param.11) | copy-start | bytes 12582916
  50.5 13.3 %copy-start.1 = (s32[432,11]{1,0:T(8,128)S(1)}, s32[432,11]{1,0:T(8,128)}, u32[]{:S(2)}) copy-start(s32[432,11]{1,0:T(8,128)} %constant.14.clone.table) | copy-start | bytes 57028
  66.3 2.9 %collective-permute-start.7 = (bf16[2,4,2,8,32,128]{5,4,3,2,1,0:T(8,128)(2,1)}, bf16[2,4,2,8,32,128]{5,4,3,2,1,0:T(8,128)(2,1)S(1)}, u32[]{:S(2)}, u32[]{:S(2)}) collective-permute-start(bf16[2,4,2,8,32,128]{5,4,3,2,1,0:T(8,128)(2,1)} %get-tuple-element.77), channel_id=1, source_target_pairs={{0,2},{2,0},{1,3},{3,1},{4,6},{6,4},{5,7},{7,5},{8,10},{10,8},{9,1... | collective-permute-start | bytes 3145736 | tf_op jit(solution)/shard_map/ppermute | solution.py:409
  70.5 23.4 %all-to-all-start.1 = ((bf16[16,8,32,128]{3,2,1,0:T(8,128)(2,1)}), bf16[16,8,32,128]{3,2,1,0:T(8,128)(2,1)}, u32[]{:S(2)}, u32[]{:S(2)}) async-start(bf16[16,8,32,128]{3,2,1,0:T(8,128)(2,1)} %bitcast.3), calls=%async_computation.1 | async-start | bytes 2097152 | tf_op jit(solution)/shard_map/all_to_all | solution.py:443
  76.6 2.2 %collective-permute-start.8 = (bf16[8,2,72,256]{3,2,1,0:T(8,128)(2,1)}, bf16[8,2,72,256]{3,2,1,0:T(8,128)(2,1)S(1)}, u32[]{:S(2)}, u32[]{:S(2)}) collective-permute-start(bf16[8,2,72,256]{3,2,1,0:T(8,128)(2,1)} %slice.3), channel_id=1, source_target_pairs={{0,2},{2,0},{1,3},{3,1},{4,6},{6,4},{5,7},{7,5},{8,10},{10,8},{9,1... | collective-permute-start | bytes 1769480 | tf_op jit(solution)/shard_map/ppermute | solution.py:409
  80.1 15.2 %collective-permute-start.9 = (bf16[256,256]{1,0:T(8,128)(2,1)S(1)}, bf16[256,256]{1,0:T(8,128)(2,1)S(1)}, u32[]{:S(2)}, u32[]{:S(2)}) collective-permute-start(bf16[256,256]{1,0:T(8,128)(2,1)S(1)} %get-tuple-element.79), channel_id=1, source_target_pairs={{0,32},{32,0},{1,33},{33,1},{2,34},{34,2},{3,35},{35,3},{4,36},{36... | collective-permute-start | bytes 393224 | tf_op jit(solution)/shard_map/ppermute | solution.py:409
  82.3 13.0 %collective-permute-start.10 = (bf16[120,512]{1,0:T(8,128)(2,1)S(1)}, bf16[120,512]{1,0:T(8,128)(2,1)S(1)}, u32[]{:S(2)}, u32[]{:S(2)}) collective-permute-start(bf16[120,512]{1,0:T(8,128)(2,1)S(1)} %get-tuple-element.80), channel_id=1, source_target_pairs={{0,1},{1,0},{2,3},{3,2},{4,5},{5,4},{6,7},{7,6},{8,9},{9,8},{10,11... | collective-permute-start | bytes 368648 | tf_op jit(solution)/shard_map/ppermute | solution.py:409
  83.8 11.5 %collective-permute-start.11 = (bf16[96,512]{1,0:T(8,128)(2,1)S(1)}, bf16[96,512]{1,0:T(8,128)(2,1)S(1)}, u32[]{:S(2)}, u32[]{:S(2)}) collective-permute-start(bf16[96,512]{1,0:T(8,128)(2,1)S(1)} %get-tuple-element.81), channel_id=1, source_target_pairs={{0,64},{64,128},{128,192},{192,0},{1,65},{65,129},{129,193},{193,1... | collective-permute-start | bytes 294920 | tf_op jit(solution)/shard_map/ppermute | solution.py:409
  96.0 14.0 %all-to-all-start.2 = ((bf16[8,32,384]{2,1,0:T(8,128)(2,1)}), bf16[8,32,384]{2,1,0:T(8,128)(2,1)S(1)}, u32[]{:S(2)}, u32[]{:S(2)}) async-start(bf16[8,32,384]{2,1,0:T(8,128)(2,1)} %pad_maximum_fusion), calls=%async_computation.2 | async-start | bytes 393216 | tf_op jit(solution)/shard_map/all_to_all | solution.py:514
  100.3 6.7 %collective-permute-start.12 = (bf16[96,512]{1,0:T(8,128)(2,1)S(1)}, bf16[96,512]{1,0:T(8,128)(2,1)S(1)}, u32[]{:S(2)}, u32[]{:S(2)}) collective-permute-start(bf16[96,512]{1,0:T(8,128)(2,1)S(1)} %get-tuple-element.84), channel_id=1, source_target_pairs={{0,65},{1,64},{64,129},{65,128},{128,193},{129,192},{192,1},{193,0... | collective-permute-start | bytes 294920 | tf_op jit(solution)/shard_map/ppermute | solution.py:424
  107.5 7.9 %collective-permute-start.13 = (bf16[108,512]{1,0:T(8,128)(2,1)S(1)}, bf16[108,512]{1,0:T(8,128)(2,1)S(1)}, u32[]{:S(2)}, u32[]{:S(2)}) collective-permute-start(bf16[108,512]{1,0:T(8,128)(2,1)S(1)} %shard_map.117), channel_id=1, source_target_pairs={{0,2},{2,4},{4,6},{6,8},{8,10},{10,12},{12,14},{14,16},{16,18},{18... | collective-permute-start | bytes 331784 | tf_op jit(solution)/shard_map/ppermute | solution.py:409
  116.1 10.3 %all-to-all-start.3 = ((bf16[8,32,384]{2,1,0:T(8,128)(2,1)}), bf16[8,32,384]{2,1,0:T(8,128)(2,1)S(1)}, u32[]{:S(2)}, u32[]{:S(2)}) async-start(bf16[8,32,384]{2,1,0:T(8,128)(2,1)} %broadcast_in_dim.2), calls=%async_computation.3 | async-start | bytes 393216 | tf_op jit(solution)/shard_map/all_to_all | solution.py:520
  (9 other events, 34.9 us)

commit v6 on v2

--- a/solution.py
+++ b/solution.py
@@ -102,10 +102,13 @@
 
 
 def gather(table, column, sources):
-    names = table[: ROWS[column], column : column + 1]
+    return gather_named(table[: ROWS[column], column : column + 1], sources)
+
+
+def gather_named(names, sources):
     total = 0.0
     for source, value in sources.items():
-        place = lax.broadcasted_iota(jnp.int32, (ROWS[column], value.shape[0]), 1) + 1000 * source
+        place = lax.broadcasted_iota(jnp.int32, (names.shape[0], value.shape[0]), 1) + 1000 * source
         total += dot_nn((names == place).astype(WIDE).astype(LOW), value)
     return total
 
@@ -147,12 +150,27 @@
     both[...] = packed[216:].astype(LOW)
 
 
-def planes_in_kernel(table, tokens, cells, *outs):
-    store_planes(gather(table, IN_FIRST, own(tokens, cells)), *outs)
-
-
-def columns_in_kernel(table, tokens, cells, grp, lat, both, out):
-    out[...] = gather(table, IN_SECOND, own(tokens, cells) | arrivals(grp, lat, both)).astype(LOW)
+def runs(target):
+    target = np.asarray(target)
+    begins = [0] + [at for at in range(1, len(target)) if target[at] != target[at - 1] + 1]
+    return [(at, int(target[at]) - at) for at in begins]
+
+
+def column_names(column):
+    row = lax.broadcasted_iota(jnp.int32, (ROWS[column], 1), 0)
+    ahead = jnp.zeros_like(row)
+    for begin, difference in runs(TABLE[: ROWS[column], column]):
+        ahead = jnp.where(row >= begin, difference, ahead)
+    return row + ahead
+
+
+def planes_in_kernel(tokens, cells, *outs):
+    store_planes(gather_named(column_names(IN_FIRST), own(tokens, cells)), *outs)
+
+
+def columns_in_kernel(tokens, cells, grp, lat, both, out):
+    sources = own(tokens, cells) | arrivals(grp, lat, both)
+    out[...] = gather_named(column_names(IN_SECOND), sources).astype(LOW)
 
 
 def columns_out_kernel(table, tokens, cells, out):
@@ -345,6 +363,25 @@
                 merging_grads[16 * g : 16 * g + 16, at : at + 256] = part.astype(WIDE)
 
 
+def planes_kernel(parts, kept, came, planes):
+    total = parts[0].astype(WIDE)
+    for k in range(1, 16):
+        total += parts[k].astype(WIDE)
+    planes[:, :, :128] = total.astype(LOW)
+    for k in range(8):
+        rows = slice(32 * k, 32 * k + 32)
+        planes[k, :, 128:] = (kept[rows].astype(WIDE) + came[rows].astype(WIDE)).astype(LOW)
+
+
+def share_kernel(parts, copies):
+    total = parts[0].astype(WIDE)
+    for k in range(1, 8):
+        total += parts[k].astype(WIDE)
+    total = total.astype(LOW)
+    for k in range(8):
+        copies[k] = total
+
+
 def call(kernel, outs, *operands, scratch=(), scalars=0, room=8, far=(), far_outs=()):
     specs = [pl.BlockSpec()] * len(operands)
     for at in range(scalars):
@@ -391,18 +428,14 @@
 
 
 def shift_forward(table, tokens, cells):
-    parts = to_neighbours(call(planes_in_kernel, PLANES, table, tokens, cells), -1)
-    (columns,) = call(columns_in_kernel, [(108, 512)], table, tokens, cells, *parts)
+    parts = to_neighbours(call(planes_in_kernel, PLANES, tokens, cells), -1)
+    (columns,) = call(columns_in_kernel, [(108, 512)], tokens, cells, *parts)
     return (*parts, from_behind(columns, LON, -1))
-
-
-def wide_sum(parts):
-    return jnp.sum(parts.astype(WIDE), axis=0).astype(LOW)
 
 
 def over_planes(terms):
     terms = terms.reshape((16,) + terms.shape[3:])
-    return wide_sum(lax.all_to_all(terms, ("xh", "lat", "grp"), 0, 0))
+    return lax.all_to_all(terms, ("xh", "lat", "grp"), 0, 0)
 
 
 def tied(*values):
@@ -469,11 +502,10 @@
     parts_out = call(planes_out_kernel, PLANES, table, token_grads, coarse_field, lon_out)
     block_planes, merging_came, *parts_out = tied(block_planes, merging_came, *parts_out)
     parts_out = to_neighbours(parts_out, 1)
-    merging_planes = (merging_kept.astype(WIDE) + merging_came.astype(WIDE)).astype(LOW).reshape(8, 32, 256)
-    planes = jnp.concatenate([block_planes, merging_planes], axis=2)
-    share = wide_sum(lax.all_to_all(planes, ("z",), 0, 0))
+    (planes,) = call(planes_kernel, [(8, 32, 384)], block_planes, merging_kept, merging_came)
+    (share,) = call(share_kernel, [(8, 32, 384)], lax.all_to_all(planes, ("z",), 0, 0))
     share, *parts_out = tied(share, *parts_out)
-    shares = lax.all_to_all(jnp.broadcast_to(share[None], (8, 32, 384)), ("lat", "grp"), 0, 0)
+    shares = lax.all_to_all(share, ("lat", "grp"), 0, 0)
     token_grads, coarse_field = call(
         all_out_kernel, [(288, 512), (72, 1024)], table, token_grads, coarse_field, *parts_out, lon_out
     )

time: 125 us -> 123 us (0.984)
  waiting for transfers between devices: 37.6 us -> 35.2 us
  starting transfers between devices: 37.6 us -> 39.8 us
  other arithmetic: 3.42 us -> 1.32 us
  Pallas kernels: 31.3 us -> 32.7 us
    all_to_all x3, waiting for transfers between devices: 14.6 us -> 8.97 us  [the longest x1 5.18 us: body(): lax.all_to_all(planes, ('z',), 0, 0)]
    ppermute x12, waiting for transfers between devices: 19.2 us -> 22.5 us  [from_behind(): return lax.ppermute(value, axis, pairs)]
    pallas_call x10 -> x12, Pallas kernels: 31.3 us -> 32.7 us  [call(): pl.pallas_call(kernel, in_specs=specs, out_specs=out_specs, out_shape=[ja...]
    reduce_sum x2 -> x0, other arithmetic: 1.41 us -> none  [wide_sum(): return jnp.sum(parts.astype(WIDE), axis=0).astype(LOW)]
    unnamed x34 -> x36, local copies, waits for them, and re-layouts: 5.09 us -> 5.08 us
  transfers between devices with their start and end apart: 18 -> 18, of which waited for: 12 -> 13; matrix products, arithmetic and copies ran while one was open for 7% -> 7% of each run, Pallas kernels for 13% -> 14%
where the time goes in v6:
time: 123 us
  starting transfers between devices  39.8 us (32%)
  waiting for transfers between devices  35.2 us (29%)
  Pallas kernels  32.7 us (27%)
  local copies, waits for them, and re-layouts  8.24 us (7%)
  matrix products  4.54 us (4%)
  other arithmetic  1.32 us (1%)
    pallas_call x12, Pallas kernels, call(): pl.pallas_call(kernel, in_specs=specs, out_specs=out_specs, out_shape=[ja...  32.7 us
    ppermute x12, waiting for transfers between devices, from_behind(): return lax.ppermute(value, axis, pairs)  22.5 us
    ppermute x12, starting transfers between devices, from_behind(): return lax.ppermute(value, axis, pairs)  16.3 us
    all_to_all x1, starting transfers between devices, body(): shares = lax.all_to_all(share, ('lat', 'grp'), 0, 0)  5.98 us
    all_to_all x1, starting transfers between devices, body(): bundle = lax.all_to_all(bundle, ('lat', 'grp'), 0, 0)  5.77 us
    all_to_all x1, waiting for transfers between devices, body(): lax.all_to_all(planes, ('z',), 0, 0)  5.18 us
    unnamed x36, local copies, waits for them, and re-layouts  5.08 us
    all_to_all x1, starting transfers between devices, over_planes(): return lax.all_to_all(terms, ('xh', 'lat', 'grp'), 0, 0)  4.61 us
  transfers between devices with their start and end apart: 18, of which 13 were waited for; matrix products, arithmetic and copies ran while one was open for 7% of the time, Pallas kernels for 14%

profile of v6, /device:TPU:2, one launch (start us, length us, event | category | flops | bytes accessed | tf_op | source)
XLA Modules:
  0.0 122.7 jit_solution(8597275601242757294)
XLA Ops:
  3.1 2.4 %collective-permute-start = (bf16[120,512]{1,0:T(8,128)(2,1)S(1)}, bf16[120,512]{1,0:T(8,128)(2,1)S(1)}, u32[]{:S(2)}, u32[]{:S(2)}) collective-permute-start(bf16[120,512]{1,0:T(8,128)(2,1)S(1)} %get-tuple-element.51), channel_id=1, source_target_pairs={{0,1},{1,0},{2,3},{3,2},{4,5},{5,4},{6,7},{7,6},{8,9},{9,8},{10,11... | collective-permute-start | bytes 368648 | tf_op jit(solution)/shard_map/ppermute | solution.py:408
  6.8 1.7 %collective-permute-start.2 = (bf16[96,512]{1,0:T(8,128)(2,1)S(1)}, bf16[96,512]{1,0:T(8,128)(2,1)S(1)}, u32[]{:S(2)}, u32[]{:S(2)}) collective-permute-start(bf16[96,512]{1,0:T(8,128)(2,1)S(1)} %get-tuple-element.53), channel_id=1, source_target_pairs={{0,193},{1,192},{64,1},{65,0},{128,65},{129,64},{192,129},{193,128... | collective-permute-start | bytes 294920 | tf_op jit(solution)/shard_map/ppermute | solution.py:423
  8.4 2.7 %collective-permute-done.1.lat = bf16[96,512]{1,0:T(8,128)(2,1)S(1)} collective-permute-done((bf16[96,512]{1,0:T(8,128)(2,1)S(1)}, bf16[96,512]{1,0:T(8,128)(2,1)S(1)}, u32[]{:S(2)}, u32[]{:S(2)}) %collective-permute-start.1) | collective-permute-done | bytes 98336 | tf_op jit(solution)/shard_map/ppermute | solution.py:408
  12.7 5.5 %collective-permute-start.3 = (bf16[108,512]{1,0:T(8,128)(2,1)S(1)}, bf16[108,512]{1,0:T(8,128)(2,1)S(1)}, u32[]{:S(2)}, u32[]{:S(2)}) collective-permute-start(bf16[108,512]{1,0:T(8,128)(2,1)S(1)} %shard_map.111), channel_id=1, source_target_pairs={{0,62},{2,0},{4,2},{6,4},{8,6},{10,8},{12,10},{14,12},{16,14},{18,... | collective-permute-start | bytes 331784 | tf_op jit(solution)/shard_map/ppermute | solution.py:408
  21.2 11.1 %shard_map.112 = (bf16[288,512]{1,0:T(8,128)(2,1)}, bf16[48,512]{1,0:T(8,128)(2,1)}, bf16[288,512]{1,0:T(8,128)(2,1)}, bf16[288,1536]{1,0:T(8,128)(2,1)}, bf16[2...) custom-call(s32[1]{0:T(128)} %bitcast.core, ...), custom_call_target="tpu_custom_call" | custom-call | tf_op jit(solution)/shard_map/pallas_call | solution.py:392
  33.3 3.7 %fusion.upstream = f32[72,2048]{1,0:T(8,128)S(1)} fusion(bf16[72,1024]{1,0:T(8,128)(2,1)} %get-tuple-element.56, bf16[2048,1024]{1,0:T(8,128)(2,1)} %param.11), kind=kOutput, calls=%fused_computation.3 | convolution fusion | flops 301989888 | bytes 4931584 | tf_op jit(solution)/shard_map/dot_general | solution.py:121
  37.9 2.2 %shard_map.113 = (bf16[72,2048]{1,0:T(8,128)(2,1)S(1)}, bf16[8,4,72,256]{3,2,1,0:T(8,128)(2,1)}, bf16[288,512]{1,0:T(8,128)(2,1)S(1)}, bf16[48,512]{1,0:T(8,128)(2,1)S(1)}) custom-call(s32[432,11]{1,0:T(8,128)S(1)} %copy-done, bf16[288,512]{1,0:T(8,128)(2,1)S(1)} %copy-done.9, bf16[48,512]{1,0:T(8,128)(2,1)S(1)} %collective-permute-done.4.prior, ...), custom_call_target="tpu_custom_call" | custom-call | tf_op jit(solution)/shard_map/pallas_call | solution.py:392
  42.3 2.7 %collective-permute-done.6.next_row = bf16[48,512]{1,0:T(8,128)(2,1)S(1)} collective-permute-done((bf16[48,512]{1,0:T(8,128)(2,1)S(1)}, bf16[48,512]{1,0:T(8,128)(2,1)S(1)}, u32[]{:S(2)}, u32[]{:S(2)}) %collective-permute-start.6) | collective-permute-done | bytes 49184 | tf_op jit(solution)/shard_map/ppermute | solution.py:408
  45.0 5.8 %all-to-all-start = ((bf16[8,4,72,256]{3,2,1,0:T(8,128)(2,1)}), bf16[8,4,72,256]{3,2,1,0:T(8,128)(2,1)S(1)}, u32[]{:S(2)}, u32[]{:S(2)}) async-start(bf16[8,4,72,256]{3,2,1,0:T(8,128)(2,1)} %get-tuple-element.72), calls=%async_computation | async-start | bytes 2359296 | tf_op jit(solution)/shard_map/all_to_all | solution.py:475
  50.7 12.3 %shard_map.114 = (bf16[288,512]{1,0:T(8,128)(2,1)}, bf16[2,4,2,8,32,128]{5,4,3,2,1,0:T(8,128)(2,1)}, bf16[2,4,2,8,32,128]{5,4,3,2,1,0:T(8,128)(2,1)}) custom-call(s32[1]{0:T(128)} %bitcast.core, s32[432,11]{1,0:T(8,128)} %constant.10.clone.table, bf16[288,512]{1,0:T(8,128)(2,1)} %copy-done.8, bf16[48,512]{1,0:T(8,128)(2,1)} %copy-done.16, ...), custom_call_target="tpu_custom_call" | custom-call | tf_op jit(solution)/shard_map/pallas_call | solution.py:392
  63.9 2.7 %all-to-all-done.bundle = bf16[8,4,72,256]{3,2,1,0:T(8,128)(2,1)S(1)} async-done(((bf16[8,4,72,256]{3,2,1,0:T(8,128)(2,1)}), bf16[8,4,72,256]{3,2,1,0:T(8,128)(2,1)S(1)}, u32[]{:S(2)}, u32[]{:S(2)}) %all-to-all-start) | async-done | bytes 1179680 | tf_op jit(solution)/shard_map/all_to_all | solution.py:475
  66.6 2.9 %collective-permute-done.7 = bf16[2,4,2,8,32,128]{5,4,3,2,1,0:T(8,128)(2,1)S(1)} collective-permute-done((bf16[2,4,2,8,32,128]{5,4,3,2,1,0:T(8,128)(2,1)}, bf16[2,4,2,8,32,128]{5,4,3,2,1,0:T(8,128)(2,1)S(1)}, u32[]{:S(2)}, u32[]{:S(2)}) %collective-permute-start.7) | collective-permute-done | bytes 1048608 | tf_op jit(solution)/shard_map/ppermute | solution.py:408
  70.7 4.6 %all-to-all-start.1 = ((bf16[16,8,32,128]{3,2,1,0:T(8,128)(2,1)}), bf16[16,8,32,128]{3,2,1,0:T(8,128)(2,1)S(1)}, u32[]{:S(2)}, u32[]{:S(2)}) async-start(bf16[16,8,32,128]{3,2,1,0:T(8,128)(2,1)} %bitcast.20), calls=%async_computation.1 | async-start | bytes 2097152 | tf_op jit(solution)/shard_map/all_to_all | solution.py:438
  76.2 2.2 %collective-permute-done.8.other_normed = bf16[8,2,72,256]{3,2,1,0:T(8,128)(2,1)S(1)} collective-permute-done((bf16[8,2,72,256]{3,2,1,0:T(8,128)(2,1)}, bf16[8,2,72,256]{3,2,1,0:T(8,128)(2,1)S(1)}, u32[]{:S(2)}, u32[]{:S(2)}) %collective-permute-start.8) | collective-permute-done | bytes 589856 | tf_op jit(solution)/shard_map/ppermute | solution.py:408
  79.8 2.2 %collective-permute-start.9 = (bf16[256,256]{1,0:T(8,128)(2,1)S(1)}, bf16[256,256]{1,0:T(8,128)(2,1)S(1)}, u32[]{:S(2)}, u32[]{:S(2)}) collective-permute-start(bf16[256,256]{1,0:T(8,128)(2,1)S(1)} %get-tuple-element.78), channel_id=1, source_target_pairs={{0,32},{32,0},{1,33},{33,1},{2,34},{34,2},{3,35},{35,3},{4,36},{36... | collective-permute-start | bytes 393224 | tf_op jit(solution)/shard_map/ppermute | solution.py:408
  82.4 7.9 %collective-permute-done.10.lon = bf16[108,512]{1,0:T(8,128)(2,1)S(1)} collective-permute-done((bf16[108,512]{1,0:T(8,128)(2,1)S(1)}, bf16[108,512]{1,0:T(8,128)(2,1)S(1)}, u32[]{:S(2)}, u32[]{:S(2)}) %collective-permute-start.10) | collective-permute-done | bytes 110624 | tf_op jit(solution)/shard_map/ppermute | solution.py:408
  91.0 3.0 %collective-permute-done.9.came = bf16[256,256]{1,0:T(8,128)(2,1)S(1)} collective-permute-done((bf16[256,256]{1,0:T(8,128)(2,1)S(1)}, bf16[256,256]{1,0:T(8,128)(2,1)S(1)}, u32[]{:S(2)}, u32[]{:S(2)}) %collective-permute-start.9) | collective-permute-done | bytes 131104 | tf_op jit(solution)/shard_map/ppermute | solution.py:408
  96.4 3.4 %all-to-all-start.2 = ((bf16[8,32,384]{2,1,0:T(8,128)(2,1)}), bf16[8,32,384]{2,1,0:T(8,128)(2,1)S(1)}, u32[]{:S(2)}, u32[]{:S(2)}) async-start(bf16[8,32,384]{2,1,0:T(8,128)(2,1)} %shard_map.118), calls=%async_computation.2 | async-start | bytes 393216 | tf_op jit(solution)/shard_map/all_to_all | solution.py:506
  99.8 1.5 %collective-permute-start.11 = (bf16[120,512]{1,0:T(8,128)(2,1)S(1)}, bf16[120,512]{1,0:T(8,128)(2,1)S(1)}, u32[]{:S(2)}, u32[]{:S(2)}) collective-permute-start(bf16[120,512]{1,0:T(8,128)(2,1)S(1)} %get-tuple-element.85), channel_id=1, source_target_pairs={{0,1},{1,0},{2,3},{3,2},{4,5},{5,4},{6,7},{7,6},{8,9},{9,8},{10,11... | collective-permute-start | bytes 368648 | tf_op jit(solution)/shard_map/ppermute | solution.py:408
  102.2 2.2 %collective-permute-start.13 = (bf16[96,512]{1,0:T(8,128)(2,1)S(1)}, bf16[96,512]{1,0:T(8,128)(2,1)S(1)}, u32[]{:S(2)}, u32[]{:S(2)}) collective-permute-start(bf16[96,512]{1,0:T(8,128)(2,1)S(1)} %get-tuple-element.87), channel_id=1, source_target_pairs={{0,65},{1,64},{64,129},{65,128},{128,193},{129,192},{192,1},{193,0... | collective-permute-start | bytes 294920 | tf_op jit(solution)/shard_map/ppermute | solution.py:423
  104.3 5.2 %all-to-all-done.2.parts = bf16[8,32,384]{2,1,0:T(8,128)(2,1)S(1)} async-done(((bf16[8,32,384]{2,1,0:T(8,128)(2,1)}), bf16[8,32,384]{2,1,0:T(8,128)(2,1)S(1)}, u32[]{:S(2)}, u32[]{:S(2)}) %all-to-all-start.2) | async-done | bytes 196640 | tf_op jit(solution)/shard_map/all_to_all | solution.py:506
  110.2 6.0 %all-to-all-start.3 = ((bf16[8,32,384]{2,1,0:T(8,128)(2,1)}), bf16[8,32,384]{2,1,0:T(8,128)(2,1)S(1)}, u32[]{:S(2)}, u32[]{:S(2)}) async-start(bf16[8,32,384]{2,1,0:T(8,128)(2,1)} %shard_map.119), calls=%async_computation.3 | async-start | bytes 393216 | tf_op jit(solution)/shard_map/all_to_all | solution.py:508
  116.2 1.8 %shard_map.120 = (bf16[288,512]{1,0:T(8,128)(2,1)}, bf16[72,1024]{1,0:T(8,128)(2,1)S(1)}) custom-call(s32[432,11]{1,0:T(8,128)S(1)} %copy-done.1, bf16[288,512]{1,0:T(8,128)(2,1)S(1)} %copy-done.3, bf16[72,1024]{1,0:T(8,128)(2,1)S(1)} %convolution_convert_fusion.cells, bf16[120,512]{1,0:T(8,128)(2,1)S(1)} %collective-permute-done.11.grp, ...), custom_call_target="tpu_custom_call" | custom-call | tf_op jit(solution)/shard_map/pallas_call | solution.py:392
  118.8 3.1 %all-to-all-done.3.shares = bf16[8,32,384]{2,1,0:T(8,128)(2,1)S(1)} async-done(((bf16[8,32,384]{2,1,0:T(8,128)(2,1)}), bf16[8,32,384]{2,1,0:T(8,128)(2,1)S(1)}, u32[]{:S(2)}, u32[]{:S(2)}) %all-to-all-start.3) | async-done | bytes 196640 | tf_op jit(solution)/shard_map/all_to_all | solution.py:508
  (70 shorter events, 23.3 us)
Async XLA Ops:
  1.6 18.9 %copy-start.4 = (bf16[72,1024]{1,0:T(8,128)(2,1)}, bf16[72,1024]{1,0:T(8,128)(2,1)S(1)}, u32[]{:S(2)}) copy-start(bf16[72,1024]{1,0:T(8,128)(2,1)S(1)} %reshape.36.cells) | copy-start | bytes 442372
  3.1 9.2 %collective-permute-start = (bf16[120,512]{1,0:T(8,128)(2,1)S(1)}, bf16[120,512]{1,0:T(8,128)(2,1)S(1)}, u32[]{:S(2)}, u32[]{:S(2)}) collective-permute-start(bf16[120,512]{1,0:T(8,128)(2,1)S(1)} %get-tuple-element.51), channel_id=1, source_target_pairs={{0,1},{1,0},{2,3},{3,2},{4,5},{5,4},{6,7},{7,6},{8,9},{9,8},{10,11... | collective-permute-start | bytes 368648 | tf_op jit(solution)/shard_map/ppermute | solution.py:408
  5.5 5.7 %collective-permute-start.1 = (bf16[96,512]{1,0:T(8,128)(2,1)S(1)}, bf16[96,512]{1,0:T(8,128)(2,1)S(1)}, u32[]{:S(2)}, u32[]{:S(2)}) collective-permute-start(bf16[96,512]{1,0:T(8,128)(2,1)S(1)} %get-tuple-element.52), channel_id=1, source_target_pairs={{0,192},{64,0},{128,64},{192,128},{1,193},{65,1},{129,65},{193,129... | collective-permute-start | bytes 294920 | tf_op jit(solution)/shard_map/ppermute | solution.py:408
  6.8 5.5 %collective-permute-start.2 = (bf16[96,512]{1,0:T(8,128)(2,1)S(1)}, bf16[96,512]{1,0:T(8,128)(2,1)S(1)}, u32[]{:S(2)}, u32[]{:S(2)}) collective-permute-start(bf16[96,512]{1,0:T(8,128)(2,1)S(1)} %get-tuple-element.53), channel_id=1, source_target_pairs={{0,193},{1,192},{64,1},{65,0},{128,65},{129,64},{192,129},{193,128... | collective-permute-start | bytes 294920 | tf_op jit(solution)/shard_map/ppermute | solution.py:423
  12.7 7.9 %collective-permute-start.3 = (bf16[108,512]{1,0:T(8,128)(2,1)S(1)}, bf16[108,512]{1,0:T(8,128)(2,1)S(1)}, u32[]{:S(2)}, u32[]{:S(2)}) collective-permute-start(bf16[108,512]{1,0:T(8,128)(2,1)S(1)} %shard_map.111), channel_id=1, source_target_pairs={{0,62},{2,0},{4,2},{6,4},{8,6},{10,8},{12,10},{14,12},{16,14},{18,... | collective-permute-start | bytes 331784 | tf_op jit(solution)/shard_map/ppermute | solution.py:408
  19.6 18.3 %copy-start = (s32[432,11]{1,0:T(8,128)S(1)}, s32[432,11]{1,0:T(8,128)}, u32[]{:S(2)}) copy-start(s32[432,11]{1,0:T(8,128)} %constant.10.clone.table) | copy-start | bytes 57028
  32.3 5.6 %collective-permute-start.4 = (bf16[48,512]{1,0:T(8,128)(2,1)}, bf16[48,512]{1,0:T(8,128)(2,1)S(1)}, u32[]{:S(2)}, u32[]{:S(2)}) collective-permute-start(bf16[48,512]{1,0:T(8,128)(2,1)} %get-tuple-element.55), channel_id=1, source_target_pairs={{0,64},{64,128},{128,192},{192,0},{1,65},{65,129},{129,193},{193,1... | collective-permute-start | bytes 147464 | tf_op jit(solution)/shard_map/ppermute | solution.py:408
  33.3 4.6 %collective-permute-start.5 = (bf16[2,72,256]{2,1,0:T(8,128)(2,1)}, bf16[2,72,256]{2,1,0:T(8,128)(2,1)S(1)}, u32[]{:S(2)}, u32[]{:S(2)}) collective-permute-start(bf16[2,72,256]{2,1,0:T(8,128)(2,1)} %get-tuple-element.58), channel_id=1, source_target_pairs={{0,2},{2,0},{1,3},{3,1},{4,6},{6,4},{5,7},{7,5},{8,10},{10,8},{9,1... | collective-permute-start | bytes 221192 | tf_op jit(solution)/shard_map/ppermute | solution.py:408
  40.9 4.1 %collective-permute-start.6 = (bf16[48,512]{1,0:T(8,128)(2,1)S(1)}, bf16[48,512]{1,0:T(8,128)(2,1)S(1)}, u32[]{:S(2)}, u32[]{:S(2)}) collective-permute-start(bf16[48,512]{1,0:T(8,128)(2,1)S(1)} %get-tuple-element.61), channel_id=1, source_target_pairs={{0,192},{64,0},{128,64},{192,128},{1,193},{65,1},{129,65},{193,129... | collective-permute-start | bytes 147464 | tf_op jit(solution)/shard_map/ppermute | solution.py:408
  45.0 21.6 %all-to-all-start = ((bf16[8,4,72,256]{3,2,1,0:T(8,128)(2,1)}), bf16[8,4,72,256]{3,2,1,0:T(8,128)(2,1)S(1)}, u32[]{:S(2)}, u32[]{:S(2)}) async-start(bf16[8,4,72,256]{3,2,1,0:T(8,128)(2,1)} %get-tuple-element.72), calls=%async_computation | async-start | bytes 2359296 | tf_op jit(solution)/shard_map/all_to_all | solution.py:475
  50.7 12.3 %copy-start.13 = (bf16[2048,1024]{1,0:T(8,128)(2,1)S(1)}, bf16[2048,1024]{1,0:T(8,128)(2,1)}, u32[]{:S(2)}) copy-start(bf16[2048,1024]{1,0:T(8,128)(2,1)} %param.11) | copy-start | bytes 12582916
  63.9 18.1 %copy-start.1 = (s32[432,11]{1,0:T(8,128)S(1)}, s32[432,11]{1,0:T(8,128)}, u32[]{:S(2)}) copy-start(s32[432,11]{1,0:T(8,128)} %constant.10.clone.table) | copy-start | bytes 57028
  63.9 18.1 %copy-start.3 = (bf16[288,512]{1,0:T(8,128)(2,1)S(1)}, bf16[288,512]{1,0:T(8,128)(2,1)}, u32[]{:S(2)}) copy-start(bf16[288,512]{1,0:T(8,128)(2,1)} %get-tuple-element.69.tokens) | copy-start | bytes 884740
  66.6 2.9 %collective-permute-start.7 = (bf16[2,4,2,8,32,128]{5,4,3,2,1,0:T(8,128)(2,1)}, bf16[2,4,2,8,32,128]{5,4,3,2,1,0:T(8,128)(2,1)S(1)}, u32[]{:S(2)}, u32[]{:S(2)}) collective-permute-start(bf16[2,4,2,8,32,128]{5,4,3,2,1,0:T(8,128)(2,1)} %get-tuple-element.76), channel_id=1, source_target_pairs={{0,2},{2,0},{1,3},{3,1},{4,6},{6,4},{5,7},{7,5},{8,10},{10,8},{9,1... | collective-permute-start | bytes 3145736 | tf_op jit(solution)/shard_map/ppermute | solution.py:408
  70.7 23.9 %all-to-all-start.1 = ((bf16[16,8,32,128]{3,2,1,0:T(8,128)(2,1)}), bf16[16,8,32,128]{3,2,1,0:T(8,128)(2,1)S(1)}, u32[]{:S(2)}, u32[]{:S(2)}) async-start(bf16[16,8,32,128]{3,2,1,0:T(8,128)(2,1)} %bitcast.20), calls=%async_computation.1 | async-start | bytes 2097152 | tf_op jit(solution)/shard_map/all_to_all | solution.py:438
  76.2 2.2 %collective-permute-start.8 = (bf16[8,2,72,256]{3,2,1,0:T(8,128)(2,1)}, bf16[8,2,72,256]{3,2,1,0:T(8,128)(2,1)S(1)}, u32[]{:S(2)}, u32[]{:S(2)}) collective-permute-start(bf16[8,2,72,256]{3,2,1,0:T(8,128)(2,1)} %slice.3), channel_id=1, source_target_pairs={{0,2},{2,0},{1,3},{3,1},{4,6},{6,4},{5,7},{7,5},{8,10},{10,8},{9,1... | collective-permute-start | bytes 1769480 | tf_op jit(solution)/shard_map/ppermute | solution.py:408
  79.7 11.2 %copy-start.10 = (bf16[256,256]{1,0:T(8,128)(2,1)}, bf16[256,256]{1,0:T(8,128)(2,1)S(1)}, u32[]{:S(2)}) copy-start(bf16[256,256]{1,0:T(8,128)(2,1)S(1)} %get-tuple-element.83.kept) | copy-start | bytes 393220
  79.8 14.2 %collective-permute-start.9 = (bf16[256,256]{1,0:T(8,128)(2,1)S(1)}, bf16[256,256]{1,0:T(8,128)(2,1)S(1)}, u32[]{:S(2)}, u32[]{:S(2)}) collective-permute-start(bf16[256,256]{1,0:T(8,128)(2,1)S(1)} %get-tuple-element.78), channel_id=1, source_target_pairs={{0,32},{32,0},{1,33},{33,1},{2,34},{34,2},{3,35},{35,3},{4,36},{36... | collective-permute-start | bytes 393224 | tf_op jit(solution)/shard_map/ppermute | solution.py:408
  82.3 8.0 %collective-permute-start.10 = (bf16[108,512]{1,0:T(8,128)(2,1)S(1)}, bf16[108,512]{1,0:T(8,128)(2,1)S(1)}, u32[]{:S(2)}, u32[]{:S(2)}) collective-permute-start(bf16[108,512]{1,0:T(8,128)(2,1)S(1)} %shard_map.116), channel_id=1, source_target_pairs={{0,2},{2,4},{4,6},{6,8},{8,10},{10,12},{12,14},{14,16},{16,18},{18... | collective-permute-start | bytes 331784 | tf_op jit(solution)/shard_map/ppermute | solution.py:408
  96.4 13.1 %all-to-all-start.2 = ((bf16[8,32,384]{2,1,0:T(8,128)(2,1)}), bf16[8,32,384]{2,1,0:T(8,128)(2,1)S(1)}, u32[]{:S(2)}, u32[]{:S(2)}) async-start(bf16[8,32,384]{2,1,0:T(8,128)(2,1)} %shard_map.118), calls=%async_computation.2 | async-start | bytes 393216 | tf_op jit(solution)/shard_map/all_to_all | solution.py:506
  99.8 10.4 %collective-permute-start.11 = (bf16[120,512]{1,0:T(8,128)(2,1)S(1)}, bf16[120,512]{1,0:T(8,128)(2,1)S(1)}, u32[]{:S(2)}, u32[]{:S(2)}) collective-permute-start(bf16[120,512]{1,0:T(8,128)(2,1)S(1)} %get-tuple-element.85), channel_id=1, source_target_pairs={{0,1},{1,0},{2,3},{3,2},{4,5},{5,4},{6,7},{7,6},{8,9},{9,8},{10,11... | collective-permute-start | bytes 368648 | tf_op jit(solution)/shard_map/ppermute | solution.py:408
  101.4 8.9 %collective-permute-start.12 = (bf16[96,512]{1,0:T(8,128)(2,1)S(1)}, bf16[96,512]{1,0:T(8,128)(2,1)S(1)}, u32[]{:S(2)}, u32[]{:S(2)}) collective-permute-start(bf16[96,512]{1,0:T(8,128)(2,1)S(1)} %get-tuple-element.86), channel_id=1, source_target_pairs={{0,64},{64,128},{128,192},{192,0},{1,65},{65,129},{129,193},{193,1... | collective-permute-start | bytes 294920 | tf_op jit(solution)/shard_map/ppermute | solution.py:408
  102.2 8.0 %collective-permute-start.13 = (bf16[96,512]{1,0:T(8,128)(2,1)S(1)}, bf16[96,512]{1,0:T(8,128)(2,1)S(1)}, u32[]{:S(2)}, u32[]{:S(2)}) collective-permute-start(bf16[96,512]{1,0:T(8,128)(2,1)S(1)} %get-tuple-element.87), channel_id=1, source_target_pairs={{0,65},{1,64},{64,129},{65,128},{128,193},{129,192},{192,1},{193,0... | collective-permute-start | bytes 294920 | tf_op jit(solution)/shard_map/ppermute | solution.py:423
  110.2 11.7 %all-to-all-start.3 = ((bf16[8,32,384]{2,1,0:T(8,128)(2,1)}), bf16[8,32,384]{2,1,0:T(8,128)(2,1)S(1)}, u32[]{:S(2)}, u32[]{:S(2)}) async-start(bf16[8,32,384]{2,1,0:T(8,128)(2,1)} %shard_map.119), calls=%async_computation.3 | async-start | bytes 393216 | tf_op jit(solution)/shard_map/all_to_all | solution.py:508
  (11 other events, 52.7 us)

commit v7 on v6

--- a/solution.py
+++ b/solution.py
@@ -488,8 +488,9 @@
     kept, sent, bundle, coarse_field = tied(kept, sent, bundle, coarse_field)
     came = from_behind(sent, ("core",), 1)
     block_terms = (kept.astype(WIDE) + came.astype(WIDE)).astype(LOW)
+    other_normed = from_behind(bundle[:, 2:], ("core",), 1)
+    block_terms, other_normed = tied(block_terms, other_normed)
     block_planes = over_planes(block_terms)
-    other_normed = from_behind(bundle[:, 2:], ("core",), 1)
     merging_kept, merging_sent = call(
         merging_kernel,
         [(256, 256), (256, 256)],

time: 123 us -> 124 us (level)
    unnamed x36 -> x34, local copies, waits for them, and re-layouts: 5.08 us -> 5.06 us
  transfers between devices with their start and end apart: 18 -> 18, of which waited for: 13 -> 12; matrix products, arithmetic and copies ran while one was open for 7% -> 8% of each run, Pallas kernels for 14% -> 14%
where the time goes in v7:
time: 124 us
  starting transfers between devices  40.4 us (33%)
  waiting for transfers between devices  35.3 us (28%)
  Pallas kernels  32.7 us (26%)
  local copies, waits for them, and re-layouts  7.39 us (6%)
  matrix products  4.54 us (4%)
  other arithmetic  2.53 us (2%)
    pallas_call x12, Pallas kernels, call(): pl.pallas_call(kernel, in_specs=specs, out_specs=out_specs, out_shape=[ja...  32.7 us
    ppermute x12, waiting for transfers between devices, from_behind(): return lax.ppermute(value, axis, pairs)  22.6 us
    ppermute x12, starting transfers between devices, from_behind(): return lax.ppermute(value, axis, pairs)  17.2 us
    all_to_all x1, starting transfers between devices, body(): bundle = lax.all_to_all(bundle, ('lat', 'grp'), 0, 0)  5.77 us
    all_to_all x1, starting transfers between devices, body(): shares = lax.all_to_all(share, ('lat', 'grp'), 0, 0)  5.73 us
    all_to_all x1, waiting for transfers between devices, body(): lax.all_to_all(planes, ('z',), 0, 0)  5.35 us
    unnamed x34, local copies, waits for them, and re-layouts  5.06 us
    all_to_all x1, starting transfers between devices, over_planes(): return lax.all_to_all(terms, ('xh', 'lat', 'grp'), 0, 0)  4.61 us
  transfers between devices with their start and end apart: 18, of which 12 were waited for; matrix products, arithmetic and copies ran while one was open for 8% of the time, Pallas kernels for 14%

profile of v7, /device:TPU:2, one launch (start us, length us, event | category | flops | bytes accessed | tf_op | source)
XLA Modules:
  0.0 123.7 jit_solution(10553683593932205021)
XLA Ops:
  3.1 2.4 %collective-permute-start = (bf16[120,512]{1,0:T(8,128)(2,1)S(1)}, bf16[120,512]{1,0:T(8,128)(2,1)S(1)}, u32[]{:S(2)}, u32[]{:S(2)}) collective-permute-start(bf16[120,512]{1,0:T(8,128)(2,1)S(1)} %get-tuple-element.53), channel_id=1, source_target_pairs={{0,1},{1,0},{2,3},{3,2},{4,5},{5,4},{6,7},{7,6},{8,9},{9,8},{10,11... | collective-permute-start | bytes 368648 | tf_op jit(solution)/shard_map/ppermute | solution.py:408
  6.8 1.7 %collective-permute-start.2 = (bf16[96,512]{1,0:T(8,128)(2,1)S(1)}, bf16[96,512]{1,0:T(8,128)(2,1)S(1)}, u32[]{:S(2)}, u32[]{:S(2)}) collective-permute-start(bf16[96,512]{1,0:T(8,128)(2,1)S(1)} %get-tuple-element.55), channel_id=1, source_target_pairs={{0,193},{1,192},{64,1},{65,0},{128,65},{129,64},{192,129},{193,128... | collective-permute-start | bytes 294920 | tf_op jit(solution)/shard_map/ppermute | solution.py:423
  8.4 2.7 %collective-permute-done.1.lat = bf16[96,512]{1,0:T(8,128)(2,1)S(1)} collective-permute-done((bf16[96,512]{1,0:T(8,128)(2,1)S(1)}, bf16[96,512]{1,0:T(8,128)(2,1)S(1)}, u32[]{:S(2)}, u32[]{:S(2)}) %collective-permute-start.1) | collective-permute-done | bytes 98336 | tf_op jit(solution)/shard_map/ppermute | solution.py:408
  12.7 5.5 %collective-permute-start.3 = (bf16[108,512]{1,0:T(8,128)(2,1)S(1)}, bf16[108,512]{1,0:T(8,128)(2,1)S(1)}, u32[]{:S(2)}, u32[]{:S(2)}) collective-permute-start(bf16[108,512]{1,0:T(8,128)(2,1)S(1)} %shard_map.111), channel_id=1, source_target_pairs={{0,62},{2,0},{4,2},{6,4},{8,6},{10,8},{12,10},{14,12},{16,14},{18,... | collective-permute-start | bytes 331784 | tf_op jit(solution)/shard_map/ppermute | solution.py:408
  21.2 11.1 %shard_map.112 = (bf16[288,512]{1,0:T(8,128)(2,1)}, bf16[48,512]{1,0:T(8,128)(2,1)}, bf16[288,512]{1,0:T(8,128)(2,1)}, bf16[288,1536]{1,0:T(8,128)(2,1)}, bf16[2...) custom-call(s32[1]{0:T(128)} %bitcast.core, ...), custom_call_target="tpu_custom_call" | custom-call | tf_op jit(solution)/shard_map/pallas_call | solution.py:392
  33.3 3.7 %fusion.upstream = f32[72,2048]{1,0:T(8,128)S(1)} fusion(bf16[72,1024]{1,0:T(8,128)(2,1)} %get-tuple-element.58, bf16[2048,1024]{1,0:T(8,128)(2,1)} %param.11), kind=kOutput, calls=%fused_computation.3 | convolution fusion | flops 301989888 | bytes 4931584 | tf_op jit(solution)/shard_map/dot_general | solution.py:121
  37.9 2.2 %shard_map.113 = (bf16[72,2048]{1,0:T(8,128)(2,1)S(1)}, bf16[8,4,72,256]{3,2,1,0:T(8,128)(2,1)}, bf16[288,512]{1,0:T(8,128)(2,1)S(1)}, bf16[48,512]{1,0:T(8,128)(2,1)S(1)}) custom-call(s32[432,11]{1,0:T(8,128)S(1)} %copy-done, bf16[288,512]{1,0:T(8,128)(2,1)S(1)} %copy-done.9, bf16[48,512]{1,0:T(8,128)(2,1)S(1)} %collective-permute-done.4.prior, ...), custom_call_target="tpu_custom_call" | custom-call | tf_op jit(solution)/shard_map/pallas_call | solution.py:392
  40.8 1.4 %collective-permute-start.6 = (bf16[48,512]{1,0:T(8,128)(2,1)S(1)}, bf16[48,512]{1,0:T(8,128)(2,1)S(1)}, u32[]{:S(2)}, u32[]{:S(2)}) collective-permute-start(bf16[48,512]{1,0:T(8,128)(2,1)S(1)} %get-tuple-element.63), channel_id=1, source_target_pairs={{0,192},{64,0},{128,64},{192,128},{1,193},{65,1},{129,65},{193,129... | collective-permute-start | bytes 147464 | tf_op jit(solution)/shard_map/ppermute | solution.py:408
  42.3 2.7 %collective-permute-done.6.next_row = bf16[48,512]{1,0:T(8,128)(2,1)S(1)} collective-permute-done((bf16[48,512]{1,0:T(8,128)(2,1)S(1)}, bf16[48,512]{1,0:T(8,128)(2,1)S(1)}, u32[]{:S(2)}, u32[]{:S(2)}) %collective-permute-start.6) | collective-permute-done | bytes 49184 | tf_op jit(solution)/shard_map/ppermute | solution.py:408
  44.9 5.8 %all-to-all-start = ((bf16[8,4,72,256]{3,2,1,0:T(8,128)(2,1)}), bf16[8,4,72,256]{3,2,1,0:T(8,128)(2,1)S(1)}, u32[]{:S(2)}, u32[]{:S(2)}) async-start(bf16[8,4,72,256]{3,2,1,0:T(8,128)(2,1)} %get-tuple-element.74), calls=%async_computation | async-start | bytes 2359296 | tf_op jit(solution)/shard_map/all_to_all | solution.py:475
  50.7 12.2 %shard_map.114 = (bf16[288,512]{1,0:T(8,128)(2,1)}, bf16[2,4,2,8,32,128]{5,4,3,2,1,0:T(8,128)(2,1)}, bf16[2,4,2,8,32,128]{5,4,3,2,1,0:T(8,128)(2,1)}) custom-call(s32[1]{0:T(128)} %bitcast.core, s32[432,11]{1,0:T(8,128)} %constant.10.clone.table, bf16[288,512]{1,0:T(8,128)(2,1)} %copy-done.8, bf16[48,512]{1,0:T(8,128)(2,1)} %copy-done.15, ...), custom_call_target="tpu_custom_call" | custom-call | tf_op jit(solution)/shard_map/pallas_call | solution.py:392
  63.9 2.7 %all-to-all-done.bundle = bf16[8,4,72,256]{3,2,1,0:T(8,128)(2,1)S(1)} async-done(((bf16[8,4,72,256]{3,2,1,0:T(8,128)(2,1)}), bf16[8,4,72,256]{3,2,1,0:T(8,128)(2,1)S(1)}, u32[]{:S(2)}, u32[]{:S(2)}) %all-to-all-start) | async-done | bytes 1179680 | tf_op jit(solution)/shard_map/all_to_all | solution.py:475
  67.2 2.4 %collective-permute-done.7 = bf16[2,4,2,8,32,128]{5,4,3,2,1,0:T(8,128)(2,1)S(1)} collective-permute-done((bf16[2,4,2,8,32,128]{5,4,3,2,1,0:T(8,128)(2,1)}, bf16[2,4,2,8,32,128]{5,4,3,2,1,0:T(8,128)(2,1)S(1)}, u32[]{:S(2)}, u32[]{:S(2)}) %collective-permute-start.7) | collective-permute-done | bytes 1048608 | tf_op jit(solution)/shard_map/ppermute | solution.py:408
  69.6 2.5 %add_convert_fusion = bf16[2,4,2,8,32,128]{5,4,3,2,1,0:T(8,128)(2,1)} fusion(bf16[2,4,2,8,32,128]{5,4,3,2,1,0:T(8,128)(2,1)S(1)} %collective-permute-done.7, bf16[2,4,2,8,32,128]{5,4,3,2,1,0:T(8,128)(2,1)} %get-tuple-element.77), kind=kLoop, calls=%fused_computation | loop fusion | flops 2097152 | bytes 3145728 | tf_op jit(solution)/shard_map/convert_element_type | solution.py:490
  72.1 4.6 %all-to-all-start.1 = ((bf16[16,8,32,128]{3,2,1,0:T(8,128)(2,1)}), bf16[16,8,32,128]{3,2,1,0:T(8,128)(2,1)S(1)}, u32[]{:S(2)}, u32[]{:S(2)}) async-start(bf16[16,8,32,128]{3,2,1,0:T(8,128)(2,1)} %bitcast.20), calls=%async_computation.1 | async-start | bytes 2097152 | tf_op jit(solution)/shard_map/all_to_all | solution.py:438
  78.0 2.2 %collective-permute-start.9 = (bf16[256,256]{1,0:T(8,128)(2,1)S(1)}, bf16[256,256]{1,0:T(8,128)(2,1)S(1)}, u32[]{:S(2)}, u32[]{:S(2)}) collective-permute-start(bf16[256,256]{1,0:T(8,128)(2,1)S(1)} %get-tuple-element.82), channel_id=1, source_target_pairs={{0,32},{32,0},{1,33},{33,1},{2,34},{34,2},{3,35},{35,3},{4,36},{36... | collective-permute-start | bytes 393224 | tf_op jit(solution)/shard_map/ppermute | solution.py:408
  80.7 7.9 %collective-permute-done.10.lon = bf16[108,512]{1,0:T(8,128)(2,1)S(1)} collective-permute-done((bf16[108,512]{1,0:T(8,128)(2,1)S(1)}, bf16[108,512]{1,0:T(8,128)(2,1)S(1)}, u32[]{:S(2)}, u32[]{:S(2)}) %collective-permute-start.10) | collective-permute-done | bytes 110624 | tf_op jit(solution)/shard_map/ppermute | solution.py:408
  89.2 5.9 %collective-permute-done.9.came = bf16[256,256]{1,0:T(8,128)(2,1)S(1)} collective-permute-done((bf16[256,256]{1,0:T(8,128)(2,1)S(1)}, bf16[256,256]{1,0:T(8,128)(2,1)S(1)}, u32[]{:S(2)}, u32[]{:S(2)}) %collective-permute-start.9) | collective-permute-done | bytes 131104 | tf_op jit(solution)/shard_map/ppermute | solution.py:408
  97.2 3.7 %all-to-all-start.2 = ((bf16[8,32,384]{2,1,0:T(8,128)(2,1)}), bf16[8,32,384]{2,1,0:T(8,128)(2,1)S(1)}, u32[]{:S(2)}, u32[]{:S(2)}) async-start(bf16[8,32,384]{2,1,0:T(8,128)(2,1)} %shard_map.118), calls=%async_computation.2 | async-start | bytes 393216 | tf_op jit(solution)/shard_map/all_to_all | solution.py:507
  103.7 1.7 %collective-permute-start.13 = (bf16[96,512]{1,0:T(8,128)(2,1)S(1)}, bf16[96,512]{1,0:T(8,128)(2,1)S(1)}, u32[]{:S(2)}, u32[]{:S(2)}) collective-permute-start(bf16[96,512]{1,0:T(8,128)(2,1)S(1)} %get-tuple-element.91), channel_id=1, source_target_pairs={{0,65},{1,64},{64,129},{65,128},{128,193},{129,192},{192,1},{193,0... | collective-permute-start | bytes 294920 | tf_op jit(solution)/shard_map/ppermute | solution.py:423
  105.4 5.4 %all-to-all-done.2.parts = bf16[8,32,384]{2,1,0:T(8,128)(2,1)S(1)} async-done(((bf16[8,32,384]{2,1,0:T(8,128)(2,1)}), bf16[8,32,384]{2,1,0:T(8,128)(2,1)S(1)}, u32[]{:S(2)}, u32[]{:S(2)}) %all-to-all-start.2) | async-done | bytes 196640 | tf_op jit(solution)/shard_map/all_to_all | solution.py:507
  111.5 5.7 %all-to-all-start.3 = ((bf16[8,32,384]{2,1,0:T(8,128)(2,1)}), bf16[8,32,384]{2,1,0:T(8,128)(2,1)S(1)}, u32[]{:S(2)}, u32[]{:S(2)}) async-start(bf16[8,32,384]{2,1,0:T(8,128)(2,1)} %shard_map.119), calls=%async_computation.3 | async-start | bytes 393216 | tf_op jit(solution)/shard_map/all_to_all | solution.py:509
  117.2 1.8 %shard_map.120 = (bf16[288,512]{1,0:T(8,128)(2,1)}, bf16[72,1024]{1,0:T(8,128)(2,1)S(1)}) custom-call(s32[432,11]{1,0:T(8,128)S(1)} %copy-done.1, bf16[288,512]{1,0:T(8,128)(2,1)S(1)} %copy-done.3, bf16[72,1024]{1,0:T(8,128)(2,1)S(1)} %convolution_convert_fusion.cells, bf16[120,512]{1,0:T(8,128)(2,1)S(1)} %collective-permute-done.11.grp, ...), custom_call_target="tpu_custom_call" | custom-call | tf_op jit(solution)/shard_map/pallas_call | solution.py:392
  119.8 3.1 %all-to-all-done.3.shares = bf16[8,32,384]{2,1,0:T(8,128)(2,1)S(1)} async-done(((bf16[8,32,384]{2,1,0:T(8,128)(2,1)}), bf16[8,32,384]{2,1,0:T(8,128)(2,1)S(1)}, u32[]{:S(2)}, u32[]{:S(2)}) %all-to-all-start.3) | async-done | bytes 196640 | tf_op jit(solution)/shard_map/all_to_all | solution.py:509
  (68 shorter events, 21.9 us)
Async XLA Ops:
  1.6 18.9 %copy-start.4 = (bf16[72,1024]{1,0:T(8,128)(2,1)}, bf16[72,1024]{1,0:T(8,128)(2,1)S(1)}, u32[]{:S(2)}) copy-start(bf16[72,1024]{1,0:T(8,128)(2,1)S(1)} %reshape.36.cells) | copy-start | bytes 442372
  3.1 9.2 %collective-permute-start = (bf16[120,512]{1,0:T(8,128)(2,1)S(1)}, bf16[120,512]{1,0:T(8,128)(2,1)S(1)}, u32[]{:S(2)}, u32[]{:S(2)}) collective-permute-start(bf16[120,512]{1,0:T(8,128)(2,1)S(1)} %get-tuple-element.53), channel_id=1, source_target_pairs={{0,1},{1,0},{2,3},{3,2},{4,5},{5,4},{6,7},{7,6},{8,9},{9,8},{10,11... | collective-permute-start | bytes 368648 | tf_op jit(solution)/shard_map/ppermute | solution.py:408
  5.5 5.7 %collective-permute-start.1 = (bf16[96,512]{1,0:T(8,128)(2,1)S(1)}, bf16[96,512]{1,0:T(8,128)(2,1)S(1)}, u32[]{:S(2)}, u32[]{:S(2)}) collective-permute-start(bf16[96,512]{1,0:T(8,128)(2,1)S(1)} %get-tuple-element.54), channel_id=1, source_target_pairs={{0,192},{64,0},{128,64},{192,128},{1,193},{65,1},{129,65},{193,129... | collective-permute-start | bytes 294920 | tf_op jit(solution)/shard_map/ppermute | solution.py:408
  6.8 5.5 %collective-permute-start.2 = (bf16[96,512]{1,0:T(8,128)(2,1)S(1)}, bf16[96,512]{1,0:T(8,128)(2,1)S(1)}, u32[]{:S(2)}, u32[]{:S(2)}) collective-permute-start(bf16[96,512]{1,0:T(8,128)(2,1)S(1)} %get-tuple-element.55), channel_id=1, source_target_pairs={{0,193},{1,192},{64,1},{65,0},{128,65},{129,64},{192,129},{193,128... | collective-permute-start | bytes 294920 | tf_op jit(solution)/shard_map/ppermute | solution.py:423
  12.7 7.9 %collective-permute-start.3 = (bf16[108,512]{1,0:T(8,128)(2,1)S(1)}, bf16[108,512]{1,0:T(8,128)(2,1)S(1)}, u32[]{:S(2)}, u32[]{:S(2)}) collective-permute-start(bf16[108,512]{1,0:T(8,128)(2,1)S(1)} %shard_map.111), channel_id=1, source_target_pairs={{0,62},{2,0},{4,2},{6,4},{8,6},{10,8},{12,10},{14,12},{16,14},{18,... | collective-permute-start | bytes 331784 | tf_op jit(solution)/shard_map/ppermute | solution.py:408
  19.6 18.3 %copy-start = (s32[432,11]{1,0:T(8,128)S(1)}, s32[432,11]{1,0:T(8,128)}, u32[]{:S(2)}) copy-start(s32[432,11]{1,0:T(8,128)} %constant.10.clone.table) | copy-start | bytes 57028
  32.3 5.6 %collective-permute-start.4 = (bf16[48,512]{1,0:T(8,128)(2,1)}, bf16[48,512]{1,0:T(8,128)(2,1)S(1)}, u32[]{:S(2)}, u32[]{:S(2)}) collective-permute-start(bf16[48,512]{1,0:T(8,128)(2,1)} %get-tuple-element.57), channel_id=1, source_target_pairs={{0,64},{64,128},{128,192},{192,0},{1,65},{65,129},{129,193},{193,1... | collective-permute-start | bytes 147464 | tf_op jit(solution)/shard_map/ppermute | solution.py:408
  33.3 4.6 %collective-permute-start.5 = (bf16[2,72,256]{2,1,0:T(8,128)(2,1)}, bf16[2,72,256]{2,1,0:T(8,128)(2,1)S(1)}, u32[]{:S(2)}, u32[]{:S(2)}) collective-permute-start(bf16[2,72,256]{2,1,0:T(8,128)(2,1)} %get-tuple-element.60), channel_id=1, source_target_pairs={{0,2},{2,0},{1,3},{3,1},{4,6},{6,4},{5,7},{7,5},{8,10},{10,8},{9,1... | collective-permute-start | bytes 221192 | tf_op jit(solution)/shard_map/ppermute | solution.py:408
  40.8 4.1 %collective-permute-start.6 = (bf16[48,512]{1,0:T(8,128)(2,1)S(1)}, bf16[48,512]{1,0:T(8,128)(2,1)S(1)}, u32[]{:S(2)}, u32[]{:S(2)}) collective-permute-start(bf16[48,512]{1,0:T(8,128)(2,1)S(1)} %get-tuple-element.63), channel_id=1, source_target_pairs={{0,192},{64,0},{128,64},{192,128},{1,193},{65,1},{129,65},{193,129... | collective-permute-start | bytes 147464 | tf_op jit(solution)/shard_map/ppermute | solution.py:408
  44.9 21.6 %all-to-all-start = ((bf16[8,4,72,256]{3,2,1,0:T(8,128)(2,1)}), bf16[8,4,72,256]{3,2,1,0:T(8,128)(2,1)S(1)}, u32[]{:S(2)}, u32[]{:S(2)}) async-start(bf16[8,4,72,256]{3,2,1,0:T(8,128)(2,1)} %get-tuple-element.74), calls=%async_computation | async-start | bytes 2359296 | tf_op jit(solution)/shard_map/all_to_all | solution.py:475
  50.7 12.3 %copy-start.13 = (bf16[2048,1024]{1,0:T(8,128)(2,1)S(1)}, bf16[2048,1024]{1,0:T(8,128)(2,1)}, u32[]{:S(2)}) copy-start(bf16[2048,1024]{1,0:T(8,128)(2,1)} %param.11) | copy-start | bytes 12582916
  63.8 16.4 %copy-start.1 = (s32[432,11]{1,0:T(8,128)S(1)}, s32[432,11]{1,0:T(8,128)}, u32[]{:S(2)}) copy-start(s32[432,11]{1,0:T(8,128)} %constant.10.clone.table) | copy-start | bytes 57028
  63.8 16.4 %copy-start.3 = (bf16[288,512]{1,0:T(8,128)(2,1)S(1)}, bf16[288,512]{1,0:T(8,128)(2,1)}, u32[]{:S(2)}) copy-start(bf16[288,512]{1,0:T(8,128)(2,1)} %get-tuple-element.71.tokens) | copy-start | bytes 884740
  66.5 3.0 %collective-permute-start.7 = (bf16[2,4,2,8,32,128]{5,4,3,2,1,0:T(8,128)(2,1)}, bf16[2,4,2,8,32,128]{5,4,3,2,1,0:T(8,128)(2,1)S(1)}, u32[]{:S(2)}, u32[]{:S(2)}) collective-permute-start(bf16[2,4,2,8,32,128]{5,4,3,2,1,0:T(8,128)(2,1)} %get-tuple-element.78), channel_id=1, source_target_pairs={{0,2},{2,0},{1,3},{3,1},{4,6},{6,4},{5,7},{7,5},{8,10},{10,8},{9,1... | collective-permute-start | bytes 3145736 | tf_op jit(solution)/shard_map/ppermute | solution.py:408
  66.6 5.5 %collective-permute-start.8 = (bf16[8,2,72,256]{3,2,1,0:T(8,128)(2,1)S(1)}, bf16[8,2,72,256]{3,2,1,0:T(8,128)(2,1)S(1)}, u32[]{:S(2)}, u32[]{:S(2)}) collective-permute-start(bf16[8,2,72,256]{3,2,1,0:T(8,128)(2,1)S(1)} %slice.3), channel_id=1, source_target_pairs={{0,2},{2,0},{1,3},{3,1},{4,6},{6,4},{5,7},{7,5},{8,10},{10,8},{9,1... | collective-permute-start | bytes 1769480 | tf_op jit(solution)/shard_map/ppermute | solution.py:408
  72.1 23.4 %all-to-all-start.1 = ((bf16[16,8,32,128]{3,2,1,0:T(8,128)(2,1)}), bf16[16,8,32,128]{3,2,1,0:T(8,128)(2,1)S(1)}, u32[]{:S(2)}, u32[]{:S(2)}) async-start(bf16[16,8,32,128]{3,2,1,0:T(8,128)(2,1)} %bitcast.20), calls=%async_computation.1 | async-start | bytes 2097152 | tf_op jit(solution)/shard_map/all_to_all | solution.py:438
  78.0 11.2 %copy-start.10 = (bf16[256,256]{1,0:T(8,128)(2,1)}, bf16[256,256]{1,0:T(8,128)(2,1)S(1)}, u32[]{:S(2)}) copy-start(bf16[256,256]{1,0:T(8,128)(2,1)S(1)} %get-tuple-element.87.kept) | copy-start | bytes 393220
  78.0 17.1 %collective-permute-start.9 = (bf16[256,256]{1,0:T(8,128)(2,1)S(1)}, bf16[256,256]{1,0:T(8,128)(2,1)S(1)}, u32[]{:S(2)}, u32[]{:S(2)}) collective-permute-start(bf16[256,256]{1,0:T(8,128)(2,1)S(1)} %get-tuple-element.82), channel_id=1, source_target_pairs={{0,32},{32,0},{1,33},{33,1},{2,34},{34,2},{3,35},{35,3},{4,36},{36... | collective-permute-start | bytes 393224 | tf_op jit(solution)/shard_map/ppermute | solution.py:408
  80.6 8.0 %collective-permute-start.10 = (bf16[108,512]{1,0:T(8,128)(2,1)S(1)}, bf16[108,512]{1,0:T(8,128)(2,1)S(1)}, u32[]{:S(2)}, u32[]{:S(2)}) collective-permute-start(bf16[108,512]{1,0:T(8,128)(2,1)S(1)} %shard_map.116), channel_id=1, source_target_pairs={{0,2},{2,4},{4,6},{6,8},{8,10},{10,12},{12,14},{14,16},{16,18},{18... | collective-permute-start | bytes 331784 | tf_op jit(solution)/shard_map/ppermute | solution.py:408
  97.2 13.5 %all-to-all-start.2 = ((bf16[8,32,384]{2,1,0:T(8,128)(2,1)}), bf16[8,32,384]{2,1,0:T(8,128)(2,1)S(1)}, u32[]{:S(2)}, u32[]{:S(2)}) async-start(bf16[8,32,384]{2,1,0:T(8,128)(2,1)} %shard_map.118), calls=%async_computation.2 | async-start | bytes 393216 | tf_op jit(solution)/shard_map/all_to_all | solution.py:507
  101.0 10.5 %collective-permute-start.11 = (bf16[120,512]{1,0:T(8,128)(2,1)S(1)}, bf16[120,512]{1,0:T(8,128)(2,1)S(1)}, u32[]{:S(2)}, u32[]{:S(2)}) collective-permute-start(bf16[120,512]{1,0:T(8,128)(2,1)S(1)} %get-tuple-element.89), channel_id=1, source_target_pairs={{0,1},{1,0},{2,3},{3,2},{4,5},{5,4},{6,7},{7,6},{8,9},{9,8},{10,11... | collective-permute-start | bytes 368648 | tf_op jit(solution)/shard_map/ppermute | solution.py:408
  102.3 9.2 %collective-permute-start.12 = (bf16[96,512]{1,0:T(8,128)(2,1)S(1)}, bf16[96,512]{1,0:T(8,128)(2,1)S(1)}, u32[]{:S(2)}, u32[]{:S(2)}) collective-permute-start(bf16[96,512]{1,0:T(8,128)(2,1)S(1)} %get-tuple-element.90), channel_id=1, source_target_pairs={{0,64},{64,128},{128,192},{192,0},{1,65},{65,129},{129,193},{193,1... | collective-permute-start | bytes 294920 | tf_op jit(solution)/shard_map/ppermute | solution.py:408
  103.7 7.8 %collective-permute-start.13 = (bf16[96,512]{1,0:T(8,128)(2,1)S(1)}, bf16[96,512]{1,0:T(8,128)(2,1)S(1)}, u32[]{:S(2)}, u32[]{:S(2)}) collective-permute-start(bf16[96,512]{1,0:T(8,128)(2,1)S(1)} %get-tuple-element.91), channel_id=1, source_target_pairs={{0,65},{1,64},{64,129},{65,128},{128,193},{129,192},{192,1},{193,0... | collective-permute-start | bytes 294920 | tf_op jit(solution)/shard_map/ppermute | solution.py:423
  111.5 11.5 %all-to-all-start.3 = ((bf16[8,32,384]{2,1,0:T(8,128)(2,1)}), bf16[8,32,384]{2,1,0:T(8,128)(2,1)S(1)}, u32[]{:S(2)}, u32[]{:S(2)}) async-start(bf16[8,32,384]{2,1,0:T(8,128)(2,1)} %shard_map.119), calls=%async_computation.3 | async-start | bytes 393216 | tf_op jit(solution)/shard_map/all_to_all | solution.py:509
  (10 other events, 46.2 us)
